TPU v7x, 32 devices: a whole 2x2x4 slice. The times are simulated.
32 devices in a mesh: groups: 1, nodes: 16 (over z, y, core), local: 2 (over x).
Axes of the slice: x: 2, y: 2, z: 4, core: 2. Of those that a mesh axis runs over, the one named last changes fastest.
Arguments:
- hidden_in: bfloat16 [256, 3584], P(('groups', 'nodes', 'local')), may hold values from -6 to 6
- queries: bfloat16 [256, 64, 576], P(('groups', 'nodes', 'local')), may hold values from -100 to 100
- cache: bfloat16 [256, 128, 576], P(('groups', 'nodes', 'local')), may hold values from -6 to 6
- lengths: int32 [256], P(('groups', 'nodes', 'local')), may hold values from 2 to 128, as said below
- expert_ids: int32 [256, 8], P(('groups', 'nodes', 'local')), may hold values from 0 to 15, all different within a row; in each aligned block of 4 rows (0 to 3, 4 to 7, ...) at most 4 rows name the same one
- gate_weights: float32 [256, 8], P(('groups', 'nodes', 'local')), may hold values from 0.1 to 1
- w_gate: bfloat16 [16, 3584, 1024], P('nodes', None, 'local'), may hold values from -0.09375 to 0.09375
- w_up: bfloat16 [16, 3584, 1024], P('nodes', None, 'local'), may hold values from -0.09375 to 0.09375
- w_down: bfloat16 [16, 1024, 3584], P('nodes', 'local'), may hold values from -0.1875 to 0.1875
Outputs:
- context: bfloat16 [256, 32768], P(('groups', 'nodes', 'local'))
- expert_out: bfloat16 [256, 3584], P(('groups', 'nodes', 'local'))
Inputs may be any that keep to these rules, and one draw needn't show every extreme that they name: `lengths`: each row has at least two live positions; in every part some row has all 128. `expert_ids`: ids of a row are distinct; in each aligned block of 4 rows no expert is named more than 4 times.
All inputs are finite; a program needn't handle non-finite values.
Results may differ from a plain program's by a relative error of at most 0.012.
Values may be sent and summed in bfloat16 or wider, within the bound.
No kernel may reach another device: no remote copies, remote signals or barrier semaphores. Data moves between devices by JAX's collectives and lax.ppermute only.
A program may use at most 64 MiB of HBM per device.

v0:
```python
import jax
import jax.numpy as jnp
from jax import lax
from jax.sharding import PartitionSpec as P

D = 3584
HEADS = 64
LATENT = 512
TOP = 8
MB = 2
ROWS_MB = 4


softmax_scale = 0.0722


def attend(queries, cache, lengths):
    scores = (
        jnp.einsum("bhd,btd->bht", queries, cache, preferred_element_type=jnp.float32)
        * softmax_scale
    )
    valid = lax.broadcasted_iota(jnp.int32, (1, 1, cache.shape[1]), 2) < lengths[:, None, None]
    scores = jnp.where(valid, scores, -1e30)
    highest = jnp.max(scores, axis=-1, keepdims=True)
    expo = jnp.exp(scores - highest)
    probs = (expo / jnp.sum(expo, axis=-1, keepdims=True)).astype(jnp.bfloat16)
    context = jnp.einsum(
        "bht,btc->bhc", probs, cache[:, :, :LATENT], preferred_element_type=jnp.float32
    )
    return context.astype(jnp.bfloat16).reshape(queries.shape[0], HEADS * LATENT)


def expert_partial(tokens_in, w_gate, w_up, w_down):
    gate = jnp.einsum("gjcd,jdf->gjcf", tokens_in, w_gate, preferred_element_type=jnp.float32)
    upper = jnp.einsum("gjcd,jdf->gjcf", tokens_in, w_up, preferred_element_type=jnp.float32)
    act = (jax.nn.silu(gate) * upper).astype(jnp.bfloat16)
    partial_value = jnp.einsum(
        "gjcf,jfd->gjcd", act, w_down, preferred_element_type=jnp.float32
    ).astype(jnp.bfloat16)
    return partial_value


def routed_layer(tokens_in, chosen, weights, w_gate, w_up, w_down, capacity):
    nodes_count = lax.axis_size("nodes")
    local_count = lax.axis_size("local")
    held = w_gate.shape[0]
    experts = held * nodes_count
    slot_count = experts * capacity
    row_count = tokens_in.shape[0]
    flat_ids = chosen.reshape(row_count * TOP)
    onehot = (flat_ids[:, None] == jnp.arange(experts, dtype=jnp.int32)[None, :]).astype(jnp.int32)
    earlier = jnp.cumsum(onehot, axis=0) - onehot
    slots = jnp.sum(earlier * onehot, axis=1)
    target = flat_ids * capacity + slots
    select = (target[:, None] == jnp.arange(slot_count, dtype=jnp.int32)[None, :]).astype(
        jnp.float32
    )
    select = select.reshape(row_count, TOP, slot_count)
    placing = jnp.sum(select, axis=1).astype(jnp.bfloat16)
    weighted = jnp.sum(select * weights[:, :, None], axis=1)
    buffer = lax.dot_general(
        placing, tokens_in, (((0,), (0,)), ((), ())), preferred_element_type=jnp.float32
    ).astype(jnp.bfloat16)
    width = held * capacity
    sending = jnp.broadcast_to(
        buffer.reshape(nodes_count, 1, width, D), (nodes_count, local_count, width, D)
    )
    sending = sending.reshape(nodes_count * local_count, width, D)
    arrived = lax.all_to_all(sending, ("nodes", "local"), split_axis=0, concat_axis=0, tiled=True)
    piece = arrived.reshape(nodes_count * local_count, held, capacity, D)
    partial_value = expert_partial(piece, w_gate, w_up, w_down).reshape(
        nodes_count * local_count, width, D
    )
    returned = lax.all_to_all(
        partial_value, ("nodes", "local"), split_axis=0, concat_axis=0, tiled=True
    )
    returned = returned.reshape(nodes_count, local_count, width, D).astype(jnp.float32)
    values = jnp.sum(returned, axis=1).astype(jnp.bfloat16).reshape(slot_count, D)
    combined = jnp.dot(weighted, values.astype(jnp.float32), precision=lax.Precision.HIGHEST)
    return combined.astype(jnp.bfloat16)


def on_device(hidden_in, queries, cache, lengths, expert_ids, gate_weights, w_gate, w_up, w_down):
    experts = w_gate.shape[0] * lax.axis_size("nodes")
    capacity = min(ROWS_MB, max(2, 2 * ROWS_MB * TOP // experts))
    context = attend(queries, cache, lengths)
    results = []
    for micro_batch in range(MB):
        first = micro_batch * ROWS_MB
        results.append(
            routed_layer(
                hidden_in[first : first + ROWS_MB],
                expert_ids[first : first + ROWS_MB],
                gate_weights[first : first + ROWS_MB],
                w_gate,
                w_up,
                w_down,
                capacity,
            )
        )
    return (context, jnp.concatenate(results, axis=0))


def solution(mesh):
    return jax.shard_map(
        on_device,
        mesh=mesh,
        in_specs=(
            P(("groups", "nodes", "local"), None),
            P(("groups", "nodes", "local"), None, None),
            P(("groups", "nodes", "local"), None, None),
            P(("groups", "nodes", "local")),
            P(("groups", "nodes", "local"), None),
            P(("groups", "nodes", "local"), None),
            P("nodes", None, "local"),
            P("nodes", None, "local"),
            P("nodes", "local", None),
        ),
        out_specs=(P(("groups", "nodes", "local"), None), P(("groups", "nodes", "local"), None)),
        check_vma=False,
    )
```

profile of v0, /device:TPU:0, one launch (start us, length us, event | category | flops | bytes accessed | tf_op | source)
XLA Modules:
  0.0 121.5 jit_solution(6161205109502524700)
XLA Ops:
  0.7 0.8 fusion.81
  2.4 0.8 fusion.80
  3.2 0.8 multiply_add_fusion.1
  4.1 1.1 convolution_convert_fusion.3
  5.3 1.2 broadcast_in_dim.23
  6.5 7.3 %all-to-all-start = ((bf16[32,4,3584]{2,1,0:T(4,128)(2,1)}), bf16[32,4,3584]{2,1,0:T(4,128)(2,1)S(1)}, u32[]{:S(2)}, u32[]{:S(2)}) async-start(bf16[32,4,3584]{2,1,0:T(4,128)(2,1)} %bitcast), calls=%async_computation | async-start | bytes 1835008 | tf_op jit(solution)/shard_map/all_to_all | solution.py:69
  14.3 23.0 %all-to-all-done = bf16[32,4,3584]{2,1,0:T(4,128)(2,1)S(1)} async-done(((bf16[32,4,3584]{2,1,0:T(4,128)(2,1)}), bf16[32,4,3584]{2,1,0:T(4,128)(2,1)S(1)}, u32[]{:S(2)}, u32[]{:S(2)}) %all-to-all-start) | async-done | bytes 917536 | tf_op jit(solution)/shard_map/all_to_all | solution.py:69
  37.2 1.2 broadcast_in_dim.42
  38.4 3.6 %all-to-all-start.2 = ((bf16[32,4,3584]{2,1,0:T(4,128)(2,1)}), bf16[32,4,3584]{2,1,0:T(4,128)(2,1)S(1)}, u32[]{:S(2)}, u32[]{:S(2)}) async-start(bf16[32,4,3584]{2,1,0:T(4,128)(2,1)} %bitcast.17), calls=%async_computation.2 | async-start | bytes 1835008 | tf_op jit(solution)/shard_map/all_to_all | solution.py:69
  42.1 3.4 %fusion.13 = f32[32,1,4,512]{3,0,2,1:T(8,128)} fusion(bf16[1,3584,512]{2,1,0:T(8,128)(2,1)} %param.15, bf16[32,4,3584]{2,1,0:T(4,128)(2,1)S(1)} %all-to-all-done), kind=kOutput, calls=%fused_computation.20 | convolution fusion | flops 469762048 | bytes 4849664 | tf_op jit(solution)/shard_map/gjcd,jdf->gjcf/dot_general | solution.py:34
  45.5 4.5 %convolution_convert_fusion.1 = bf16[32,4,3584]{2,0,1:T(8,128)(2,1)S(1)} fusion(bf16[1,512,3584]{2,1,0:T(8,128)(2,1)} %param.17, bf16[1,3584,512]{2,1,0:T(8,128)(2,1)} %param.16, bf16[32,4,3584]{2,1,0:T(4,128)(2,1)S(1)} %all-to-all-done, f32[32,1,4,512]{3,0,2,1:T(8,128)} %fusion.13), kind=kOutput, calls=%fused_computation.2 | convolution fusion | flops 940376064 | bytes 9437184 | tf_op jit(solution)/shard_map/gjcf,jfd->gjcd/dot_general | solution.py:37
  50.0 1.6 %copy.37 = bf16[32,4,3584]{2,1,0:T(4,128)(2,1)} copy(bf16[32,4,3584]{2,0,1:T(8,128)(2,1)S(1)} %convolution_convert_fusion.1) | data formatting | bytes 1835008 | tf_op jit(solution)/shard_map/convert_element_type | solution.py:39
  51.6 13.9 %all-to-all-done.2 = bf16[32,4,3584]{2,1,0:T(4,128)(2,1)S(1)} async-done(((bf16[32,4,3584]{2,1,0:T(4,128)(2,1)}), bf16[32,4,3584]{2,1,0:T(4,128)(2,1)S(1)}, u32[]{:S(2)}, u32[]{:S(2)}) %all-to-all-start.2) | async-done | bytes 917536 | tf_op jit(solution)/shard_map/all_to_all | solution.py:69
  65.5 3.6 %all-to-all-start.1 = ((bf16[32,4,3584]{2,1,0:T(4,128)(2,1)}), bf16[32,4,3584]{2,1,0:T(4,128)(2,1)S(1)}, u32[]{:S(2)}, u32[]{:S(2)}) async-start(bf16[32,4,3584]{2,1,0:T(4,128)(2,1)} %copy.37), calls=%async_computation.1 | async-start | bytes 1835008 | tf_op jit(solution)/shard_map/all_to_all | solution.py:74
  69.1 3.4 %fusion.16 = f32[32,1,4,512]{3,0,2,1:T(8,128)} fusion(bf16[1,3584,512]{2,1,0:T(8,128)(2,1)} %param.15, bf16[32,4,3584]{2,1,0:T(4,128)(2,1)S(1)} %all-to-all-done.2), kind=kOutput, calls=%fused_computation.21 | convolution fusion | flops 469762048 | bytes 4849664 | tf_op jit(solution)/shard_map/gjcd,jdf->gjcf/dot_general | solution.py:34
  72.5 4.5 %convolution_convert_fusion = bf16[32,4,3584]{2,0,1:T(8,128)(2,1)S(1)} fusion(bf16[1,512,3584]{2,1,0:T(8,128)(2,1)} %param.17, bf16[1,3584,512]{2,1,0:T(8,128)(2,1)} %param.16, bf16[32,4,3584]{2,1,0:T(4,128)(2,1)S(1)} %all-to-all-done.2, f32[32,1,4,512]{3,0,2,1:T(8,128)} %fusion.16), kind=kOutput, calls=%fused_computation.1 | convolution fusion | flops 940376064 | bytes 9437184 | tf_op jit(solution)/shard_map/gjcf,jfd->gjcd/dot_general | solution.py:37
  77.0 1.7 %copy.42 = bf16[32,4,3584]{2,1,0:T(4,128)(2,1)} copy(bf16[32,4,3584]{2,0,1:T(8,128)(2,1)S(1)} %convolution_convert_fusion) | data formatting | bytes 1835008 | tf_op jit(solution)/shard_map/convert_element_type | solution.py:39
  78.7 13.8 %all-to-all-done.1 = bf16[32,4,3584]{2,1,0:T(4,128)(2,1)S(1)} async-done(((bf16[32,4,3584]{2,1,0:T(4,128)(2,1)}), bf16[32,4,3584]{2,1,0:T(4,128)(2,1)S(1)}, u32[]{:S(2)}, u32[]{:S(2)}) %all-to-all-start.1) | async-done | bytes 917536 | tf_op jit(solution)/shard_map/all_to_all | solution.py:74
  92.5 3.6 %all-to-all-start.3 = ((bf16[32,4,3584]{2,1,0:T(4,128)(2,1)}), bf16[32,4,3584]{2,1,0:T(4,128)(2,1)S(1)}, u32[]{:S(2)}, u32[]{:S(2)}) async-start(bf16[32,4,3584]{2,1,0:T(4,128)(2,1)} %copy.42), calls=%async_computation.3 | async-start | bytes 1835008 | tf_op jit(solution)/shard_map/all_to_all | solution.py:74
  96.3 1.6 %fusion.26 = f32[8,64,128]{2,1,0:T(8,128)S(1)} fusion(bf16[8,64,576]{2,1,0:T(8,128)(2,1)S(1)} %copy-done, bf16[8,128,576]{1,2,0:T(8,128)(2,1)} %param.11, pred[8,128]{1,0:T(8,128)(4,1)S(1)} %iota_compare_fusion.4), kind=kOutput, calls=%fused_computation.26 | convolution fusion | flops 75628544 | bytes 2032640 | tf_op jit(solution)/shard_map/bhd,btd->bht/dot_general | solution.py:19
  98.1 2.2 %fusion.11 = bf16[1,8,64,512]{3,2,1,0:T(8,128)(2,1)S(1)} fusion(bf16[8,128,576]{1,2,0:T(8,128)(2,1)} %param.11, f32[8,64]{1,0:T(8,128)S(1)} %fusion.82, f32[8,64,128]{2,1,0:T(8,128)S(1)} %fusion.26), kind=kOutput, calls=%fused_computation.18 | convolution fusion | flops 67568256 | bytes 2101248 | tf_op jit(solution)/shard_map/bht,btc->bhc/dot_general | solution.py:27
  100.4 1.1 copy.48
  102.1 17.5 %all-to-all-done.3 = bf16[32,4,3584]{2,1,0:T(4,128)(2,1)S(1)} async-done(((bf16[32,4,3584]{2,1,0:T(4,128)(2,1)}), bf16[32,4,3584]{2,1,0:T(4,128)(2,1)S(1)}, u32[]{:S(2)}, u32[]{:S(2)}) %all-to-all-start.3) | async-done | bytes 917536 | tf_op jit(solution)/shard_map/all_to_all | solution.py:74
  120.8 0.7 pad_maximum_fusion
  (28 shorter events, 3.8 us)
Async XLA Ops:
  0.6 95.6 %copy-start = (bf16[8,64,576]{2,1,0:T(8,128)(2,1)S(1)}, bf16[8,64,576]{2,1,0:T(8,128)(2,1)}, u32[]{:S(2)}) copy-start(bf16[8,64,576]{2,1,0:T(8,128)(2,1)} %param.10) | copy-start | bytes 1769476
  0.6 13.2 %copy-start.1 = (bf16[8,3584]{1,0:T(8,128)(2,1)S(1)}, bf16[8,3584]{1,0:T(8,128)(2,1)}, u32[]{:S(2)}) copy-start(bf16[8,3584]{1,0:T(8,128)(2,1)} %param.9) | copy-start | bytes 172036
  6.5 30.7 %all-to-all-start = ((bf16[32,4,3584]{2,1,0:T(4,128)(2,1)}), bf16[32,4,3584]{2,1,0:T(4,128)(2,1)S(1)}, u32[]{:S(2)}, u32[]{:S(2)}) async-start(bf16[32,4,3584]{2,1,0:T(4,128)(2,1)} %bitcast), calls=%async_computation | async-start | bytes 1835008 | tf_op jit(solution)/shard_map/all_to_all | solution.py:69
  38.4 27.1 %all-to-all-start.2 = ((bf16[32,4,3584]{2,1,0:T(4,128)(2,1)}), bf16[32,4,3584]{2,1,0:T(4,128)(2,1)S(1)}, u32[]{:S(2)}, u32[]{:S(2)}) async-start(bf16[32,4,3584]{2,1,0:T(4,128)(2,1)} %bitcast.17), calls=%async_computation.2 | async-start | bytes 1835008 | tf_op jit(solution)/shard_map/all_to_all | solution.py:69
  65.5 27.1 %all-to-all-start.1 = ((bf16[32,4,3584]{2,1,0:T(4,128)(2,1)}), bf16[32,4,3584]{2,1,0:T(4,128)(2,1)S(1)}, u32[]{:S(2)}, u32[]{:S(2)}) async-start(bf16[32,4,3584]{2,1,0:T(4,128)(2,1)} %copy.37), calls=%async_computation.1 | async-start | bytes 1835008 | tf_op jit(solution)/shard_map/all_to_all | solution.py:74
  77.0 19.2 %copy-start.2 = (s32[8]{0:T(128)S(1)}, s32[8]{0:T(128)}, u32[]{:S(2)}) copy-start(s32[8]{0:T(128)} %param.12) | copy-start | bytes 100
  92.5 27.1 %all-to-all-start.3 = ((bf16[32,4,3584]{2,1,0:T(4,128)(2,1)}), bf16[32,4,3584]{2,1,0:T(4,128)(2,1)S(1)}, u32[]{:S(2)}, u32[]{:S(2)}) async-start(bf16[32,4,3584]{2,1,0:T(4,128)(2,1)} %copy.42), calls=%async_computation.3 | async-start | bytes 1835008 | tf_op jit(solution)/shard_map/all_to_all | solution.py:74
where the time goes:
time: 122 us
  waiting for transfers between devices  68.2 us (56%)
  matrix products  21.7 us (18%)
  starting transfers between devices  18.1 us (15%)
  local copies, waits for them, and re-layouts  9.14 us (7%)
  other arithmetic  3.54 us (3%)
    all_to_all x2, waiting for transfers between devices, routed_layer(): lax.all_to_all(sending, ('nodes', 'local'), split_axis=0, concat_axis=0,...  36.9 us
    all_to_all x2, waiting for transfers between devices, routed_layer(): lax.all_to_all(partial_value, ('nodes', 'local'), split_axis=0, concat_ax...  31.3 us
    all_to_all x2, starting transfers between devices, routed_layer(): lax.all_to_all(sending, ('nodes', 'local'), split_axis=0, concat_axis=0,...  10.9 us
    dot_general x2, matrix products, expert_partial(): jnp.einsum('gjcf,jfd->gjcd', act, w_down, preferred_element_type=jnp.floa...  8.98 us
    all_to_all x2, starting transfers between devices, routed_layer(): lax.all_to_all(partial_value, ('nodes', 'local'), split_axis=0, concat_ax...  7.24 us
    dot_general x2, matrix products, expert_partial(): jnp.einsum('gjcd,jdf->gjcf', tokens_in, w_gate, preferred_element_type=jn...  6.79 us
    convert_element_type x2, local copies, waits for them, and re-layouts, expert_partial(): partial_value = jnp.einsum('gjcf,jfd->gjcd', act, w_down, preferred_eleme...  3.32 us
    broadcast_in_dim x4, local copies, waits for them, and re-layouts, routed_layer(): jnp.broadcast_to(buffer.reshape(nodes_count, 1, width, D), (nodes_count,...  2.59 us
  transfers between devices with their start and end apart: 4, of which 4 were waited for; matrix products, arithmetic and copies ran while one was open for 21% of the time, Pallas kernels for 0%

commit v1 on v0

v1 whole, which is shorter than its diff:
```python
import jax
import jax.numpy as jnp
from jax import lax
from jax.experimental import pallas as pl
from jax.experimental.pallas import tpu as pltpu
from jax.sharding import Mesh, PartitionSpec as P

LATENT = 512
LANES = 128
TERMS = 3

softmax_scale = 0.0722


def attend(queries, cache, lengths):
    scores = (
        jnp.einsum("bhd,btd->bht", queries, cache, preferred_element_type=jnp.float32)
        * softmax_scale
    )
    valid = lax.broadcasted_iota(jnp.int32, (1, 1, cache.shape[1]), 2) < lengths[:, None, None]
    scores = jnp.where(valid, scores, -1e30)
    highest = jnp.max(scores, axis=-1, keepdims=True)
    expo = jnp.exp(scores - highest)
    probs = (expo / jnp.sum(expo, axis=-1, keepdims=True)).astype(jnp.bfloat16)
    context = jnp.einsum(
        "bht,btc->bhc", probs, cache[:, :, :LATENT], preferred_element_type=jnp.float32
    )
    return context.astype(jnp.bfloat16).reshape(queries.shape[0], queries.shape[1] * LATENT)


def pack_kernel(experts, hidden_ref, ids_ref, weights_ref, out_ref):
    rows, width = hidden_ref.shape
    extra = out_ref.shape[1] - width
    out_ref[:, :width] = hidden_ref[...]
    lane = lax.broadcasted_iota(jnp.int32, (rows, extra), 1)
    expert, term = lane % experts, lane // experts
    dense = jnp.zeros((rows, extra), jnp.float32)
    for k in range(ids_ref.shape[1]):
        dense = dense + jnp.where(ids_ref[:, k : k + 1] == expert, weights_ref[:, k : k + 1], 0.0)
    high = dense.astype(jnp.bfloat16).astype(jnp.float32)
    rest = dense - high
    middle = rest.astype(jnp.bfloat16).astype(jnp.float32)
    low = rest - middle
    terms = jnp.where(term == 0, high, jnp.where(term == 1, middle, low))
    out_ref[:, width:] = jnp.where(term < TERMS, terms, 0.0).astype(jnp.bfloat16)


def pack(hidden, ids, weights, experts):
    rows, width = hidden.shape
    extra = -(-experts * TERMS // LANES) * LANES
    return pl.pallas_call(
        lambda *refs: pack_kernel(experts, *refs),
        out_shape=jax.ShapeDtypeStruct((rows, width + extra), jnp.bfloat16),
        name="pack",
    )(hidden, ids, weights)


def expert_kernel(experts, chunk, me_ref, mine_ref, other_ref, gate_hbm, up_hbm, down_hbm, mine_out, other_out, rows_ref, gate_w, up_w, down_w, gate_acc, up_acc, sems):
    half = mine_ref.shape[0]
    width = mine_out.shape[1]
    units = gate_w.shape[1]
    steps = width // chunk
    copies = []
    for k in range(steps):
        part = pl.ds(k * chunk, chunk)
        copies.append(pltpu.make_async_copy(gate_hbm.at[part], gate_w.at[part], sems.at[0, k]))
        copies.append(pltpu.make_async_copy(up_hbm.at[part], up_w.at[part], sems.at[1, k]))
    for k in range(steps):
        part = pl.ds(k * chunk, chunk)
        copies.append(pltpu.make_async_copy(down_hbm.at[:, part], down_w.at[:, part], sems.at[2, k]))
    for copy in copies:
        copy.start()
    rows_ref[:half] = mine_ref[...]
    rows_ref[half:] = other_ref[...]
    for k in range(steps):
        copies[2 * k].wait()
        copies[2 * k + 1].wait()
        piece = rows_ref[:, k * chunk : (k + 1) * chunk]
        gate = jnp.dot(piece, gate_w[k * chunk : (k + 1) * chunk], preferred_element_type=jnp.float32)
        up = jnp.dot(piece, up_w[k * chunk : (k + 1) * chunk], preferred_element_type=jnp.float32)
        if k == 0:
            gate_acc[...] = gate
            up_acc[...] = up
        else:
            gate_acc[...] += gate
            up_acc[...] += up
    gate = gate_acc[...]
    act = (gate / (1.0 + jnp.exp(-gate)) * up_acc[...]).astype(jnp.bfloat16)
    info = rows_ref[:, width:].astype(jnp.float32)
    lane = lax.broadcasted_iota(jnp.int32, info.shape, 1)
    me = me_ref[0]
    mask = (lane == me) | (lane == me + experts) | (lane == me + 2 * experts)
    weight = jnp.sum(jnp.where(mask, info, 0.0), axis=1, keepdims=True)
    for k in range(steps):
        copies[2 * steps + k].wait()
        value = jnp.dot(act, down_w[:, k * chunk : (k + 1) * chunk], preferred_element_type=jnp.float32)
        value = (value * weight).astype(jnp.bfloat16)
        mine_out[:, k * chunk : (k + 1) * chunk] = value[:half]
        other_out[:, k * chunk : (k + 1) * chunk] = value[half:]


def expert_values(mine, other, w_gate, w_up, w_down, experts):
    half, packed = mine.shape
    width, units = w_gate.shape
    chunk = 512
    steps = width // chunk
    me = (lax.axis_index(("z1", "mid", "core"))).astype(jnp.int32).reshape(1)
    vmem = pl.BlockSpec(memory_space=pltpu.VMEM)
    hbm = pl.BlockSpec(memory_space=pl.ANY)
    out = jax.ShapeDtypeStruct((half, width), jnp.bfloat16)
    return pl.pallas_call(
        lambda *refs: expert_kernel(experts, chunk, *refs),
        out_shape=(out, out),
        in_specs=[pl.BlockSpec(memory_space=pltpu.SMEM), vmem, vmem, hbm, hbm, hbm],
        out_specs=(vmem, vmem),
        scratch_shapes=[
            pltpu.VMEM((2 * half, packed), jnp.bfloat16),
            pltpu.VMEM((width, units), jnp.bfloat16),
            pltpu.VMEM((width, units), jnp.bfloat16),
            pltpu.VMEM((units, width), jnp.bfloat16),
            pltpu.VMEM((2 * half, units), jnp.float32),
            pltpu.VMEM((2 * half, units), jnp.float32),
            pltpu.SemaphoreType.DMA((3, steps)),
        ],
        compiler_params=pltpu.CompilerParams(vmem_limit_bytes=60 * 1024 * 1024),
        cost_estimate=pl.CostEstimate(
            flops=2 * 2 * half * width * units * 3,
            bytes_accessed=3 * width * units * 2 + 4 * half * packed * 2,
            transcendentals=2 * half * units,
        ),
        name="expert",
    )(me, mine, other, w_gate, w_up, w_down)


def routed_layer(hidden, ids, weights, w_gate, w_up, w_down):
    rows, width = hidden.shape
    block = lax.axis_size("mid") * lax.axis_size("local")
    experts = w_gate.shape[0] * lax.axis_size("z1") * lax.axis_size("mid") * lax.axis_size("core")
    swap = [(0, 1), (1, 0)]
    packed = pack(hidden, ids, weights, experts)
    far = lax.ppermute(packed, "z1", swap)
    pair = jnp.concatenate([packed, far], axis=0)
    sending = jnp.broadcast_to(pair[None], (block,) + pair.shape)
    mine = lax.all_to_all(sending, ("mid", "local"), split_axis=0, concat_axis=0, tiled=True)
    mine = mine.reshape(block * 2 * rows, packed.shape[1])
    other = lax.ppermute(mine, "core", swap)
    mine_out, other_out = expert_values(mine, other, w_gate[0], w_up[0], w_down[0], experts)
    from_other = lax.ppermute(other_out, "core", swap)
    total = (mine_out.astype(jnp.float32) + from_other.astype(jnp.float32)).astype(jnp.bfloat16)
    back = lax.all_to_all(
        total.reshape(block, 2 * rows, width), ("mid", "local"), split_axis=0, concat_axis=0, tiled=True
    )
    back = jnp.sum(back.astype(jnp.float32), axis=0)
    for_far = back[rows:].astype(jnp.bfloat16)
    from_far = lax.ppermute(for_far, "z1", swap)
    return (back[:rows] + from_far.astype(jnp.float32)).astype(jnp.bfloat16)


def on_device(hidden_in, queries, cache, lengths, expert_ids, gate_weights, w_gate, w_up, w_down):
    expert_out = routed_layer(hidden_in, expert_ids, gate_weights, w_gate, w_up, w_down)
    context = attend(queries, cache, lengths)
    return (context, expert_out)


def solution(mesh):
    groups, nodes, local = mesh.shape["groups"], mesh.shape["nodes"], mesh.shape["local"]
    fine = Mesh(
        mesh.devices.reshape(groups, 2, nodes // 4, 2, local),
        ("groups", "z1", "mid", "core", "local"),
    )
    every = ("groups", "z1", "mid", "core", "local")
    nodes = ("z1", "mid", "core")
    return jax.shard_map(
        on_device,
        mesh=fine,
        in_specs=(
            P(every, None),
            P(every, None, None),
            P(every, None, None),
            P(every),
            P(every, None),
            P(every, None),
            P(nodes, None, "local"),
            P(nodes, None, "local"),
            P(nodes, "local", None),
        ),
        out_specs=(P(every, None), P(every, None)),
        check_vma=False,
    )
```

time: 122 us -> 70.6 us (0.58)
  waiting for transfers between devices: 68.2 us -> 22.3 us
  matrix products: 21.7 us -> 1.38 us
  blocking collectives: 0 us -> 17.4 us
  Pallas kernels: 0 us -> 10.2 us
  local copies, waits for them, and re-layouts: 9.14 us -> 2.16 us
  starting transfers between devices: 18.1 us -> 11.8 us
    all_to_all x4 -> x1, waiting for transfers between devices: 68.2 us -> 13 us  [routed_layer(): lax.all_to_all(total.reshape(block, 2 * rows, width), ('mid', 'local'), s...]
    dot_general x8 -> x0, matrix products: 17.8 us -> none  [the longest x2 8.98 us: expert_partial(): jnp.einsum('gjcf,jfd->gjcd', act, w_down, preferred_element_type=jnp.floa...]
    all_to_all x0 -> x1, blocking collectives: none -> 17.4 us  [routed_layer(): lax.all_to_all(sending, ('mid', 'local'), split_axis=0, concat_axis=0, ti...]
    all_to_all x4 -> x1, starting transfers between devices: 18.1 us -> 3.55 us  [routed_layer(): lax.all_to_all(total.reshape(block, 2 * rows, width), ('mid', 'local'), s...]
    pallas_call x0 -> x2, Pallas kernels: none -> 10.2 us  [the longest x1 8.57 us: expert_values(): pl.pallas_call(lambda *refs: expert_kernel(experts, chunk, *refs), out_sh...]
    ppermute x0 -> x4, waiting for transfers between devices: none -> 9.36 us  [the longest x1 3.02 us: routed_layer(): far = lax.ppermute(packed, 'z1', swap)]
    ppermute x0 -> x4, starting transfers between devices: none -> 8.21 us  [the longest x1 4.04 us: routed_layer(): far = lax.ppermute(packed, 'z1', swap)]
    convert_element_type x2 -> x0, local copies, waits for them, and re-layouts: 3.32 us -> none  [expert_partial(): partial_value = jnp.einsum('gjcf,jfd->gjcd', act, w_down, preferred_eleme...]
  transfers between devices with their start and end apart: 4 -> 5, of which waited for: 4 -> 5; matrix products, arithmetic and copies ran while one was open for 21% -> 4% of each run, Pallas kernels for 0% -> 0%
where the time goes in v1:
time: 70.6 us; the launch traced here: 70.2 us
  waiting for transfers between devices  22.3 us (32%)
  blocking collectives  17.4 us (25%)
  starting transfers between devices  11.8 us (17%)
  Pallas kernels  10.2 us (14%)
  other arithmetic  4.34 us (6%)
  local copies, waits for them, and re-layouts  2.16 us (3%)
  matrix products  1.38 us (2%)
  between operations  0.71 us (1%)
    all_to_all x1, blocking collectives, routed_layer(): lax.all_to_all(sending, ('mid', 'local'), split_axis=0, concat_axis=0, ti...  17.4 us
    all_to_all x1, waiting for transfers between devices, routed_layer(): lax.all_to_all(total.reshape(block, 2 * rows, width), ('mid', 'local'), s...  13 us
    pallas_call x1, Pallas kernels, expert_values(): pl.pallas_call(lambda *refs: expert_kernel(experts, chunk, *refs), out_sh...  8.57 us
    ppermute x1, starting transfers between devices, routed_layer(): far = lax.ppermute(packed, 'z1', swap)  4.04 us
    ppermute x1, starting transfers between devices, routed_layer(): from_far = lax.ppermute(for_far, 'z1', swap)  3.97 us
    all_to_all x1, starting transfers between devices, routed_layer(): lax.all_to_all(total.reshape(block, 2 * rows, width), ('mid', 'local'), s...  3.55 us
    ppermute x1, waiting for transfers between devices, routed_layer(): far = lax.ppermute(packed, 'z1', swap)  3.02 us
    ppermute x1, waiting for transfers between devices, routed_layer(): from_other = lax.ppermute(other_out, 'core', swap)  2.55 us
  transfers between devices with their start and end apart: 5, of which 5 were waited for; matrix products, arithmetic and copies ran while one was open for 4% of the time, Pallas kernels for 0%

profile of v1, /device:TPU:0, one launch (start us, length us, event | category | flops | bytes accessed | tf_op | source)
XLA Modules:
  0.0 70.2 jit_solution(15890393458909528452)
XLA Ops:
  0.6 0.0 copy-start
  0.6 1.6 %pack.1 = bf16[8,3712]{1,0:T(8,128)(2,1)} custom-call(bf16[8,3584]{1,0:T(8,128)(2,1)} %refs_0_.1, s32[8,8]{1,0:T(8,128)} %refs_1_.1, f32[8,8]{1,0:T(8,128)} %refs_2_.1), custom_call_target="tpu_custom_call" | custom-call | tf_op jit(solution)/shard_map/pack/pallas_call | solution.py:51
  2.3 4.0 %collective-permute-start = (bf16[8,3712]{1,0:T(8,128)(2,1)}, bf16[8,3712]{1,0:T(8,128)(2,1)S(1)}, u32[]{:S(2)}, u32[]{:S(2)}) collective-permute-start(bf16[8,3712]{1,0:T(8,128)(2,1)} %pack.1), channel_id=1, source_target_pairs={{0,16},{16,0},{1,17},{17,1},{2,18},{18,2},{3,19},{19,3},{4,20},{20... | collective-permute-start | bytes 178184 | tf_op jit(solution)/shard_map/ppermute | solution.py:141
  6.3 3.0 %collective-permute-done = bf16[8,3712]{1,0:T(8,128)(2,1)S(1)} collective-permute-done((bf16[8,3712]{1,0:T(8,128)(2,1)}, bf16[8,3712]{1,0:T(8,128)(2,1)S(1)}, u32[]{:S(2)}, u32[]{:S(2)}) %collective-permute-start) | collective-permute-done | bytes 59424 | tf_op jit(solution)/shard_map/ppermute | solution.py:141
  9.3 0.8 %pad_maximum_fusion = bf16[16,3712]{1,0:T(8,128)(2,1)S(1)} fusion(bf16[8,3712]{1,0:T(8,128)(2,1)S(1)} %collective-permute-done, bf16[8,3712]{1,0:T(8,128)(2,1)} %pack.1), kind=kLoop, calls=%fused_computation.12 | loop fusion | flops 237568 | bytes 237568 | tf_op jit(solution)/shard_map/concatenate | solution.py:142
  10.2 0.1 broadcast_in_dim.23
  10.2 17.4 %all_to_all.10 = bf16[8,16,3712]{2,1,0:T(8,128)(2,1)S(1)} all-to-all(bf16[8,16,3712]{2,1,0:T(8,128)(2,1)S(1)} %broadcast_in_dim.23), channel_id=1, replica_groups=mesh['groups'=1,'z1'=2,'mid'=4,'core'=2,'local'=2] {'mid','local'}, dimensions={0} | all-to-all | bytes 1900544 | tf_op jit(solution)/shard_map/all_to_all | solution.py:144
  27.6 2.5 %collective-permute-done.1.refs_2_ = bf16[128,3712]{1,0:T(8,128)(2,1)S(1)} collective-permute-done((bf16[128,3712]{1,0:T(8,128)(2,1)S(1)}, bf16[128,3712]{1,0:T(8,128)(2,1)S(1)}, u32[]{:S(2)}, u32[]{:S(2)}) %collective-permute-start.1) | collective-permute-done | bytes 950304 | tf_op jit(solution)/shard_map/ppermute | solution.py:146
  30.1 1.0 %copy-done.3 = bf16[128,3712]{1,0:T(8,128)(2,1)} copy-done((bf16[128,3712]{1,0:T(8,128)(2,1)}, bf16[128,3712]{1,0:T(8,128)(2,1)S(1)}, u32[]{:S(2)}) %copy-start.3) | copy-done | bytes 950296
  31.1 8.6 %expert.1 = (bf16[128,3584]{1,0:T(8,128)(2,1)}, bf16[128,3584]{1,0:T(8,128)(2,1)}) custom-call(s32[1]{0:T(128)} %bitcast.refs_0_, bf16[128,3712]{1,0:T(8,128)(2,1)} %bitcast.14, bf16[128,3712]{1,0:T(8,128)(2,1)} %copy-done.3, bf16[3584,512]{1,0:T(8,128)(2,1)} %bitcast.15, bf16[3584,512]{1,0:T(8,128)(2,1)} %bitcast.16, bf16[512,3584]{1,0:T(8,128)(2,1)} %bitcast.17), custom_call_target="tpu_custom_call" | custom-call | flops 2818572288 | bytes 14811136 | tf_op jit(solution)/shard_map/expert/pallas_call | solution.py:111
  39.7 0.2 collective-permute-start.2
  39.9 2.5 %collective-permute-done.2 = bf16[128,3584]{1,0:T(8,128)(2,1)S(1)} collective-permute-done((bf16[128,3584]{1,0:T(8,128)(2,1)}, bf16[128,3584]{1,0:T(8,128)(2,1)S(1)}, u32[]{:S(2)}, u32[]{:S(2)}) %collective-permute-start.2) | collective-permute-done | bytes 917536 | tf_op jit(solution)/shard_map/ppermute | solution.py:148
  42.4 2.4 %add_convert_fusion = bf16[128,3584]{1,0:T(8,128)(2,1)} fusion(bf16[128,3584]{1,0:T(8,128)(2,1)S(1)} %collective-permute-done.2, bf16[128,3584]{1,0:T(8,128)(2,1)} %get-tuple-element.4), kind=kLoop, calls=%fused_computation.2 | loop fusion | flops 1835008 | bytes 2752512 | tf_op jit(solution)/shard_map/convert_element_type | solution.py:149
  44.9 3.6 %all-to-all-start.1 = ((bf16[8,16,3584]{2,1,0:T(8,128)(2,1)}), bf16[8,16,3584]{2,1,0:T(8,128)(2,1)S(1)}, u32[]{:S(2)}, u32[]{:S(2)}) async-start(bf16[8,16,3584]{2,1,0:T(8,128)(2,1)} %bitcast.5), calls=%async_computation.1 | async-start | bytes 1835008 | tf_op jit(solution)/shard_map/all_to_all | solution.py:150
  48.4 0.1 iota_compare_fusion
  48.5 0.4 fusion.4
  48.9 0.2 fusion.9
  49.1 13.0 %all-to-all-done.1 = bf16[8,16,3584]{2,1,0:T(8,128)(2,1)S(1)} async-done(((bf16[8,16,3584]{2,1,0:T(8,128)(2,1)}), bf16[8,16,3584]{2,1,0:T(8,128)(2,1)S(1)}, u32[]{:S(2)}, u32[]{:S(2)}) %all-to-all-start.1) | async-done | bytes 917536 | tf_op jit(solution)/shard_map/all_to_all | solution.py:150
  62.1 0.1 convert_reduce_fusion
  62.2 4.0 %collective-permute-start.3 = (bf16[8,3584]{1,0:T(8,128)(2,1)S(1)}, bf16[8,3584]{1,0:T(8,128)(2,1)S(1)}, u32[]{:S(2)}, u32[]{:S(2)}) collective-permute-start(bf16[8,3584]{1,0:T(8,128)(2,1)S(1)} %slice.21), channel_id=1, source_target_pairs={{0,16},{16,0},{1,17},{17,1},{2,18},{18,2},{3,19},{19,3},{4,20},{20... | collective-permute-start | bytes 172040 | tf_op jit(solution)/shard_map/ppermute | solution.py:155
  66.2 1.0 %fusion.1 = bf16[1,8,64,512]{3,2,1,0:T(8,128)(2,1)S(1)} fusion(bf16[8,128,576]{1,2,0:T(8,128)(2,1)S(1)} %copy-done.2, f32[8,64]{1,0:T(8,128)S(1)} %fusion.9, f32[8,64,128]{2,1,0:T(8,128)S(1)} %fusion.4), kind=kOutput, calls=%fused_computation.4 | convolution fusion | flops 67568256 | bytes 2101248 | tf_op jit(solution)/shard_map/bht,btc->bhc/dot_general | solution.py:25
  67.2 1.1 %copy.13 = bf16[1,8,64,512]{3,1,2,0:T(8,128)(2,1)} copy(bf16[1,8,64,512]{3,2,1,0:T(8,128)(2,1)S(1)} %fusion.1) | data formatting | bytes 1048576
  68.3 1.3 %collective-permute-done.3 = bf16[8,3584]{1,0:T(8,128)(2,1)S(1)} collective-permute-done((bf16[8,3584]{1,0:T(8,128)(2,1)S(1)}, bf16[8,3584]{1,0:T(8,128)(2,1)S(1)}, u32[]{:S(2)}, u32[]{:S(2)}) %collective-permute-start.3) | collective-permute-done | bytes 57376 | tf_op jit(solution)/shard_map/ppermute | solution.py:155
  69.6 0.6 fusion.7
  (10 shorter events, 0.0 us)
Async XLA Ops:
  0.6 47.9 %copy-start = (bf16[8,64,576]{2,1,0:T(8,128)(2,1)S(1)}, bf16[8,64,576]{2,1,0:T(8,128)(2,1)}, u32[]{:S(2)}) copy-start(bf16[8,64,576]{2,1,0:T(8,128)(2,1)} %param.10) | copy-start | bytes 1769476
  2.3 7.1 %collective-permute-start = (bf16[8,3712]{1,0:T(8,128)(2,1)}, bf16[8,3712]{1,0:T(8,128)(2,1)S(1)}, u32[]{:S(2)}, u32[]{:S(2)}) collective-permute-start(bf16[8,3712]{1,0:T(8,128)(2,1)} %pack.1), channel_id=1, source_target_pairs={{0,16},{16,0},{1,17},{17,1},{2,18},{18,2},{3,19},{19,3},{4,20},{20... | collective-permute-start | bytes 178184 | tf_op jit(solution)/shard_map/ppermute | solution.py:141
  27.6 2.5 %copy-start.1 = (bf16[8,16,3712]{2,1,0:T(8,128)(2,1)}, bf16[8,16,3712]{2,1,0:T(8,128)(2,1)S(1)}, u32[]{:S(2)}) copy-start(bf16[8,16,3712]{2,1,0:T(8,128)(2,1)S(1)} %all_to_all.10) | copy-start | bytes 2850820
  27.6 2.5 %collective-permute-start.1 = (bf16[128,3712]{1,0:T(8,128)(2,1)S(1)}, bf16[128,3712]{1,0:T(8,128)(2,1)S(1)}, u32[]{:S(2)}, u32[]{:S(2)}) collective-permute-start(bf16[128,3712]{1,0:T(8,128)(2,1)S(1)} %bitcast.13), channel_id=1, source_target_pairs={{0,2},{2,0},{1,3},{3,1},{4,6},{6,4},{5,7},{7,5},{8,10},{10,8},{9,1... | collective-permute-start | bytes 2850824 | tf_op jit(solution)/shard_map/ppermute | solution.py:146
  30.1 1.0 %copy-start.3 = (bf16[128,3712]{1,0:T(8,128)(2,1)}, bf16[128,3712]{1,0:T(8,128)(2,1)S(1)}, u32[]{:S(2)}) copy-start(bf16[128,3712]{1,0:T(8,128)(2,1)S(1)} %collective-permute-done.1.refs_2_) | copy-start | bytes 2850820
  39.7 2.7 %collective-permute-start.2 = (bf16[128,3584]{1,0:T(8,128)(2,1)}, bf16[128,3584]{1,0:T(8,128)(2,1)S(1)}, u32[]{:S(2)}, u32[]{:S(2)}) collective-permute-start(bf16[128,3584]{1,0:T(8,128)(2,1)} %get-tuple-element.5), channel_id=1, source_target_pairs={{0,2},{2,0},{1,3},{3,1},{4,6},{6,4},{5,7},{7,5},{8,10},{10,8},{9,1... | collective-permute-start | bytes 2752520 | tf_op jit(solution)/shard_map/ppermute | solution.py:148
  42.4 6.0 %copy-start.4 = (s32[8]{0:T(128)S(1)}, s32[8]{0:T(128)}, u32[]{:S(2)}) copy-start(s32[8]{0:T(128)} %param.12) | copy-start | bytes 100
  42.4 6.1 %copy-start.2 = (bf16[8,128,576]{1,2,0:T(8,128)(2,1)S(1)}, bf16[8,128,576]{1,2,0:T(8,128)(2,1)}, u32[]{:S(2)}) copy-start(bf16[8,128,576]{1,2,0:T(8,128)(2,1)} %param.11) | copy-start | bytes 3538948
  44.9 17.2 %all-to-all-start.1 = ((bf16[8,16,3584]{2,1,0:T(8,128)(2,1)}), bf16[8,16,3584]{2,1,0:T(8,128)(2,1)S(1)}, u32[]{:S(2)}, u32[]{:S(2)}) async-start(bf16[8,16,3584]{2,1,0:T(8,128)(2,1)} %bitcast.5), calls=%async_computation.1 | async-start | bytes 1835008 | tf_op jit(solution)/shard_map/all_to_all | solution.py:150
  62.2 7.4 %collective-permute-start.3 = (bf16[8,3584]{1,0:T(8,128)(2,1)S(1)}, bf16[8,3584]{1,0:T(8,128)(2,1)S(1)}, u32[]{:S(2)}, u32[]{:S(2)}) collective-permute-start(bf16[8,3584]{1,0:T(8,128)(2,1)S(1)} %slice.21), channel_id=1, source_target_pairs={{0,16},{16,0},{1,17},{17,1},{2,18},{18,2},{3,19},{19,3},{4,20},{20... | collective-permute-start | bytes 172040 | tf_op jit(solution)/shard_map/ppermute | solution.py:155

commit v2 on v1

--- a/solution.py
+++ b/solution.py
@@ -55,81 +55,68 @@
     )(hidden, ids, weights)
 
 
-def expert_kernel(experts, chunk, me_ref, mine_ref, other_ref, gate_hbm, up_hbm, down_hbm, mine_out, other_out, rows_ref, gate_w, up_w, down_w, gate_acc, up_acc, sems):
-    half = mine_ref.shape[0]
-    width = mine_out.shape[1]
-    units = gate_w.shape[1]
-    steps = width // chunk
-    copies = []
-    for k in range(steps):
-        part = pl.ds(k * chunk, chunk)
-        copies.append(pltpu.make_async_copy(gate_hbm.at[part], gate_w.at[part], sems.at[0, k]))
-        copies.append(pltpu.make_async_copy(up_hbm.at[part], up_w.at[part], sems.at[1, k]))
-    for k in range(steps):
-        part = pl.ds(k * chunk, chunk)
-        copies.append(pltpu.make_async_copy(down_hbm.at[:, part], down_w.at[:, part], sems.at[2, k]))
-    for copy in copies:
-        copy.start()
-    rows_ref[:half] = mine_ref[...]
-    rows_ref[half:] = other_ref[...]
-    for k in range(steps):
-        copies[2 * k].wait()
-        copies[2 * k + 1].wait()
-        piece = rows_ref[:, k * chunk : (k + 1) * chunk]
-        gate = jnp.dot(piece, gate_w[k * chunk : (k + 1) * chunk], preferred_element_type=jnp.float32)
-        up = jnp.dot(piece, up_w[k * chunk : (k + 1) * chunk], preferred_element_type=jnp.float32)
-        if k == 0:
-            gate_acc[...] = gate
-            up_acc[...] = up
-        else:
-            gate_acc[...] += gate
-            up_acc[...] += up
-    gate = gate_acc[...]
-    act = (gate / (1.0 + jnp.exp(-gate)) * up_acc[...]).astype(jnp.bfloat16)
-    info = rows_ref[:, width:].astype(jnp.float32)
+def expert_kernel(experts, chunk, me_ref, mine_ref, other_ref, gate_w, up_w, down_w, mine_out, other_out):
+    half, width = mine_out.shape
+    info = jnp.concatenate([mine_ref[:, width:], other_ref[:, width:]], axis=0).astype(jnp.float32)
     lane = lax.broadcasted_iota(jnp.int32, info.shape, 1)
     me = me_ref[0]
     mask = (lane == me) | (lane == me + experts) | (lane == me + 2 * experts)
     weight = jnp.sum(jnp.where(mask, info, 0.0), axis=1, keepdims=True)
-    for k in range(steps):
-        copies[2 * steps + k].wait()
-        value = jnp.dot(act, down_w[:, k * chunk : (k + 1) * chunk], preferred_element_type=jnp.float32)
+    rows = jnp.concatenate([mine_ref[:, :width], other_ref[:, :width]], axis=0)
+    gate = jnp.dot(rows, gate_w[...], preferred_element_type=jnp.float32)
+    up = jnp.dot(rows, up_w[...], preferred_element_type=jnp.float32)
+    act = (gate / (1.0 + jnp.exp(-gate)) * up).astype(jnp.bfloat16)
+    for k in range(width // chunk):
+        part = slice(k * chunk, (k + 1) * chunk)
+        value = jnp.dot(act, down_w[:, part], preferred_element_type=jnp.float32)
         value = (value * weight).astype(jnp.bfloat16)
-        mine_out[:, k * chunk : (k + 1) * chunk] = value[:half]
-        other_out[:, k * chunk : (k + 1) * chunk] = value[half:]
+        mine_out[:, part] = value[:half]
+        other_out[:, part] = value[half:]
+
+
+def load_kernel(gate_hbm, up_hbm, down_hbm, gate_out, up_out, down_out, sems):
+    pairs = ((gate_hbm, gate_out), (up_hbm, up_out), (down_hbm, down_out))
+    copies = [pltpu.make_async_copy(a, b, sems.at[i]) for i, (a, b) in enumerate(pairs)]
+    for copy in copies:
+        copy.start()
+    for copy in copies:
+        copy.wait()
+
+
+def load(*matrices):
+    size = sum(m.size * m.dtype.itemsize for m in matrices)
+    return pl.pallas_call(
+        load_kernel,
+        out_shape=tuple(pltpu.VMEM(m.shape, m.dtype) for m in matrices),
+        in_specs=[pl.BlockSpec(memory_space=pltpu.HBM)] * len(matrices),
+        out_specs=tuple(pl.BlockSpec(memory_space=pltpu.VMEM) for _ in matrices),
+        scratch_shapes=[pltpu.SemaphoreType.DMA((len(matrices),))],
+        compiler_params=pltpu.CompilerParams(vmem_limit_bytes=1024 * 1024),
+        cost_estimate=pl.CostEstimate(flops=0, bytes_accessed=2 * size, transcendentals=0),
+        name="load",
+    )(*(pltpu.with_memory_space_constraint(m, pltpu.HBM) for m in matrices))
 
 
 def expert_values(mine, other, w_gate, w_up, w_down, experts):
     half, packed = mine.shape
     width, units = w_gate.shape
-    chunk = 512
-    steps = width // chunk
-    me = (lax.axis_index(("z1", "mid", "core"))).astype(jnp.int32).reshape(1)
+    me = lax.axis_index(("z1", "mid", "core")).astype(jnp.int32).reshape(1)
     vmem = pl.BlockSpec(memory_space=pltpu.VMEM)
-    hbm = pl.BlockSpec(memory_space=pl.ANY)
-    out = jax.ShapeDtypeStruct((half, width), jnp.bfloat16)
+    fast = lambda w: pltpu.with_memory_space_constraint(w, pltpu.VMEM)
+    out = pltpu.VMEM((half, width), jnp.bfloat16)
     return pl.pallas_call(
-        lambda *refs: expert_kernel(experts, chunk, *refs),
+        lambda *refs: expert_kernel(experts, 512, *refs),
         out_shape=(out, out),
-        in_specs=[pl.BlockSpec(memory_space=pltpu.SMEM), vmem, vmem, hbm, hbm, hbm],
+        in_specs=[pl.BlockSpec(memory_space=pltpu.SMEM)] + [vmem] * 5,
         out_specs=(vmem, vmem),
-        scratch_shapes=[
-            pltpu.VMEM((2 * half, packed), jnp.bfloat16),
-            pltpu.VMEM((width, units), jnp.bfloat16),
-            pltpu.VMEM((width, units), jnp.bfloat16),
-            pltpu.VMEM((units, width), jnp.bfloat16),
-            pltpu.VMEM((2 * half, units), jnp.float32),
-            pltpu.VMEM((2 * half, units), jnp.float32),
-            pltpu.SemaphoreType.DMA((3, steps)),
-        ],
-        compiler_params=pltpu.CompilerParams(vmem_limit_bytes=60 * 1024 * 1024),
+        compiler_params=pltpu.CompilerParams(vmem_limit_bytes=12 * 1024 * 1024),
         cost_estimate=pl.CostEstimate(
             flops=2 * 2 * half * width * units * 3,
             bytes_accessed=3 * width * units * 2 + 4 * half * packed * 2,
             transcendentals=2 * half * units,
         ),
         name="expert",
-    )(me, mine, other, w_gate, w_up, w_down)
+    )(me, fast(mine), fast(other), fast(w_gate), fast(w_up), fast(w_down))
 
 
 def routed_layer(hidden, ids, weights, w_gate, w_up, w_down):
@@ -144,7 +131,7 @@
     mine = lax.all_to_all(sending, ("mid", "local"), split_axis=0, concat_axis=0, tiled=True)
     mine = mine.reshape(block * 2 * rows, packed.shape[1])
     other = lax.ppermute(mine, "core", swap)
-    mine_out, other_out = expert_values(mine, other, w_gate[0], w_up[0], w_down[0], experts)
+    mine_out, other_out = expert_values(mine, other, *load(w_gate[0], w_up[0], w_down[0]), experts)
     from_other = lax.ppermute(other_out, "core", swap)
     total = (mine_out.astype(jnp.float32) + from_other.astype(jnp.float32)).astype(jnp.bfloat16)
     back = lax.all_to_all(

time: 70.6 us -> 64.7 us (0.916)
  waiting for transfers between devices: 22.3 us -> 19.6 us
  other arithmetic: 4.34 us -> 3.06 us
  Pallas kernels: 10.2 us -> 8.95 us
  local copies, waits for them, and re-layouts: 2.16 us -> 1.19 us
    ppermute x1, waiting for transfers between devices: 2.52 us -> 0.01 us  [routed_layer(): other = lax.ppermute(mine, 'core', swap)]
    convert_element_type x1, other arithmetic: 2.42 us -> 1.14 us  [routed_layer(): (mine_out.astype(jnp.float32) + from_other.astype(jnp.float32)).astype(jn...]
    pallas_call x1 -> x2, Pallas kernels: 8.57 us -> 7.33 us  [the longest x1 4.23 us: load(): pl.pallas_call(load_kernel, out_shape=tuple((pltpu.VMEM(m.shape, m.dtype)...]
    unnamed x11 -> x7, local copies, waits for them, and re-layouts: 2.09 us -> 1.12 us
  transfers between devices with their start and end apart: 5 -> 5, of which waited for: 5 -> 4; matrix products, arithmetic and copies ran while one was open for 4% -> 4% of each run, Pallas kernels for 0% -> 7%
where the time goes in v2:
time: 64.7 us; the launch traced here: 64.4 us
  waiting for transfers between devices  19.6 us (30%)
  blocking collectives  17.4 us (27%)
  starting transfers between devices  12.1 us (19%)
  Pallas kernels  8.95 us (14%)
  other arithmetic  3.06 us (5%)
  matrix products  1.37 us (2%)
  local copies, waits for them, and re-layouts  1.19 us (2%)
  between operations  0.72 us (1%)
    all_to_all x1, blocking collectives, routed_layer(): lax.all_to_all(sending, ('mid', 'local'), split_axis=0, concat_axis=0, ti...  17.4 us
    all_to_all x1, waiting for transfers between devices, routed_layer(): lax.all_to_all(total.reshape(block, 2 * rows, width), ('mid', 'local'), s...  13.2 us
    pallas_call x1, Pallas kernels, load(): pl.pallas_call(load_kernel, out_shape=tuple((pltpu.VMEM(m.shape, m.dtype)...  4.23 us
    ppermute x1, starting transfers between devices, routed_layer(): far = lax.ppermute(packed, 'z1', swap)  4.04 us
    ppermute x1, starting transfers between devices, routed_layer(): from_far = lax.ppermute(for_far, 'z1', swap)  3.97 us
    all_to_all x1, starting transfers between devices, routed_layer(): lax.all_to_all(total.reshape(block, 2 * rows, width), ('mid', 'local'), s...  3.55 us
    pallas_call x1, Pallas kernels, expert_values(): pl.pallas_call(lambda *refs: expert_kernel(experts, 512, *refs), out_shap...  3.1 us
    ppermute x1, waiting for transfers between devices, routed_layer(): far = lax.ppermute(packed, 'z1', swap)  3.02 us
  transfers between devices with their start and end apart: 5, of which 4 were waited for; matrix products, arithmetic and copies ran while one was open for 4% of the time, Pallas kernels for 7%

profile of v2, /device:TPU:0, one launch (start us, length us, event | category | flops | bytes accessed | tf_op | source)
XLA Modules:
  0.0 64.4 jit_solution(6338129366965161647)
XLA Ops:
  0.6 0.0 copy-start
  0.6 1.6 %pack.1 = bf16[8,3712]{1,0:T(8,128)(2,1)} custom-call(bf16[8,3584]{1,0:T(8,128)(2,1)} %refs_0_.1, s32[8,8]{1,0:T(8,128)} %refs_1_.1, f32[8,8]{1,0:T(8,128)} %refs_2_.1), custom_call_target="tpu_custom_call" | custom-call | tf_op jit(solution)/shard_map/pack/pallas_call | solution.py:51
  2.3 4.0 %collective-permute-start = (bf16[8,3712]{1,0:T(8,128)(2,1)}, bf16[8,3712]{1,0:T(8,128)(2,1)S(1)}, u32[]{:S(2)}, u32[]{:S(2)}) collective-permute-start(bf16[8,3712]{1,0:T(8,128)(2,1)} %pack.1), channel_id=1, source_target_pairs={{0,16},{16,0},{1,17},{17,1},{2,18},{18,2},{3,19},{19,3},{4,20},{20... | collective-permute-start | bytes 178184 | tf_op jit(solution)/shard_map/ppermute | solution.py:128
  6.3 3.0 %collective-permute-done = bf16[8,3712]{1,0:T(8,128)(2,1)S(1)} collective-permute-done((bf16[8,3712]{1,0:T(8,128)(2,1)}, bf16[8,3712]{1,0:T(8,128)(2,1)S(1)}, u32[]{:S(2)}, u32[]{:S(2)}) %collective-permute-start) | collective-permute-done | bytes 59424 | tf_op jit(solution)/shard_map/ppermute | solution.py:128
  9.3 0.8 %pad_maximum_fusion = bf16[16,3712]{1,0:T(8,128)(2,1)S(1)} fusion(bf16[8,3712]{1,0:T(8,128)(2,1)S(1)} %collective-permute-done, bf16[8,3712]{1,0:T(8,128)(2,1)} %pack.1), kind=kLoop, calls=%fused_computation.12 | loop fusion | flops 237568 | bytes 237568 | tf_op jit(solution)/shard_map/concatenate | solution.py:129
  10.2 0.1 broadcast_in_dim.23
  10.2 17.4 %all_to_all.10 = bf16[8,16,3712]{2,1,0:T(8,128)(2,1)S(1)} all-to-all(bf16[8,16,3712]{2,1,0:T(8,128)(2,1)S(1)} %broadcast_in_dim.23), channel_id=1, replica_groups=mesh['groups'=1,'z1'=2,'mid'=4,'core'=2,'local'=2] {'mid','local'}, dimensions={0} | all-to-all | bytes 1900544 | tf_op jit(solution)/shard_map/all_to_all | solution.py:131
  27.6 0.0 collective-permute-start.1
  27.6 4.2 %load.1 = (bf16[3584,512]{1,0:T(8,128)(2,1)S(1)}, bf16[3584,512]{1,0:T(8,128)(2,1)S(1)}, bf16[512,3584]{1,0:T(8,128)(2,1)S(1)}) custom-call(bf16[3584,512]{1,0:T(8,128)(2,1)} %bitcast.15, bf16[3584,512]{1,0:T(8,128)(2,1)} %bitcast.16, bf16[512,3584]{1,0:T(8,128)(2,1)} %bitcast.17), custom_call_target="tpu_custom_call" | custom-call | bytes 22020096 | tf_op jit(solution)/shard_map/load/pallas_call | solution.py:88
  31.9 3.1 %expert.1 = (bf16[128,3584]{1,0:T(8,128)(2,1)S(1)}, bf16[128,3584]{1,0:T(8,128)(2,1)S(1)}) custom-call(s32[1]{0:T(128)} %bitcast.refs_0_, bf16[128,3712]{1,0:T(8,128)(2,1)S(1)} %bitcast.14, bf16[128,3712]{1,0:T(8,128)(2,1)S(1)} %collective-permute-done.1.refs_2_, bf16[3584,512]{1,0:T(8,128)(2,1)S(1)} %get-tuple-element.7.refs_3_, ...), custom_call_target="tpu_custom_call" | custom-call | flops 2818572288 | bytes 14811136 | tf_op jit(solution)/shard_map/expert/pallas_call | solution.py:107
  35.0 0.6 collective-permute-start.2
  35.5 2.1 %collective-permute-done.2 = bf16[128,3584]{1,0:T(8,128)(2,1)S(1)} collective-permute-done((bf16[128,3584]{1,0:T(8,128)(2,1)S(1)}, bf16[128,3584]{1,0:T(8,128)(2,1)S(1)}, u32[]{:S(2)}, u32[]{:S(2)}) %collective-permute-start.2) | collective-permute-done | bytes 917536 | tf_op jit(solution)/shard_map/ppermute | solution.py:135
  37.6 1.1 %add_convert_fusion = bf16[128,3584]{1,0:T(8,128)(2,1)} fusion(bf16[128,3584]{1,0:T(8,128)(2,1)S(1)} %collective-permute-done.2, bf16[128,3584]{1,0:T(8,128)(2,1)S(1)} %get-tuple-element.10), kind=kLoop, calls=%fused_computation.2 | loop fusion | flops 1835008 | bytes 2752512 | tf_op jit(solution)/shard_map/convert_element_type | solution.py:136
  38.8 3.6 %all-to-all-start.1 = ((bf16[8,16,3584]{2,1,0:T(8,128)(2,1)}), bf16[8,16,3584]{2,1,0:T(8,128)(2,1)S(1)}, u32[]{:S(2)}, u32[]{:S(2)}) async-start(bf16[8,16,3584]{2,1,0:T(8,128)(2,1)} %bitcast.5), calls=%async_computation.1 | async-start | bytes 1835008 | tf_op jit(solution)/shard_map/all_to_all | solution.py:137
  42.3 0.1 iota_compare_fusion
  42.4 0.4 fusion.4
  42.8 0.2 fusion.9
  43.0 13.2 %all-to-all-done.1 = bf16[8,16,3584]{2,1,0:T(8,128)(2,1)S(1)} async-done(((bf16[8,16,3584]{2,1,0:T(8,128)(2,1)}), bf16[8,16,3584]{2,1,0:T(8,128)(2,1)S(1)}, u32[]{:S(2)}, u32[]{:S(2)}) %all-to-all-start.1) | async-done | bytes 917536 | tf_op jit(solution)/shard_map/all_to_all | solution.py:137
  56.3 0.1 convert_reduce_fusion
  56.4 4.0 %collective-permute-start.3 = (bf16[8,3584]{1,0:T(8,128)(2,1)S(1)}, bf16[8,3584]{1,0:T(8,128)(2,1)S(1)}, u32[]{:S(2)}, u32[]{:S(2)}) collective-permute-start(bf16[8,3584]{1,0:T(8,128)(2,1)S(1)} %slice.21), channel_id=1, source_target_pairs={{0,16},{16,0},{1,17},{17,1},{2,18},{18,2},{3,19},{19,3},{4,20},{20... | collective-permute-start | bytes 172040 | tf_op jit(solution)/shard_map/ppermute | solution.py:142
  60.4 1.0 %fusion.1 = bf16[1,8,64,512]{3,2,1,0:T(8,128)(2,1)S(1)} fusion(bf16[8,128,576]{1,2,0:T(8,128)(2,1)S(1)} %copy-done.1, f32[8,64]{1,0:T(8,128)S(1)} %fusion.9, f32[8,64,128]{2,1,0:T(8,128)S(1)} %fusion.4), kind=kOutput, calls=%fused_computation.4 | convolution fusion | flops 67568256 | bytes 2101248 | tf_op jit(solution)/shard_map/bht,btc->bhc/dot_general | solution.py:25
  61.4 1.1 %copy.13 = bf16[1,8,64,512]{3,1,2,0:T(8,128)(2,1)} copy(bf16[1,8,64,512]{3,2,1,0:T(8,128)(2,1)S(1)} %fusion.1) | data formatting | bytes 1048576
  62.5 1.3 %collective-permute-done.3 = bf16[8,3584]{1,0:T(8,128)(2,1)S(1)} collective-permute-done((bf16[8,3584]{1,0:T(8,128)(2,1)S(1)}, bf16[8,3584]{1,0:T(8,128)(2,1)S(1)}, u32[]{:S(2)}, u32[]{:S(2)}) %collective-permute-start.3) | collective-permute-done | bytes 57376 | tf_op jit(solution)/shard_map/ppermute | solution.py:142
  63.8 0.6 fusion.7
  (7 shorter events, 0.0 us)
Async XLA Ops:
  0.6 41.8 %copy-start = (bf16[8,64,576]{2,1,0:T(8,128)(2,1)S(1)}, bf16[8,64,576]{2,1,0:T(8,128)(2,1)}, u32[]{:S(2)}) copy-start(bf16[8,64,576]{2,1,0:T(8,128)(2,1)} %param.10) | copy-start | bytes 1769476
  2.3 7.1 %collective-permute-start = (bf16[8,3712]{1,0:T(8,128)(2,1)}, bf16[8,3712]{1,0:T(8,128)(2,1)S(1)}, u32[]{:S(2)}, u32[]{:S(2)}) collective-permute-start(bf16[8,3712]{1,0:T(8,128)(2,1)} %pack.1), channel_id=1, source_target_pairs={{0,16},{16,0},{1,17},{17,1},{2,18},{18,2},{3,19},{19,3},{4,20},{20... | collective-permute-start | bytes 178184 | tf_op jit(solution)/shard_map/ppermute | solution.py:128
  27.6 4.2 %collective-permute-start.1 = (bf16[128,3712]{1,0:T(8,128)(2,1)S(1)}, bf16[128,3712]{1,0:T(8,128)(2,1)S(1)}, u32[]{:S(2)}, u32[]{:S(2)}) collective-permute-start(bf16[128,3712]{1,0:T(8,128)(2,1)S(1)} %bitcast.13), channel_id=1, source_target_pairs={{0,2},{2,0},{1,3},{3,1},{4,6},{6,4},{5,7},{7,5},{8,10},{10,8},{9,1... | collective-permute-start | bytes 2850824 | tf_op jit(solution)/shard_map/ppermute | solution.py:133
  35.0 2.7 %collective-permute-start.2 = (bf16[128,3584]{1,0:T(8,128)(2,1)S(1)}, bf16[128,3584]{1,0:T(8,128)(2,1)S(1)}, u32[]{:S(2)}, u32[]{:S(2)}) collective-permute-start(bf16[128,3584]{1,0:T(8,128)(2,1)S(1)} %get-tuple-element.11), channel_id=1, source_target_pairs={{0,2},{2,0},{1,3},{3,1},{4,6},{6,4},{5,7},{7,5},{8,10},{10,8},{9,1... | collective-permute-start | bytes 2752520 | tf_op jit(solution)/shard_map/ppermute | solution.py:135
  37.6 4.7 %copy-start.2 = (s32[8]{0:T(128)S(1)}, s32[8]{0:T(128)}, u32[]{:S(2)}) copy-start(s32[8]{0:T(128)} %param.12) | copy-start | bytes 100
  37.6 4.8 %copy-start.1 = (bf16[8,128,576]{1,2,0:T(8,128)(2,1)S(1)}, bf16[8,128,576]{1,2,0:T(8,128)(2,1)}, u32[]{:S(2)}) copy-start(bf16[8,128,576]{1,2,0:T(8,128)(2,1)} %param.11) | copy-start | bytes 3538948
  38.8 17.5 %all-to-all-start.1 = ((bf16[8,16,3584]{2,1,0:T(8,128)(2,1)}), bf16[8,16,3584]{2,1,0:T(8,128)(2,1)S(1)}, u32[]{:S(2)}, u32[]{:S(2)}) async-start(bf16[8,16,3584]{2,1,0:T(8,128)(2,1)} %bitcast.5), calls=%async_computation.1 | async-start | bytes 1835008 | tf_op jit(solution)/shard_map/all_to_all | solution.py:137
  56.4 7.4 %collective-permute-start.3 = (bf16[8,3584]{1,0:T(8,128)(2,1)S(1)}, bf16[8,3584]{1,0:T(8,128)(2,1)S(1)}, u32[]{:S(2)}, u32[]{:S(2)}) collective-permute-start(bf16[8,3584]{1,0:T(8,128)(2,1)S(1)} %slice.21), channel_id=1, source_target_pairs={{0,16},{16,0},{1,17},{17,1},{2,18},{18,2},{3,19},{19,3},{4,20},{20... | collective-permute-start | bytes 172040 | tf_op jit(solution)/shard_map/ppermute | solution.py:142

commit v3 on v2

v3 whole, which is shorter than its diff:
```python
import jax
import jax.numpy as jnp
from jax import lax
from jax.experimental import pallas as pl
from jax.experimental.pallas import tpu as pltpu
from jax.sharding import PartitionSpec as P

LATENT = 512
LANES = 128
TERMS = 3

softmax_scale = 0.0722


def attend(queries, cache, lengths):
    scores = (
        jnp.einsum("bhd,btd->bht", queries, cache, preferred_element_type=jnp.float32)
        * softmax_scale
    )
    valid = lax.broadcasted_iota(jnp.int32, (1, 1, cache.shape[1]), 2) < lengths[:, None, None]
    scores = jnp.where(valid, scores, -1e30)
    highest = jnp.max(scores, axis=-1, keepdims=True)
    expo = jnp.exp(scores - highest)
    probs = (expo / jnp.sum(expo, axis=-1, keepdims=True)).astype(jnp.bfloat16)
    context = jnp.einsum(
        "bht,btc->bhc", probs, cache[:, :, :LATENT], preferred_element_type=jnp.float32
    )
    return context.astype(jnp.bfloat16).reshape(queries.shape[0], queries.shape[1] * LATENT)


def pack_kernel(experts, hidden_ref, ids_ref, weights_ref, out_ref):
    rows, width = hidden_ref.shape
    extra = out_ref.shape[1] - width
    out_ref[:, :width] = hidden_ref[...]
    lane = lax.broadcasted_iota(jnp.int32, (rows, extra), 1)
    expert, term = lane % experts, lane // experts
    dense = jnp.zeros((rows, extra), jnp.float32)
    for k in range(ids_ref.shape[1]):
        dense = dense + jnp.where(ids_ref[:, k : k + 1] == expert, weights_ref[:, k : k + 1], 0.0)
    high = dense.astype(jnp.bfloat16).astype(jnp.float32)
    rest = dense - high
    middle = rest.astype(jnp.bfloat16).astype(jnp.float32)
    low = rest - middle
    terms = jnp.where(term == 0, high, jnp.where(term == 1, middle, low))
    out_ref[:, width:] = jnp.where(term < TERMS, terms, 0.0).astype(jnp.bfloat16)


def pack(hidden, ids, weights, experts):
    rows, width = hidden.shape
    extra = -(-experts * TERMS // LANES) * LANES
    return pl.pallas_call(
        lambda *refs: pack_kernel(experts, *refs),
        out_shape=jax.ShapeDtypeStruct((rows, width + extra), jnp.bfloat16),
        name="pack",
    )(hidden, ids, weights)


def expert_kernel(experts, pieces, chunk, me_ref, *refs):
    ins, (gate_w, up_w, down_w), outs = refs[:pieces], refs[pieces : pieces + 3], refs[pieces + 3 :]
    step, width = outs[0].shape
    info = jnp.concatenate([ref[:, width:] for ref in ins], axis=0).astype(jnp.float32)
    lane = lax.broadcasted_iota(jnp.int32, info.shape, 1)
    me = me_ref[0]
    mask = (lane == me) | (lane == me + experts) | (lane == me + 2 * experts)
    weight = jnp.sum(jnp.where(mask, info, 0.0), axis=1, keepdims=True)
    rows = jnp.concatenate([ref[:, :width] for ref in ins], axis=0)
    gate = jnp.dot(rows, gate_w[...], preferred_element_type=jnp.float32)
    up = jnp.dot(rows, up_w[...], preferred_element_type=jnp.float32)
    act = (gate / (1.0 + jnp.exp(-gate)) * up).astype(jnp.bfloat16)
    for k in range(width // chunk):
        part = slice(k * chunk, (k + 1) * chunk)
        value = jnp.dot(act, down_w[:, part], preferred_element_type=jnp.float32)
        value = (value * weight).astype(jnp.bfloat16)
        for p in range(pieces):
            outs[p][:, part] = value[p * step : (p + 1) * step]


def expert_values(pieces, weights, experts):
    step, packed = pieces[0].shape
    width, units = weights[0].shape
    rows = step * len(pieces)
    me = lax.axis_index("nodes").astype(jnp.int32).reshape(1)
    vmem = pl.BlockSpec(memory_space=pltpu.VMEM)
    fast = lambda w: pltpu.with_memory_space_constraint(w, pltpu.VMEM)
    return pl.pallas_call(
        lambda *refs: expert_kernel(experts, len(pieces), 512, *refs),
        out_shape=tuple(pltpu.VMEM((step, width), jnp.bfloat16) for _ in pieces),
        in_specs=[pl.BlockSpec(memory_space=pltpu.SMEM)] + [vmem] * (len(pieces) + 3),
        out_specs=tuple(vmem for _ in pieces),
        compiler_params=pltpu.CompilerParams(vmem_limit_bytes=12 * 1024 * 1024),
        cost_estimate=pl.CostEstimate(
            flops=2 * rows * width * units * 3,
            bytes_accessed=3 * width * units * 2 + 2 * rows * packed * 2,
            transcendentals=rows * units,
        ),
        name="expert",
    )(me, *(fast(p) for p in pieces), *(fast(w) for w in weights))


def load_kernel(gate_hbm, up_hbm, down_hbm, gate_out, up_out, down_out, sems):
    pairs = ((gate_hbm, gate_out), (up_hbm, up_out), (down_hbm, down_out))
    copies = [pltpu.make_async_copy(a, b, sems.at[i]) for i, (a, b) in enumerate(pairs)]
    for copy in copies:
        copy.start()
    for copy in copies:
        copy.wait()


def load(*matrices):
    size = sum(m.size * m.dtype.itemsize for m in matrices)
    return pl.pallas_call(
        load_kernel,
        out_shape=tuple(pltpu.VMEM(m.shape, m.dtype) for m in matrices),
        in_specs=[pl.BlockSpec(memory_space=pltpu.HBM)] * len(matrices),
        out_specs=tuple(pl.BlockSpec(memory_space=pltpu.VMEM) for _ in matrices),
        scratch_shapes=[pltpu.SemaphoreType.DMA((len(matrices),))],
        compiler_params=pltpu.CompilerParams(vmem_limit_bytes=1024 * 1024),
        cost_estimate=pl.CostEstimate(flops=0, bytes_accessed=2 * size, transcendentals=0),
        name="load",
    )(*(pltpu.with_memory_space_constraint(m, pltpu.HBM) for m in matrices))


def flip(x, masks):
    axes = ("nodes", "local")
    core = lax.axis_size("local")
    count = core * lax.axis_size("nodes")
    return lax.ppermute(x, axes, [(i, i ^ masks[bool(i & core)]) for i in range(count)])


def add(*terms):
    total = terms[0].astype(jnp.float32)
    for term in terms[1:]:
        total = total + term.astype(jnp.float32)
    return total


def routed_layer(hidden, ids, weights, w_gate, w_up, w_down):
    width = hidden.shape[1]
    core, nodes = lax.axis_size("local"), lax.axis_size("nodes")
    experts = w_gate.shape[0] * nodes
    far_bit = core * nodes // 2
    cube = [1 << k for k in range((core * nodes).bit_length() - 1) if (1 << k) not in (core, far_bit)]
    turn = lambda k: cube[k:] + cube[:k]
    near_steps = list(zip(turn(0), turn(1)))
    far_steps = list(zip(turn(2), turn(0)))
    sibling, across = (core, core), (far_bit, far_bit)

    packed = pack(hidden, ids, weights, experts)
    loaded = load(w_gate[0], w_up[0], w_down[0])

    def gather(held, steps):
        for masks in steps[:-1]:
            held = jnp.concatenate([held, flip(held, masks)], axis=0)
        return held, flip(held, steps[-1])

    def scatter(low, high, from_low, from_high, steps):
        sent = flip(add(high, flip(from_high, sibling)).astype(jnp.bfloat16), steps[-1])
        held = add(low, flip(from_low, sibling), sent)
        for masks in steps[-2::-1]:
            half = held.shape[0] // 2
            sent = flip(held[half:].astype(jnp.bfloat16), masks)
            held = add(held[:half], sent)
        return held

    far = flip(packed, across)
    results = []
    for held, steps in ((packed, near_steps), (far, far_steps)):
        low, high = gather(held, steps)
        pieces = (low, high, flip(low, sibling), flip(high, sibling))
        results.append(scatter(*expert_values(pieces, loaded, experts), steps))
    near, far = results
    return add(near, flip(far.astype(jnp.bfloat16), across)).astype(jnp.bfloat16)


def on_device(hidden_in, queries, cache, lengths, expert_ids, gate_weights, w_gate, w_up, w_down):
    expert_out = routed_layer(hidden_in, expert_ids, gate_weights, w_gate, w_up, w_down)
    context = attend(queries, cache, lengths)
    return (context, expert_out)


def solution(mesh):
    every = ("groups", "nodes", "local")
    return jax.shard_map(
        on_device,
        mesh=mesh,
        in_specs=(
            P(every, None),
            P(every, None, None),
            P(every, None, None),
            P(every),
            P(every, None),
            P(every, None),
            P("nodes", None, "local"),
            P("nodes", None, "local"),
            P("nodes", "local", None),
        ),
        out_specs=(P(every, None), P(every, None)),
        check_vma=False,
    )
```

time: 64.7 us -> 57.6 us (0.89)
  blocking collectives: 17.4 us -> 0 us
  starting transfers between devices: 12.1 us -> 19.8 us
  waiting for transfers between devices: 19.6 us -> 22.9 us
  other arithmetic: 3.06 us -> 1.98 us
    all_to_all x1 -> x0, blocking collectives: 17.4 us -> none  [routed_layer(): lax.all_to_all(sending, ('mid', 'local'), split_axis=0, concat_axis=0, ti...]
    ppermute x4 -> x22, waiting for transfers between devices: 6.4 us -> 22.9 us  [flip(): lax.ppermute(x, axes, [(i, i ^ masks[bool(i & core)]) for i in range(coun...]
    all_to_all x1 -> x0, waiting for transfers between devices: 13.2 us -> none  [routed_layer(): lax.all_to_all(total.reshape(block, 2 * rows, width), ('mid', 'local'), s...]
    ppermute x4 -> x22, starting transfers between devices: 8.58 us -> 19.8 us  [flip(): lax.ppermute(x, axes, [(i, i ^ masks[bool(i & core)]) for i in range(coun...]
    all_to_all x1 -> x0, starting transfers between devices: 3.55 us -> none  [routed_layer(): lax.all_to_all(total.reshape(block, 2 * rows, width), ('mid', 'local'), s...]
    convert_element_type x2 -> x4, other arithmetic: 1.77 us -> 0.77 us  [the longest x1 0.65 us: routed_layer(): add(near, flip(far.astype(jnp.bfloat16), across)).astype(jnp.bfloat16)]
    concatenate x1 -> x3, other arithmetic: 0.83 us -> 0.04 us  [gather(): held = jnp.concatenate([held, flip(held, masks)], axis=0)]
    lt x1, other arithmetic: 0.07 us -> 0.73 us  [attend(): lax.broadcasted_iota(jnp.int32, (1, 1, cache.shape[1]), 2)]
  transfers between devices with their start and end apart: 5 -> 22, of which waited for: 4 -> 9; matrix products, arithmetic and copies ran while one was open for 4% -> 7% of each run, Pallas kernels for 7% -> 13%
where the time goes in v3:
time: 57.6 us; the launch traced here: 57.5 us
  waiting for transfers between devices  22.9 us (40%)
  starting transfers between devices  19.8 us (34%)
  Pallas kernels  9.38 us (16%)
  other arithmetic  1.98 us (3%)
  matrix products  1.37 us (2%)
  local copies, waits for them, and re-layouts  1.19 us (2%)
  between operations  0.81 us (1%)
    ppermute x22, waiting for transfers between devices, flip(): lax.ppermute(x, axes, [(i, i ^ masks[bool(i & core)]) for i in range(coun...  22.9 us
    ppermute x22, starting transfers between devices, flip(): lax.ppermute(x, axes, [(i, i ^ masks[bool(i & core)]) for i in range(coun...  19.8 us
    pallas_call x1, Pallas kernels, load(): pl.pallas_call(load_kernel, out_shape=tuple((pltpu.VMEM(m.shape, m.dtype)...  4.31 us
    pallas_call x2, Pallas kernels, expert_values(): pl.pallas_call(lambda *refs: expert_kernel(experts, len(pieces), 512, *re...  3.44 us
    pallas_call x1, Pallas kernels, pack(): pl.pallas_call(lambda *refs: pack_kernel(experts, *refs), out_shape=jax.S...  1.63 us
  transfers between devices with their start and end apart: 22, of which 9 were waited for; matrix products, arithmetic and copies ran while one was open for 7% of the time, Pallas kernels for 13%

profile of v3, /device:TPU:0, one launch (start us, length us, event | category | flops | bytes accessed | tf_op | source)
XLA Modules:
  0.0 57.5 jit_solution(13745166946072836477)
XLA Ops:
  0.6 1.6 %pack.1 = bf16[8,3712]{1,0:T(8,128)(2,1)} custom-call(bf16[8,3584]{1,0:T(8,128)(2,1)} %refs_0_.1, s32[8,8]{1,0:T(8,128)} %refs_1_.1, f32[8,8]{1,0:T(8,128)} %refs_2_.1), custom_call_target="tpu_custom_call" | custom-call | tf_op jit(solution)/shard_map/pack/pallas_call | solution.py:51
  2.3 4.0 %collective-permute-start.10 = (bf16[8,3712]{1,0:T(8,128)(2,1)}, bf16[8,3712]{1,0:T(8,128)(2,1)S(1)}, u32[]{:S(2)}, u32[]{:S(2)}) collective-permute-start(bf16[8,3712]{1,0:T(8,128)(2,1)} %pack.1), channel_id=1, source_target_pairs={{0,16},{1,17},{2,18},{3,19},{4,20},{5,21},{6,22},{7,23},{8,24},{9,... | collective-permute-start | bytes 178184 | tf_op jit(solution)/shard_map/ppermute | solution.py:127
  6.3 1.5 %collective-permute-start = (bf16[8,3712]{1,0:T(8,128)(2,1)}, bf16[8,3712]{1,0:T(8,128)(2,1)S(1)}, u32[]{:S(2)}, u32[]{:S(2)}) collective-permute-start(bf16[8,3712]{1,0:T(8,128)(2,1)} %pack.1), channel_id=1, source_target_pairs={{0,1},{1,0},{2,6},{3,7},{4,5},{5,4},{6,2},{7,3},{8,9},{9,8},{10,14... | collective-permute-start | bytes 178184 | tf_op jit(solution)/shard_map/ppermute | solution.py:127
  7.8 0.7 %iota_compare_fusion = pred[8,128]{1,0:T(8,128)(4,1)S(1)} fusion(s32[8]{0:T(128)} %param.12), kind=kLoop, calls=%fused_computation.31 | loop fusion | flops 1024 | bytes 1056 | tf_op jit(solution)/shard_map/lt | solution.py:20
  8.5 4.3 %load.1 = (bf16[3584,512]{1,0:T(8,128)(2,1)S(1)}, bf16[3584,512]{1,0:T(8,128)(2,1)S(1)}, bf16[512,3584]{1,0:T(8,128)(2,1)S(1)}) custom-call(bf16[3584,512]{1,0:T(8,128)(2,1)} %bitcast.11, bf16[3584,512]{1,0:T(8,128)(2,1)} %bitcast.12, bf16[512,3584]{1,0:T(8,128)(2,1)} %bitcast.13), custom_call_target="tpu_custom_call" | custom-call | bytes 22020096 | tf_op jit(solution)/shard_map/load/pallas_call | solution.py:111
  12.9 1.6 %collective-permute-start.1 = (bf16[16,3712]{1,0:T(8,128)(2,1)S(1)}, bf16[16,3712]{1,0:T(8,128)(2,1)S(1)}, u32[]{:S(2)}, u32[]{:S(2)}) collective-permute-start(bf16[16,3712]{1,0:T(8,128)(2,1)S(1)} %pad_maximum_fusion.1), channel_id=1, source_target_pairs={{0,4},{1,5},{2,10},{3,11},{4,0},{5,1},{6,14},{7,15},{8,12},{9,13},... | collective-permute-start | bytes 356360 | tf_op jit(solution)/shard_map/ppermute | solution.py:127
  14.5 1.6 %collective-permute-start.11 = (bf16[8,3712]{1,0:T(8,128)(2,1)S(1)}, bf16[8,3712]{1,0:T(8,128)(2,1)S(1)}, u32[]{:S(2)}, u32[]{:S(2)}) collective-permute-start(bf16[8,3712]{1,0:T(8,128)(2,1)S(1)} %collective-permute-done.10), channel_id=1, source_target_pairs={{0,8},{1,9},{2,3},{3,2},{4,12},{5,13},{6,7},{7,6},{8,0},{9,1},{10,... | collective-permute-start | bytes 178184 | tf_op jit(solution)/shard_map/ppermute | solution.py:127
  16.1 2.6 %collective-permute-done.11 = bf16[8,3712]{1,0:T(8,128)(2,1)S(1)} collective-permute-done((bf16[8,3712]{1,0:T(8,128)(2,1)S(1)}, bf16[8,3712]{1,0:T(8,128)(2,1)S(1)}, u32[]{:S(2)}, u32[]{:S(2)}) %collective-permute-start.11) | collective-permute-done | bytes 59424 | tf_op jit(solution)/shard_map/ppermute | solution.py:127
  19.3 4.4 %collective-permute-done.12 = bf16[16,3712]{1,0:T(8,128)(2,1)S(1)} collective-permute-done((bf16[16,3712]{1,0:T(8,128)(2,1)S(1)}, bf16[16,3712]{1,0:T(8,128)(2,1)S(1)}, u32[]{:S(2)}, u32[]{:S(2)}) %collective-permute-start.12) | collective-permute-done | bytes 118816 | tf_op jit(solution)/shard_map/ppermute | solution.py:127
  24.2 1.8 %collective-permute-start.2 = (bf16[32,3712]{1,0:T(8,128)(2,1)S(1)}, bf16[32,3712]{1,0:T(8,128)(2,1)S(1)}, u32[]{:S(2)}, u32[]{:S(2)}) collective-permute-start(bf16[32,3712]{1,0:T(8,128)(2,1)S(1)} %pad_maximum_fusion.refs_1_), channel_id=1, source_target_pairs={{0,8},{1,9},{2,3},{3,2},{4,12},{5,13},{6,7},{7,6},{8,0},{9,1},{10,... | collective-permute-start | bytes 712712 | tf_op jit(solution)/shard_map/ppermute | solution.py:127
  26.1 3.8 %collective-permute-done.13.refs_2_ = bf16[32,3712]{1,0:T(8,128)(2,1)S(1)} collective-permute-done((bf16[32,3712]{1,0:T(8,128)(2,1)S(1)}, bf16[32,3712]{1,0:T(8,128)(2,1)S(1)}, u32[]{:S(2)}, u32[]{:S(2)}) %collective-permute-start.13) | collective-permute-done | bytes 237600 | tf_op jit(solution)/shard_map/ppermute | solution.py:127
  31.4 1.7 %expert.3 = (bf16[32,3584]{1,0:T(8,128)(2,1)S(1)}, bf16[32,3584]{1,0:T(8,128)(2,1)S(1)}, bf16[32,3584]{1,0:T(8,128)(2,1)S(1)}, bf16[32,3584]{1,0:T(8,128)(2,1)S(1)}) custom-call(s32[1]{0:T(128)} %bitcast.refs_0_, bf16[32,3712]{1,0:T(8,128)(2,1)S(1)} %constant_dynamic-update-slice_fusion.refs_1_, bf16[32,3712]{1,0:T(8,128)(2,1)S(1)} %collective-permute-done.13.refs_2_, ...), custom_call_target="tpu_custom_call" | custom-call | flops 1409286144 | bytes 12910592 | tf_op jit(solution)/shard_map/expert/pallas_call | solution.py:85
  33.6 1.7 %expert.2 = (bf16[32,3584]{1,0:T(8,128)(2,1)S(1)}, bf16[32,3584]{1,0:T(8,128)(2,1)S(1)}, bf16[32,3584]{1,0:T(8,128)(2,1)S(1)}, bf16[32,3584]{1,0:T(8,128)(2,1)S(1)}) custom-call(s32[1]{0:T(128)} %bitcast.refs_0_, bf16[32,3712]{1,0:T(8,128)(2,1)S(1)} %pad_maximum_fusion.refs_1_, bf16[32,3712]{1,0:T(8,128)(2,1)S(1)} %collective-permute-done.2.refs_2_, ...), custom_call_target="tpu_custom_call" | custom-call | flops 1409286144 | bytes 12910592 | tf_op jit(solution)/shard_map/expert/pallas_call | solution.py:85
  36.3 0.8 %collective-permute-start.18 = (bf16[32,3584]{1,0:T(8,128)(2,1)S(1)}, bf16[32,3584]{1,0:T(8,128)(2,1)S(1)}, u32[]{:S(2)}, u32[]{:S(2)}) collective-permute-start(bf16[32,3584]{1,0:T(8,128)(2,1)S(1)} %add_convert_fusion), channel_id=1, source_target_pairs={{0,4},{1,5},{2,10},{3,11},{4,0},{5,1},{6,14},{7,15},{8,12},{9,13},... | collective-permute-start | bytes 688136 | tf_op jit(solution)/shard_map/ppermute | solution.py:127
  37.2 1.5 %collective-permute-start.7 = (bf16[32,3584]{1,0:T(8,128)(2,1)S(1)}, bf16[32,3584]{1,0:T(8,128)(2,1)S(1)}, u32[]{:S(2)}, u32[]{:S(2)}) collective-permute-start(bf16[32,3584]{1,0:T(8,128)(2,1)S(1)} %add_convert_fusion.1), channel_id=1, source_target_pairs={{0,8},{1,9},{2,3},{3,2},{4,12},{5,13},{6,7},{7,6},{8,0},{9,1},{10,... | collective-permute-start | bytes 688136 | tf_op jit(solution)/shard_map/ppermute | solution.py:127
  38.7 3.7 %collective-permute-done.18 = bf16[32,3584]{1,0:T(8,128)(2,1)S(1)} collective-permute-done((bf16[32,3584]{1,0:T(8,128)(2,1)S(1)}, bf16[32,3584]{1,0:T(8,128)(2,1)S(1)}, u32[]{:S(2)}, u32[]{:S(2)}) %collective-permute-start.18) | collective-permute-done | bytes 229408 | tf_op jit(solution)/shard_map/ppermute | solution.py:127
  43.0 1.0 %collective-permute-done.7 = bf16[32,3584]{1,0:T(8,128)(2,1)S(1)} collective-permute-done((bf16[32,3584]{1,0:T(8,128)(2,1)S(1)}, bf16[32,3584]{1,0:T(8,128)(2,1)S(1)}, u32[]{:S(2)}, u32[]{:S(2)}) %collective-permute-start.7) | collective-permute-done | bytes 229408 | tf_op jit(solution)/shard_map/ppermute | solution.py:127
  44.1 1.1 %collective-permute-start.8 = (bf16[16,3584]{1,0:T(8,128)(2,1)S(1)}, bf16[16,3584]{1,0:T(8,128)(2,1)S(1)}, u32[]{:S(2)}, u32[]{:S(2)}) collective-permute-start(bf16[16,3584]{1,0:T(8,128)(2,1)S(1)} %slice.65), channel_id=1, source_target_pairs={{0,4},{1,5},{2,10},{3,11},{4,0},{5,1},{6,14},{7,15},{8,12},{9,13},... | collective-permute-start | bytes 344072 | tf_op jit(solution)/shard_map/ppermute | solution.py:127
  45.2 2.2 %collective-permute-done.19 = bf16[16,3584]{1,0:T(8,128)(2,1)S(1)} collective-permute-done((bf16[16,3584]{1,0:T(8,128)(2,1)S(1)}, bf16[16,3584]{1,0:T(8,128)(2,1)S(1)}, u32[]{:S(2)}, u32[]{:S(2)}) %collective-permute-start.19) | collective-permute-done | bytes 114720 | tf_op jit(solution)/shard_map/ppermute | solution.py:127
  47.4 1.5 %collective-permute-start.20 = (bf16[8,3584]{1,0:T(8,128)(2,1)S(1)}, bf16[8,3584]{1,0:T(8,128)(2,1)S(1)}, u32[]{:S(2)}, u32[]{:S(2)}) collective-permute-start(bf16[8,3584]{1,0:T(8,128)(2,1)S(1)} %slice.66), channel_id=1, source_target_pairs={{0,8},{1,9},{2,3},{3,2},{4,12},{5,13},{6,7},{7,6},{8,0},{9,1},{10,... | collective-permute-start | bytes 172040 | tf_op jit(solution)/shard_map/ppermute | solution.py:127
  49.7 2.0 %collective-permute-done.20 = bf16[8,3584]{1,0:T(8,128)(2,1)S(1)} collective-permute-done((bf16[8,3584]{1,0:T(8,128)(2,1)S(1)}, bf16[8,3584]{1,0:T(8,128)(2,1)S(1)}, u32[]{:S(2)}, u32[]{:S(2)}) %collective-permute-start.20) | collective-permute-done | bytes 57376 | tf_op jit(solution)/shard_map/ppermute | solution.py:127
  52.1 1.0 %fusion.1 = bf16[1,8,64,512]{3,2,1,0:T(8,128)(2,1)S(1)} fusion(bf16[8,128,576]{1,2,0:T(8,128)(2,1)S(1)} %copy-done.1, f32[8,64]{1,0:T(8,128)S(1)} %fusion.11, f32[8,64,128]{2,1,0:T(8,128)S(1)} %fusion.4), kind=kOutput, calls=%fused_computation.2 | convolution fusion | flops 67568256 | bytes 2101248 | tf_op jit(solution)/shard_map/bht,btc->bhc/dot_general | solution.py:25
  53.1 1.1 %copy.13 = bf16[1,8,64,512]{3,1,2,0:T(8,128)(2,1)} copy(bf16[1,8,64,512]{3,2,1,0:T(8,128)(2,1)S(1)} %fusion.1) | data formatting | bytes 1048576
  54.2 2.6 %collective-permute-done.21 = bf16[8,3584]{1,0:T(8,128)(2,1)S(1)} collective-permute-done((bf16[8,3584]{1,0:T(8,128)(2,1)S(1)}, bf16[8,3584]{1,0:T(8,128)(2,1)S(1)}, u32[]{:S(2)}, u32[]{:S(2)}) %collective-permute-start.21) | collective-permute-done | bytes 57376 | tf_op jit(solution)/shard_map/ppermute | solution.py:127
  (53 shorter events, 6.7 us)
Async XLA Ops:
  0.6 29.3 %copy-start = (bf16[8,64,576]{2,1,0:T(8,128)(2,1)S(1)}, bf16[8,64,576]{2,1,0:T(8,128)(2,1)}, u32[]{:S(2)}) copy-start(bf16[8,64,576]{2,1,0:T(8,128)(2,1)} %param.10) | copy-start | bytes 1769476
  2.3 12.2 %collective-permute-start.10 = (bf16[8,3712]{1,0:T(8,128)(2,1)}, bf16[8,3712]{1,0:T(8,128)(2,1)S(1)}, u32[]{:S(2)}, u32[]{:S(2)}) collective-permute-start(bf16[8,3712]{1,0:T(8,128)(2,1)} %pack.1), channel_id=1, source_target_pairs={{0,16},{1,17},{2,18},{3,19},{4,20},{5,21},{6,22},{7,23},{8,24},{9,... | collective-permute-start | bytes 178184 | tf_op jit(solution)/shard_map/ppermute | solution.py:127
  6.3 6.5 %collective-permute-start = (bf16[8,3712]{1,0:T(8,128)(2,1)}, bf16[8,3712]{1,0:T(8,128)(2,1)S(1)}, u32[]{:S(2)}, u32[]{:S(2)}) collective-permute-start(bf16[8,3712]{1,0:T(8,128)(2,1)} %pack.1), channel_id=1, source_target_pairs={{0,1},{1,0},{2,6},{3,7},{4,5},{5,4},{6,2},{7,3},{8,9},{9,8},{10,14... | collective-permute-start | bytes 178184 | tf_op jit(solution)/shard_map/ppermute | solution.py:127
  8.5 21.4 %copy-start.1 = (bf16[8,128,576]{1,2,0:T(8,128)(2,1)S(1)}, bf16[8,128,576]{1,2,0:T(8,128)(2,1)}, u32[]{:S(2)}) copy-start(bf16[8,128,576]{1,2,0:T(8,128)(2,1)} %param.11) | copy-start | bytes 3538948
  12.9 11.3 %collective-permute-start.1 = (bf16[16,3712]{1,0:T(8,128)(2,1)S(1)}, bf16[16,3712]{1,0:T(8,128)(2,1)S(1)}, u32[]{:S(2)}, u32[]{:S(2)}) collective-permute-start(bf16[16,3712]{1,0:T(8,128)(2,1)S(1)} %pad_maximum_fusion.1), channel_id=1, source_target_pairs={{0,4},{1,5},{2,10},{3,11},{4,0},{5,1},{6,14},{7,15},{8,12},{9,13},... | collective-permute-start | bytes 356360 | tf_op jit(solution)/shard_map/ppermute | solution.py:127
  14.5 4.2 %collective-permute-start.11 = (bf16[8,3712]{1,0:T(8,128)(2,1)S(1)}, bf16[8,3712]{1,0:T(8,128)(2,1)S(1)}, u32[]{:S(2)}, u32[]{:S(2)}) collective-permute-start(bf16[8,3712]{1,0:T(8,128)(2,1)S(1)} %collective-permute-done.10), channel_id=1, source_target_pairs={{0,8},{1,9},{2,3},{3,2},{4,12},{5,13},{6,7},{7,6},{8,0},{9,1},{10,... | collective-permute-start | bytes 178184 | tf_op jit(solution)/shard_map/ppermute | solution.py:127
  18.7 5.0 %collective-permute-start.12 = (bf16[16,3712]{1,0:T(8,128)(2,1)S(1)}, bf16[16,3712]{1,0:T(8,128)(2,1)S(1)}, u32[]{:S(2)}, u32[]{:S(2)}) collective-permute-start(bf16[16,3712]{1,0:T(8,128)(2,1)S(1)} %pad_maximum_fusion.2), channel_id=1, source_target_pairs={{0,1},{1,0},{2,6},{3,7},{4,5},{5,4},{6,2},{7,3},{8,9},{9,8},{10,14... | collective-permute-start | bytes 356360 | tf_op jit(solution)/shard_map/ppermute | solution.py:127
  23.7 6.2 %collective-permute-start.13 = (bf16[32,3712]{1,0:T(8,128)(2,1)S(1)}, bf16[32,3712]{1,0:T(8,128)(2,1)S(1)}, u32[]{:S(2)}, u32[]{:S(2)}) collective-permute-start(bf16[32,3712]{1,0:T(8,128)(2,1)S(1)} %constant_dynamic-update-slice_fusion.refs_1_), channel_id=1, source_target_pairs={{0,4},{1,5},{2,10},{3,11},{4,0},{5,1},{6,14},{7,15},{8,12},{9,13},... | collective-permute-start | bytes 712712 | tf_op jit(solution)/shard_map/ppermute | solution.py:127
  24.2 6.7 %collective-permute-start.2 = (bf16[32,3712]{1,0:T(8,128)(2,1)S(1)}, bf16[32,3712]{1,0:T(8,128)(2,1)S(1)}, u32[]{:S(2)}, u32[]{:S(2)}) collective-permute-start(bf16[32,3712]{1,0:T(8,128)(2,1)S(1)} %pad_maximum_fusion.refs_1_), channel_id=1, source_target_pairs={{0,8},{1,9},{2,3},{3,2},{4,12},{5,13},{6,7},{7,6},{8,0},{9,1},{10,... | collective-permute-start | bytes 712712 | tf_op jit(solution)/shard_map/ppermute | solution.py:127
  26.0 4.9 %collective-permute-start.14 = (bf16[32,3712]{1,0:T(8,128)(2,1)S(1)}, bf16[32,3712]{1,0:T(8,128)(2,1)S(1)}, u32[]{:S(2)}, u32[]{:S(2)}) collective-permute-start(bf16[32,3712]{1,0:T(8,128)(2,1)S(1)} %constant_dynamic-update-slice_fusion.refs_1_), channel_id=1, source_target_pairs={{0,2},{1,3},{2,0},{3,1},{4,6},{5,7},{6,4},{7,5},{8,10},{9,11},{10,... | collective-permute-start | bytes 712712 | tf_op jit(solution)/shard_map/ppermute | solution.py:127
  29.9 1.5 %collective-permute-start.15 = (bf16[32,3712]{1,0:T(8,128)(2,1)S(1)}, bf16[32,3712]{1,0:T(8,128)(2,1)S(1)}, u32[]{:S(2)}, u32[]{:S(2)}) collective-permute-start(bf16[32,3712]{1,0:T(8,128)(2,1)S(1)} %collective-permute-done.13.refs_2_), channel_id=1, source_target_pairs={{0,2},{1,3},{2,0},{3,1},{4,6},{5,7},{6,4},{7,5},{8,10},{9,11},{10,... | collective-permute-start | bytes 712712 | tf_op jit(solution)/shard_map/ppermute | solution.py:127
  30.3 3.3 %collective-permute-start.3 = (bf16[32,3712]{1,0:T(8,128)(2,1)S(1)}, bf16[32,3712]{1,0:T(8,128)(2,1)S(1)}, u32[]{:S(2)}, u32[]{:S(2)}) collective-permute-start(bf16[32,3712]{1,0:T(8,128)(2,1)S(1)} %pad_maximum_fusion.refs_1_), channel_id=1, source_target_pairs={{0,2},{1,3},{2,0},{3,1},{4,6},{5,7},{6,4},{7,5},{8,10},{9,11},{10,... | collective-permute-start | bytes 712712 | tf_op jit(solution)/shard_map/ppermute | solution.py:127
  30.9 2.7 %collective-permute-start.4 = (bf16[32,3712]{1,0:T(8,128)(2,1)S(1)}, bf16[32,3712]{1,0:T(8,128)(2,1)S(1)}, u32[]{:S(2)}, u32[]{:S(2)}) collective-permute-start(bf16[32,3712]{1,0:T(8,128)(2,1)S(1)} %collective-permute-done.2.refs_2_), channel_id=1, source_target_pairs={{0,2},{1,3},{2,0},{3,1},{4,6},{5,7},{6,4},{7,5},{8,10},{9,11},{10,... | collective-permute-start | bytes 712712 | tf_op jit(solution)/shard_map/ppermute | solution.py:127
  33.1 3.2 %collective-permute-start.17 = (bf16[32,3584]{1,0:T(8,128)(2,1)S(1)}, bf16[32,3584]{1,0:T(8,128)(2,1)S(1)}, u32[]{:S(2)}, u32[]{:S(2)}) collective-permute-start(bf16[32,3584]{1,0:T(8,128)(2,1)S(1)} %get-tuple-element.23), channel_id=1, source_target_pairs={{0,2},{1,3},{2,0},{3,1},{4,6},{5,7},{6,4},{7,5},{8,10},{9,11},{10,... | collective-permute-start | bytes 688136 | tf_op jit(solution)/shard_map/ppermute | solution.py:127
  35.3 1.8 %collective-permute-start.6 = (bf16[32,3584]{1,0:T(8,128)(2,1)S(1)}, bf16[32,3584]{1,0:T(8,128)(2,1)S(1)}, u32[]{:S(2)}, u32[]{:S(2)}) collective-permute-start(bf16[32,3584]{1,0:T(8,128)(2,1)S(1)} %get-tuple-element.19), channel_id=1, source_target_pairs={{0,2},{1,3},{2,0},{3,1},{4,6},{5,7},{6,4},{7,5},{8,10},{9,11},{10,... | collective-permute-start | bytes 688136 | tf_op jit(solution)/shard_map/ppermute | solution.py:127
  35.8 7.3 %collective-permute-start.5 = (bf16[32,3584]{1,0:T(8,128)(2,1)S(1)}, bf16[32,3584]{1,0:T(8,128)(2,1)S(1)}, u32[]{:S(2)}, u32[]{:S(2)}) collective-permute-start(bf16[32,3584]{1,0:T(8,128)(2,1)S(1)} %get-tuple-element.17), channel_id=1, source_target_pairs={{0,2},{1,3},{2,0},{3,1},{4,6},{5,7},{6,4},{7,5},{8,10},{9,11},{10,... | collective-permute-start | bytes 688136 | tf_op jit(solution)/shard_map/ppermute | solution.py:127
  35.9 2.8 %collective-permute-start.16 = (bf16[32,3584]{1,0:T(8,128)(2,1)S(1)}, bf16[32,3584]{1,0:T(8,128)(2,1)S(1)}, u32[]{:S(2)}, u32[]{:S(2)}) collective-permute-start(bf16[32,3584]{1,0:T(8,128)(2,1)S(1)} %get-tuple-element.21), channel_id=1, source_target_pairs={{0,2},{1,3},{2,0},{3,1},{4,6},{5,7},{6,4},{7,5},{8,10},{9,11},{10,... | collective-permute-start | bytes 688136 | tf_op jit(solution)/shard_map/ppermute | solution.py:127
  36.3 6.1 %collective-permute-start.18 = (bf16[32,3584]{1,0:T(8,128)(2,1)S(1)}, bf16[32,3584]{1,0:T(8,128)(2,1)S(1)}, u32[]{:S(2)}, u32[]{:S(2)}) collective-permute-start(bf16[32,3584]{1,0:T(8,128)(2,1)S(1)} %add_convert_fusion), channel_id=1, source_target_pairs={{0,4},{1,5},{2,10},{3,11},{4,0},{5,1},{6,14},{7,15},{8,12},{9,13},... | collective-permute-start | bytes 688136 | tf_op jit(solution)/shard_map/ppermute | solution.py:127
  37.2 6.9 %collective-permute-start.7 = (bf16[32,3584]{1,0:T(8,128)(2,1)S(1)}, bf16[32,3584]{1,0:T(8,128)(2,1)S(1)}, u32[]{:S(2)}, u32[]{:S(2)}) collective-permute-start(bf16[32,3584]{1,0:T(8,128)(2,1)S(1)} %add_convert_fusion.1), channel_id=1, source_target_pairs={{0,8},{1,9},{2,3},{3,2},{4,12},{5,13},{6,7},{7,6},{8,0},{9,1},{10,... | collective-permute-start | bytes 688136 | tf_op jit(solution)/shard_map/ppermute | solution.py:127
  42.5 4.9 %collective-permute-start.19 = (bf16[16,3584]{1,0:T(8,128)(2,1)S(1)}, bf16[16,3584]{1,0:T(8,128)(2,1)S(1)}, u32[]{:S(2)}, u32[]{:S(2)}) collective-permute-start(bf16[16,3584]{1,0:T(8,128)(2,1)S(1)} %slice.64), channel_id=1, source_target_pairs={{0,1},{1,0},{2,6},{3,7},{4,5},{5,4},{6,2},{7,3},{8,9},{9,8},{10,14... | collective-permute-start | bytes 344072 | tf_op jit(solution)/shard_map/ppermute | solution.py:127
  44.1 4.9 %collective-permute-start.8 = (bf16[16,3584]{1,0:T(8,128)(2,1)S(1)}, bf16[16,3584]{1,0:T(8,128)(2,1)S(1)}, u32[]{:S(2)}, u32[]{:S(2)}) collective-permute-start(bf16[16,3584]{1,0:T(8,128)(2,1)S(1)} %slice.65), channel_id=1, source_target_pairs={{0,4},{1,5},{2,10},{3,11},{4,0},{5,1},{6,14},{7,15},{8,12},{9,13},... | collective-permute-start | bytes 344072 | tf_op jit(solution)/shard_map/ppermute | solution.py:127
  47.4 4.2 %collective-permute-start.20 = (bf16[8,3584]{1,0:T(8,128)(2,1)S(1)}, bf16[8,3584]{1,0:T(8,128)(2,1)S(1)}, u32[]{:S(2)}, u32[]{:S(2)}) collective-permute-start(bf16[8,3584]{1,0:T(8,128)(2,1)S(1)} %slice.66), channel_id=1, source_target_pairs={{0,8},{1,9},{2,3},{3,2},{4,12},{5,13},{6,7},{7,6},{8,0},{9,1},{10,... | collective-permute-start | bytes 172040 | tf_op jit(solution)/shard_map/ppermute | solution.py:127
  49.0 5.2 %collective-permute-start.9 = (bf16[8,3584]{1,0:T(8,128)(2,1)S(1)}, bf16[8,3584]{1,0:T(8,128)(2,1)S(1)}, u32[]{:S(2)}, u32[]{:S(2)}) collective-permute-start(bf16[8,3584]{1,0:T(8,128)(2,1)S(1)} %slice.67), channel_id=1, source_target_pairs={{0,1},{1,0},{2,6},{3,7},{4,5},{5,4},{6,2},{7,3},{8,9},{9,8},{10,14... | collective-permute-start | bytes 172040 | tf_op jit(solution)/shard_map/ppermute | solution.py:127
  51.7 5.1 %collective-permute-start.21 = (bf16[8,3584]{1,0:T(8,128)(2,1)S(1)}, bf16[8,3584]{1,0:T(8,128)(2,1)S(1)}, u32[]{:S(2)}, u32[]{:S(2)}) collective-permute-start(bf16[8,3584]{1,0:T(8,128)(2,1)S(1)} %fusion.7), channel_id=1, source_target_pairs={{0,16},{1,17},{2,18},{3,19},{4,20},{5,21},{6,22},{7,23},{8,24},{9,... | collective-permute-start | bytes 172040 | tf_op jit(solution)/shard_map/ppermute | solution.py:127
  (1 other events, 4.3 us)

commit v4 on v3

--- a/solution.py
+++ b/solution.py
@@ -50,7 +50,7 @@
     extra = -(-experts * TERMS // LANES) * LANES
     return pl.pallas_call(
         lambda *refs: pack_kernel(experts, *refs),
-        out_shape=jax.ShapeDtypeStruct((rows, width + extra), jnp.bfloat16),
+        out_shape=pltpu.VMEM((rows, width + extra), jnp.bfloat16),
         name="pack",
     )(hidden, ids, weights)
 
@@ -97,27 +97,25 @@
     )(me, *(fast(p) for p in pieces), *(fast(w) for w in weights))
 
 
-def load_kernel(gate_hbm, up_hbm, down_hbm, gate_out, up_out, down_out, sems):
-    pairs = ((gate_hbm, gate_out), (up_hbm, up_out), (down_hbm, down_out))
-    copies = [pltpu.make_async_copy(a, b, sems.at[i]) for i, (a, b) in enumerate(pairs)]
-    for copy in copies:
-        copy.start()
-    for copy in copies:
-        copy.wait()
-
-
-def load(*matrices):
-    size = sum(m.size * m.dtype.itemsize for m in matrices)
+def load_kernel(source, target, sem):
+    copy = pltpu.make_async_copy(source, target, sem)
+    copy.start()
+    copy.wait()
+
+
+def load(matrix, after):
+    matrix, _ = lax.optimization_barrier((matrix, after))
+    size = matrix.size * matrix.dtype.itemsize
     return pl.pallas_call(
         load_kernel,
-        out_shape=tuple(pltpu.VMEM(m.shape, m.dtype) for m in matrices),
-        in_specs=[pl.BlockSpec(memory_space=pltpu.HBM)] * len(matrices),
-        out_specs=tuple(pl.BlockSpec(memory_space=pltpu.VMEM) for _ in matrices),
-        scratch_shapes=[pltpu.SemaphoreType.DMA((len(matrices),))],
+        out_shape=pltpu.VMEM(matrix.shape, matrix.dtype),
+        in_specs=[pl.BlockSpec(memory_space=pltpu.HBM)],
+        out_specs=pl.BlockSpec(memory_space=pltpu.VMEM),
+        scratch_shapes=[pltpu.SemaphoreType.DMA],
         compiler_params=pltpu.CompilerParams(vmem_limit_bytes=1024 * 1024),
         cost_estimate=pl.CostEstimate(flops=0, bytes_accessed=2 * size, transcendentals=0),
         name="load",
-    )(*(pltpu.with_memory_space_constraint(m, pltpu.HBM) for m in matrices))
+    )(pltpu.with_memory_space_constraint(matrix, pltpu.HBM))
 
 
 def flip(x, masks):
@@ -146,12 +144,15 @@
     sibling, across = (core, core), (far_bit, far_bit)
 
     packed = pack(hidden, ids, weights, experts)
-    loaded = load(w_gate[0], w_up[0], w_down[0])
-
-    def gather(held, steps):
+
+    def gather(held, steps, beside=None):
         for masks in steps[:-1]:
-            held = jnp.concatenate([held, flip(held, masks)], axis=0)
-        return held, flip(held, steps[-1])
+            sent = flip(held, masks)
+            if beside is not None and masks == steps[-2]:
+                beside = load(beside, held)
+                sent, beside = lax.optimization_barrier((sent, beside))
+            held = jnp.concatenate([held, sent], axis=0)
+        return held, flip(held, steps[-1]), beside
 
     def scatter(low, high, from_low, from_high, steps):
         sent = flip(add(high, flip(from_high, sibling)).astype(jnp.bfloat16), steps[-1])
@@ -163,9 +164,13 @@
         return held
 
     far = flip(packed, across)
+    near_low, near_high, _ = gather(packed, near_steps)
+    far_low, far_high, gate = gather(far, far_steps, w_gate[0])
+    up, down = load(w_up[0], far_low), load(w_down[0], far_low)
+    far_high, up, down = lax.optimization_barrier((far_high, up, down))
+    loaded = (gate, up, down)
     results = []
-    for held, steps in ((packed, near_steps), (far, far_steps)):
-        low, high = gather(held, steps)
+    for low, high, steps in ((near_low, near_high, near_steps), (far_low, far_high, far_steps)):
         pieces = (low, high, flip(low, sibling), flip(high, sibling))
         results.append(scatter(*expert_values(pieces, loaded, experts), steps))
     near, far = results

time: 57.6 us -> 53.7 us (0.932)
  waiting for transfers between devices: 22.9 us -> 10.8 us
  starting transfers between devices: 19.8 us -> 26.6 us
  Pallas kernels: 9.38 us -> 10.7 us
    ppermute x22, waiting for transfers between devices: 22.9 us -> 10.8 us  [flip(): lax.ppermute(x, axes, [(i, i ^ masks[bool(i & core)]) for i in range(coun...]
    ppermute x22, starting transfers between devices: 19.8 us -> 26.6 us  [flip(): lax.ppermute(x, axes, [(i, i ^ masks[bool(i & core)]) for i in range(coun...]
    pallas_call x2 -> x4, Pallas kernels: 5.94 us -> 7.24 us  [the longest x3 6.24 us: load(): pl.pallas_call(load_kernel, out_shape=pltpu.VMEM(matrix.shape, matrix.dty...]
  transfers between devices with their start and end apart: 22 -> 22, of which waited for: 9 -> 8; matrix products, arithmetic and copies ran while one was open for 7% -> 7% of each run, Pallas kernels for 13% -> 18%
where the time goes in v4:
time: 53.7 us; the launch traced here: 53.4 us
  starting transfers between devices  26.6 us (50%)
  waiting for transfers between devices  10.8 us (20%)
  Pallas kernels  10.7 us (20%)
  other arithmetic  1.99 us (4%)
  matrix products  1.37 us (3%)
  local copies, waits for them, and re-layouts  1.2 us (2%)
  between operations  0.85 us (2%)
    ppermute x22, starting transfers between devices, flip(): lax.ppermute(x, axes, [(i, i ^ masks[bool(i & core)]) for i in range(coun...  26.6 us
    ppermute x22, waiting for transfers between devices, flip(): lax.ppermute(x, axes, [(i, i ^ masks[bool(i & core)]) for i in range(coun...  10.8 us
    pallas_call x3, Pallas kernels, load(): pl.pallas_call(load_kernel, out_shape=pltpu.VMEM(matrix.shape, matrix.dty...  6.24 us
    pallas_call x2, Pallas kernels, expert_values(): pl.pallas_call(lambda *refs: expert_kernel(experts, len(pieces), 512, *re...  3.48 us
    unnamed x7, local copies, waits for them, and re-layouts  1.14 us
  transfers between devices with their start and end apart: 22, of which 8 were waited for; matrix products, arithmetic and copies ran while one was open for 7% of the time, Pallas kernels for 18%

profile of v4, /device:TPU:0, one launch (start us, length us, event | category | flops | bytes accessed | tf_op | source)
XLA Modules:
  0.0 53.4 jit_solution(11596040069178661579)
XLA Ops:
  0.6 1.0 %pack.1 = bf16[8,3712]{1,0:T(8,128)(2,1)S(1)} custom-call(bf16[8,3584]{1,0:T(8,128)(2,1)} %refs_0_.1, s32[8,8]{1,0:T(8,128)} %refs_1_.1, f32[8,8]{1,0:T(8,128)} %refs_2_.1), custom_call_target="tpu_custom_call" | custom-call | tf_op jit(solution)/shard_map/pack/pallas_call | solution.py:51
  1.7 4.1 %collective-permute-start.5 = (bf16[8,3712]{1,0:T(8,128)(2,1)S(1)}, bf16[8,3712]{1,0:T(8,128)(2,1)S(1)}, u32[]{:S(2)}, u32[]{:S(2)}) collective-permute-start(bf16[8,3712]{1,0:T(8,128)(2,1)S(1)} %pack.1), channel_id=1, source_target_pairs={{0,16},{1,17},{2,18},{3,19},{4,20},{5,21},{6,22},{7,23},{8,24},{9,... | collective-permute-start | bytes 178184 | tf_op jit(solution)/shard_map/ppermute | solution.py:125
  5.8 1.5 %collective-permute-start = (bf16[8,3712]{1,0:T(8,128)(2,1)S(1)}, bf16[8,3712]{1,0:T(8,128)(2,1)S(1)}, u32[]{:S(2)}, u32[]{:S(2)}) collective-permute-start(bf16[8,3712]{1,0:T(8,128)(2,1)S(1)} %pack.1), channel_id=1, source_target_pairs={{0,1},{1,0},{2,6},{3,7},{4,5},{5,4},{6,2},{7,3},{8,9},{9,8},{10,14... | collective-permute-start | bytes 178184 | tf_op jit(solution)/shard_map/ppermute | solution.py:125
  8.6 1.3 %collective-permute-start.6 = (bf16[8,3712]{1,0:T(8,128)(2,1)S(1)}, bf16[8,3712]{1,0:T(8,128)(2,1)S(1)}, u32[]{:S(2)}, u32[]{:S(2)}) collective-permute-start(bf16[8,3712]{1,0:T(8,128)(2,1)S(1)} %collective-permute-done.5), channel_id=1, source_target_pairs={{0,8},{1,9},{2,3},{3,2},{4,12},{5,13},{6,7},{7,6},{8,0},{9,1},{10,... | collective-permute-start | bytes 178184 | tf_op jit(solution)/shard_map/ppermute | solution.py:125
  9.9 2.9 %collective-permute-done.6 = bf16[8,3712]{1,0:T(8,128)(2,1)S(1)} collective-permute-done((bf16[8,3712]{1,0:T(8,128)(2,1)S(1)}, bf16[8,3712]{1,0:T(8,128)(2,1)S(1)}, u32[]{:S(2)}, u32[]{:S(2)}) %collective-permute-start.6) | collective-permute-done | bytes 59424 | tf_op jit(solution)/shard_map/ppermute | solution.py:125
  12.8 2.4 %collective-permute-start.7 = (bf16[16,3712]{1,0:T(8,128)(2,1)S(1)}, bf16[16,3712]{1,0:T(8,128)(2,1)S(1)}, u32[]{:S(2)}, u32[]{:S(2)}) collective-permute-start(bf16[16,3712]{1,0:T(8,128)(2,1)S(1)} %get-tuple-element.35), channel_id=1, source_target_pairs={{0,1},{1,0},{2,6},{3,7},{4,5},{5,4},{6,2},{7,3},{8,9},{9,8},{10,14... | collective-permute-start | bytes 356360 | tf_op jit(solution)/shard_map/ppermute | solution.py:125
  15.2 1.9 %collective-permute-start.1 = (bf16[16,3712]{1,0:T(8,128)(2,1)S(1)}, bf16[16,3712]{1,0:T(8,128)(2,1)S(1)}, u32[]{:S(2)}, u32[]{:S(2)}) collective-permute-start(bf16[16,3712]{1,0:T(8,128)(2,1)S(1)} %pad_maximum_fusion.1), channel_id=1, source_target_pairs={{0,4},{1,5},{2,10},{3,11},{4,0},{5,1},{6,14},{7,15},{8,12},{9,13},... | collective-permute-start | bytes 356360 | tf_op jit(solution)/shard_map/ppermute | solution.py:125
  17.1 2.0 %load.3.refs_5_ = bf16[3584,512]{1,0:T(8,128)(2,1)S(1)} custom-call(bf16[3584,512]{1,0:T(8,128)(2,1)} %bitcast.11), custom_call_target="tpu_custom_call" | custom-call | bytes 7340032 | tf_op jit(solution)/shard_map/load/pallas_call | solution.py:109
  19.2 1.9 %collective-permute-start.8 = (bf16[32,3712]{1,0:T(8,128)(2,1)S(1)}, bf16[32,3712]{1,0:T(8,128)(2,1)S(1)}, u32[]{:S(2)}, u32[]{:S(2)}) collective-permute-start(bf16[32,3712]{1,0:T(8,128)(2,1)S(1)} %constant_dynamic-update-slice_fusion.2.refs_1_), channel_id=1, source_target_pairs={{0,4},{1,5},{2,10},{3,11},{4,0},{5,1},{6,14},{7,15},{8,12},{9,13},... | collective-permute-start | bytes 712712 | tf_op jit(solution)/shard_map/ppermute | solution.py:125
  21.2 2.0 %load.4.refs_6_ = bf16[3584,512]{1,0:T(8,128)(2,1)S(1)} custom-call(bf16[3584,512]{1,0:T(8,128)(2,1)} %bitcast.12), custom_call_target="tpu_custom_call" | custom-call | bytes 7340032 | tf_op jit(solution)/shard_map/load/pallas_call | solution.py:109
  23.3 2.1 %load.5.refs_7_ = bf16[512,3584]{1,0:T(8,128)(2,1)S(1)} custom-call(bf16[512,3584]{1,0:T(8,128)(2,1)} %bitcast.13), custom_call_target="tpu_custom_call" | custom-call | bytes 7340032 | tf_op jit(solution)/shard_map/load/pallas_call | solution.py:109
  27.3 1.7 %expert.3 = (bf16[32,3584]{1,0:T(8,128)(2,1)S(1)}, bf16[32,3584]{1,0:T(8,128)(2,1)S(1)}, bf16[32,3584]{1,0:T(8,128)(2,1)S(1)}, bf16[32,3584]{1,0:T(8,128)(2,1)S(1)}) custom-call(s32[1]{0:T(128)} %bitcast.refs_0_, bf16[32,3712]{1,0:T(8,128)(2,1)S(1)} %constant_dynamic-update-slice_fusion.2.refs_1_, bf16[32,3712]{1,0:T(8,128)(2,1)S(1)} %collective-permute-done.8.refs_2_, ...), custom_call_target="tpu_custom_call" | custom-call | flops 1409286144 | bytes 12910592 | tf_op jit(solution)/shard_map/expert/pallas_call | solution.py:85
  29.8 1.7 %expert.2 = (bf16[32,3584]{1,0:T(8,128)(2,1)S(1)}, bf16[32,3584]{1,0:T(8,128)(2,1)S(1)}, bf16[32,3584]{1,0:T(8,128)(2,1)S(1)}, bf16[32,3584]{1,0:T(8,128)(2,1)S(1)}) custom-call(s32[1]{0:T(128)} %bitcast.refs_0_, bf16[32,3712]{1,0:T(8,128)(2,1)S(1)} %pad_maximum_fusion.refs_1_, bf16[32,3712]{1,0:T(8,128)(2,1)S(1)} %collective-permute-done.2.refs_2_, ...), custom_call_target="tpu_custom_call" | custom-call | flops 1409286144 | bytes 12910592 | tf_op jit(solution)/shard_map/expert/pallas_call | solution.py:85
  32.3 1.4 %collective-permute-start.18 = (bf16[32,3584]{1,0:T(8,128)(2,1)S(1)}, bf16[32,3584]{1,0:T(8,128)(2,1)S(1)}, u32[]{:S(2)}, u32[]{:S(2)}) collective-permute-start(bf16[32,3584]{1,0:T(8,128)(2,1)S(1)} %add_convert_fusion), channel_id=1, source_target_pairs={{0,4},{1,5},{2,10},{3,11},{4,0},{5,1},{6,14},{7,15},{8,12},{9,13},... | collective-permute-start | bytes 688136 | tf_op jit(solution)/shard_map/ppermute | solution.py:125
  33.8 1.4 %collective-permute-start.11 = (bf16[32,3584]{1,0:T(8,128)(2,1)S(1)}, bf16[32,3584]{1,0:T(8,128)(2,1)S(1)}, u32[]{:S(2)}, u32[]{:S(2)}) collective-permute-start(bf16[32,3584]{1,0:T(8,128)(2,1)S(1)} %add_convert_fusion.1), channel_id=1, source_target_pairs={{0,8},{1,9},{2,3},{3,2},{4,12},{5,13},{6,7},{7,6},{8,0},{9,1},{10,... | collective-permute-start | bytes 688136 | tf_op jit(solution)/shard_map/ppermute | solution.py:125
  35.1 3.2 %collective-permute-done.18 = bf16[32,3584]{1,0:T(8,128)(2,1)S(1)} collective-permute-done((bf16[32,3584]{1,0:T(8,128)(2,1)S(1)}, bf16[32,3584]{1,0:T(8,128)(2,1)S(1)}, u32[]{:S(2)}, u32[]{:S(2)}) %collective-permute-start.18) | collective-permute-done | bytes 229408 | tf_op jit(solution)/shard_map/ppermute | solution.py:125
  38.5 1.6 %collective-permute-start.19 = (bf16[16,3584]{1,0:T(8,128)(2,1)S(1)}, bf16[16,3584]{1,0:T(8,128)(2,1)S(1)}, u32[]{:S(2)}, u32[]{:S(2)}) collective-permute-start(bf16[16,3584]{1,0:T(8,128)(2,1)S(1)} %slice.64), channel_id=1, source_target_pairs={{0,1},{1,0},{2,6},{3,7},{4,5},{5,4},{6,2},{7,3},{8,9},{9,8},{10,14... | collective-permute-start | bytes 344072 | tf_op jit(solution)/shard_map/ppermute | solution.py:125
  40.4 1.1 %collective-permute-start.12 = (bf16[16,3584]{1,0:T(8,128)(2,1)S(1)}, bf16[16,3584]{1,0:T(8,128)(2,1)S(1)}, u32[]{:S(2)}, u32[]{:S(2)}) collective-permute-start(bf16[16,3584]{1,0:T(8,128)(2,1)S(1)} %slice.65), channel_id=1, source_target_pairs={{0,4},{1,5},{2,10},{3,11},{4,0},{5,1},{6,14},{7,15},{8,12},{9,13},... | collective-permute-start | bytes 344072 | tf_op jit(solution)/shard_map/ppermute | solution.py:125
  41.6 1.8 %collective-permute-done.19 = bf16[16,3584]{1,0:T(8,128)(2,1)S(1)} collective-permute-done((bf16[16,3584]{1,0:T(8,128)(2,1)S(1)}, bf16[16,3584]{1,0:T(8,128)(2,1)S(1)}, u32[]{:S(2)}, u32[]{:S(2)}) %collective-permute-start.19) | collective-permute-done | bytes 114720 | tf_op jit(solution)/shard_map/ppermute | solution.py:125
  43.4 1.8 %collective-permute-start.20 = (bf16[8,3584]{1,0:T(8,128)(2,1)S(1)}, bf16[8,3584]{1,0:T(8,128)(2,1)S(1)}, u32[]{:S(2)}, u32[]{:S(2)}) collective-permute-start(bf16[8,3584]{1,0:T(8,128)(2,1)S(1)} %slice.66), channel_id=1, source_target_pairs={{0,8},{1,9},{2,3},{3,2},{4,12},{5,13},{6,7},{7,6},{8,0},{9,1},{10,... | collective-permute-start | bytes 172040 | tf_op jit(solution)/shard_map/ppermute | solution.py:125
  45.3 1.6 %collective-permute-start.13 = (bf16[8,3584]{1,0:T(8,128)(2,1)S(1)}, bf16[8,3584]{1,0:T(8,128)(2,1)S(1)}, u32[]{:S(2)}, u32[]{:S(2)}) collective-permute-start(bf16[8,3584]{1,0:T(8,128)(2,1)S(1)} %slice.67), channel_id=1, source_target_pairs={{0,1},{1,0},{2,6},{3,7},{4,5},{5,4},{6,2},{7,3},{8,9},{9,8},{10,14... | collective-permute-start | bytes 172040 | tf_op jit(solution)/shard_map/ppermute | solution.py:125
  47.7 2.6 %collective-permute-start.21 = (bf16[8,3584]{1,0:T(8,128)(2,1)S(1)}, bf16[8,3584]{1,0:T(8,128)(2,1)S(1)}, u32[]{:S(2)}, u32[]{:S(2)}) collective-permute-start(bf16[8,3584]{1,0:T(8,128)(2,1)S(1)} %fusion.7), channel_id=1, source_target_pairs={{0,16},{1,17},{2,18},{3,19},{4,20},{5,21},{6,22},{7,23},{8,24},{9,... | collective-permute-start | bytes 172040 | tf_op jit(solution)/shard_map/ppermute | solution.py:125
  50.2 1.0 %fusion.1 = bf16[1,8,64,512]{3,2,1,0:T(8,128)(2,1)S(1)} fusion(bf16[8,128,576]{1,2,0:T(8,128)(2,1)S(1)} %copy-done.1, f32[8,64]{1,0:T(8,128)S(1)} %fusion.11, f32[8,64,128]{2,1,0:T(8,128)S(1)} %fusion.4), kind=kOutput, calls=%fused_computation.2 | convolution fusion | flops 67568256 | bytes 2101248 | tf_op jit(solution)/shard_map/bht,btc->bhc/dot_general | solution.py:25
  51.2 1.1 %copy.13 = bf16[1,8,64,512]{3,1,2,0:T(8,128)(2,1)} copy(bf16[1,8,64,512]{3,2,1,0:T(8,128)(2,1)S(1)} %fusion.1) | data formatting | bytes 1048576
  (52 shorter events, 7.4 us)
Async XLA Ops:
  0.6 25.4 %copy-start = (bf16[8,64,576]{2,1,0:T(8,128)(2,1)S(1)}, bf16[8,64,576]{2,1,0:T(8,128)(2,1)}, u32[]{:S(2)}) copy-start(bf16[8,64,576]{2,1,0:T(8,128)(2,1)} %param.10) | copy-start | bytes 1769476
  1.7 6.9 %collective-permute-start.5 = (bf16[8,3712]{1,0:T(8,128)(2,1)S(1)}, bf16[8,3712]{1,0:T(8,128)(2,1)S(1)}, u32[]{:S(2)}, u32[]{:S(2)}) collective-permute-start(bf16[8,3712]{1,0:T(8,128)(2,1)S(1)} %pack.1), channel_id=1, source_target_pairs={{0,16},{1,17},{2,18},{3,19},{4,20},{5,21},{6,22},{7,23},{8,24},{9,... | collective-permute-start | bytes 178184 | tf_op jit(solution)/shard_map/ppermute | solution.py:125
  5.8 9.4 %collective-permute-start = (bf16[8,3712]{1,0:T(8,128)(2,1)S(1)}, bf16[8,3712]{1,0:T(8,128)(2,1)S(1)}, u32[]{:S(2)}, u32[]{:S(2)}) collective-permute-start(bf16[8,3712]{1,0:T(8,128)(2,1)S(1)} %pack.1), channel_id=1, source_target_pairs={{0,1},{1,0},{2,6},{3,7},{4,5},{5,4},{6,2},{7,3},{8,9},{9,8},{10,14... | collective-permute-start | bytes 178184 | tf_op jit(solution)/shard_map/ppermute | solution.py:125
  8.6 4.2 %collective-permute-start.6 = (bf16[8,3712]{1,0:T(8,128)(2,1)S(1)}, bf16[8,3712]{1,0:T(8,128)(2,1)S(1)}, u32[]{:S(2)}, u32[]{:S(2)}) collective-permute-start(bf16[8,3712]{1,0:T(8,128)(2,1)S(1)} %collective-permute-done.5), channel_id=1, source_target_pairs={{0,8},{1,9},{2,3},{3,2},{4,12},{5,13},{6,7},{7,6},{8,0},{9,1},{10,... | collective-permute-start | bytes 178184 | tf_op jit(solution)/shard_map/ppermute | solution.py:125
  12.8 6.4 %collective-permute-start.7 = (bf16[16,3712]{1,0:T(8,128)(2,1)S(1)}, bf16[16,3712]{1,0:T(8,128)(2,1)S(1)}, u32[]{:S(2)}, u32[]{:S(2)}) collective-permute-start(bf16[16,3712]{1,0:T(8,128)(2,1)S(1)} %get-tuple-element.35), channel_id=1, source_target_pairs={{0,1},{1,0},{2,6},{3,7},{4,5},{5,4},{6,2},{7,3},{8,9},{9,8},{10,14... | collective-permute-start | bytes 356360 | tf_op jit(solution)/shard_map/ppermute | solution.py:125
  15.2 5.9 %collective-permute-start.1 = (bf16[16,3712]{1,0:T(8,128)(2,1)S(1)}, bf16[16,3712]{1,0:T(8,128)(2,1)S(1)}, u32[]{:S(2)}, u32[]{:S(2)}) collective-permute-start(bf16[16,3712]{1,0:T(8,128)(2,1)S(1)} %pad_maximum_fusion.1), channel_id=1, source_target_pairs={{0,4},{1,5},{2,10},{3,11},{4,0},{5,1},{6,14},{7,15},{8,12},{9,13},... | collective-permute-start | bytes 356360 | tf_op jit(solution)/shard_map/ppermute | solution.py:125
  19.2 6.3 %collective-permute-start.8 = (bf16[32,3712]{1,0:T(8,128)(2,1)S(1)}, bf16[32,3712]{1,0:T(8,128)(2,1)S(1)}, u32[]{:S(2)}, u32[]{:S(2)}) collective-permute-start(bf16[32,3712]{1,0:T(8,128)(2,1)S(1)} %constant_dynamic-update-slice_fusion.2.refs_1_), channel_id=1, source_target_pairs={{0,4},{1,5},{2,10},{3,11},{4,0},{5,1},{6,14},{7,15},{8,12},{9,13},... | collective-permute-start | bytes 712712 | tf_op jit(solution)/shard_map/ppermute | solution.py:125
  21.1 6.2 %collective-permute-start.2 = (bf16[32,3712]{1,0:T(8,128)(2,1)S(1)}, bf16[32,3712]{1,0:T(8,128)(2,1)S(1)}, u32[]{:S(2)}, u32[]{:S(2)}) collective-permute-start(bf16[32,3712]{1,0:T(8,128)(2,1)S(1)} %pad_maximum_fusion.refs_1_), channel_id=1, source_target_pairs={{0,8},{1,9},{2,3},{3,2},{4,12},{5,13},{6,7},{7,6},{8,0},{9,1},{10,... | collective-permute-start | bytes 712712 | tf_op jit(solution)/shard_map/ppermute | solution.py:125
  21.2 6.1 %collective-permute-start.14 = (bf16[32,3712]{1,0:T(8,128)(2,1)S(1)}, bf16[32,3712]{1,0:T(8,128)(2,1)S(1)}, u32[]{:S(2)}, u32[]{:S(2)}) collective-permute-start(bf16[32,3712]{1,0:T(8,128)(2,1)S(1)} %constant_dynamic-update-slice_fusion.2.refs_1_), channel_id=1, source_target_pairs={{0,2},{1,3},{2,0},{3,1},{4,6},{5,7},{6,4},{7,5},{8,10},{9,11},{10,... | collective-permute-start | bytes 712712 | tf_op jit(solution)/shard_map/ppermute | solution.py:125
  23.3 2.7 %copy-start.1 = (bf16[8,128,576]{1,2,0:T(8,128)(2,1)S(1)}, bf16[8,128,576]{1,2,0:T(8,128)(2,1)}, u32[]{:S(2)}) copy-start(bf16[8,128,576]{1,2,0:T(8,128)(2,1)} %param.11) | copy-start | bytes 3538948
  25.5 1.8 %collective-permute-start.15 = (bf16[32,3712]{1,0:T(8,128)(2,1)S(1)}, bf16[32,3712]{1,0:T(8,128)(2,1)S(1)}, u32[]{:S(2)}, u32[]{:S(2)}) collective-permute-start(bf16[32,3712]{1,0:T(8,128)(2,1)S(1)} %collective-permute-done.8.refs_2_), channel_id=1, source_target_pairs={{0,2},{1,3},{2,0},{3,1},{4,6},{5,7},{6,4},{7,5},{8,10},{9,11},{10,... | collective-permute-start | bytes 712712 | tf_op jit(solution)/shard_map/ppermute | solution.py:125
  26.4 3.4 %collective-permute-start.3 = (bf16[32,3712]{1,0:T(8,128)(2,1)S(1)}, bf16[32,3712]{1,0:T(8,128)(2,1)S(1)}, u32[]{:S(2)}, u32[]{:S(2)}) collective-permute-start(bf16[32,3712]{1,0:T(8,128)(2,1)S(1)} %pad_maximum_fusion.refs_1_), channel_id=1, source_target_pairs={{0,2},{1,3},{2,0},{3,1},{4,6},{5,7},{6,4},{7,5},{8,10},{9,11},{10,... | collective-permute-start | bytes 712712 | tf_op jit(solution)/shard_map/ppermute | solution.py:125
  27.3 2.6 %collective-permute-start.4 = (bf16[32,3712]{1,0:T(8,128)(2,1)S(1)}, bf16[32,3712]{1,0:T(8,128)(2,1)S(1)}, u32[]{:S(2)}, u32[]{:S(2)}) collective-permute-start(bf16[32,3712]{1,0:T(8,128)(2,1)S(1)} %collective-permute-done.2.refs_2_), channel_id=1, source_target_pairs={{0,2},{1,3},{2,0},{3,1},{4,6},{5,7},{6,4},{7,5},{8,10},{9,11},{10,... | collective-permute-start | bytes 712712 | tf_op jit(solution)/shard_map/ppermute | solution.py:125
  29.0 3.2 %collective-permute-start.17 = (bf16[32,3584]{1,0:T(8,128)(2,1)S(1)}, bf16[32,3584]{1,0:T(8,128)(2,1)S(1)}, u32[]{:S(2)}, u32[]{:S(2)}) collective-permute-start(bf16[32,3584]{1,0:T(8,128)(2,1)S(1)} %get-tuple-element.33), channel_id=1, source_target_pairs={{0,2},{1,3},{2,0},{3,1},{4,6},{5,7},{6,4},{7,5},{8,10},{9,11},{10,... | collective-permute-start | bytes 688136 | tf_op jit(solution)/shard_map/ppermute | solution.py:125
  31.6 2.1 %collective-permute-start.10 = (bf16[32,3584]{1,0:T(8,128)(2,1)S(1)}, bf16[32,3584]{1,0:T(8,128)(2,1)S(1)}, u32[]{:S(2)}, u32[]{:S(2)}) collective-permute-start(bf16[32,3584]{1,0:T(8,128)(2,1)S(1)} %get-tuple-element.28), channel_id=1, source_target_pairs={{0,2},{1,3},{2,0},{3,1},{4,6},{5,7},{6,4},{7,5},{8,10},{9,11},{10,... | collective-permute-start | bytes 688136 | tf_op jit(solution)/shard_map/ppermute | solution.py:125
  31.7 8.4 %collective-permute-start.9 = (bf16[32,3584]{1,0:T(8,128)(2,1)S(1)}, bf16[32,3584]{1,0:T(8,128)(2,1)S(1)}, u32[]{:S(2)}, u32[]{:S(2)}) collective-permute-start(bf16[32,3584]{1,0:T(8,128)(2,1)S(1)} %get-tuple-element.26), channel_id=1, source_target_pairs={{0,2},{1,3},{2,0},{3,1},{4,6},{5,7},{6,4},{7,5},{8,10},{9,11},{10,... | collective-permute-start | bytes 688136 | tf_op jit(solution)/shard_map/ppermute | solution.py:125
  32.2 3.0 %collective-permute-start.16 = (bf16[32,3584]{1,0:T(8,128)(2,1)S(1)}, bf16[32,3584]{1,0:T(8,128)(2,1)S(1)}, u32[]{:S(2)}, u32[]{:S(2)}) collective-permute-start(bf16[32,3584]{1,0:T(8,128)(2,1)S(1)} %get-tuple-element.31), channel_id=1, source_target_pairs={{0,2},{1,3},{2,0},{3,1},{4,6},{5,7},{6,4},{7,5},{8,10},{9,11},{10,... | collective-permute-start | bytes 688136 | tf_op jit(solution)/shard_map/ppermute | solution.py:125
  32.3 6.1 %collective-permute-start.18 = (bf16[32,3584]{1,0:T(8,128)(2,1)S(1)}, bf16[32,3584]{1,0:T(8,128)(2,1)S(1)}, u32[]{:S(2)}, u32[]{:S(2)}) collective-permute-start(bf16[32,3584]{1,0:T(8,128)(2,1)S(1)} %add_convert_fusion), channel_id=1, source_target_pairs={{0,4},{1,5},{2,10},{3,11},{4,0},{5,1},{6,14},{7,15},{8,12},{9,13},... | collective-permute-start | bytes 688136 | tf_op jit(solution)/shard_map/ppermute | solution.py:125
  33.8 6.5 %collective-permute-start.11 = (bf16[32,3584]{1,0:T(8,128)(2,1)S(1)}, bf16[32,3584]{1,0:T(8,128)(2,1)S(1)}, u32[]{:S(2)}, u32[]{:S(2)}) collective-permute-start(bf16[32,3584]{1,0:T(8,128)(2,1)S(1)} %add_convert_fusion.1), channel_id=1, source_target_pairs={{0,8},{1,9},{2,3},{3,2},{4,12},{5,13},{6,7},{7,6},{8,0},{9,1},{10,... | collective-permute-start | bytes 688136 | tf_op jit(solution)/shard_map/ppermute | solution.py:125
  38.5 4.9 %collective-permute-start.19 = (bf16[16,3584]{1,0:T(8,128)(2,1)S(1)}, bf16[16,3584]{1,0:T(8,128)(2,1)S(1)}, u32[]{:S(2)}, u32[]{:S(2)}) collective-permute-start(bf16[16,3584]{1,0:T(8,128)(2,1)S(1)} %slice.64), channel_id=1, source_target_pairs={{0,1},{1,0},{2,6},{3,7},{4,5},{5,4},{6,2},{7,3},{8,9},{9,8},{10,14... | collective-permute-start | bytes 344072 | tf_op jit(solution)/shard_map/ppermute | solution.py:125
  40.4 4.9 %collective-permute-start.12 = (bf16[16,3584]{1,0:T(8,128)(2,1)S(1)}, bf16[16,3584]{1,0:T(8,128)(2,1)S(1)}, u32[]{:S(2)}, u32[]{:S(2)}) collective-permute-start(bf16[16,3584]{1,0:T(8,128)(2,1)S(1)} %slice.65), channel_id=1, source_target_pairs={{0,4},{1,5},{2,10},{3,11},{4,0},{5,1},{6,14},{7,15},{8,12},{9,13},... | collective-permute-start | bytes 344072 | tf_op jit(solution)/shard_map/ppermute | solution.py:125
  43.4 4.2 %collective-permute-start.20 = (bf16[8,3584]{1,0:T(8,128)(2,1)S(1)}, bf16[8,3584]{1,0:T(8,128)(2,1)S(1)}, u32[]{:S(2)}, u32[]{:S(2)}) collective-permute-start(bf16[8,3584]{1,0:T(8,128)(2,1)S(1)} %slice.66), channel_id=1, source_target_pairs={{0,8},{1,9},{2,3},{3,2},{4,12},{5,13},{6,7},{7,6},{8,0},{9,1},{10,... | collective-permute-start | bytes 172040 | tf_op jit(solution)/shard_map/ppermute | solution.py:125
  45.3 7.0 %collective-permute-start.13 = (bf16[8,3584]{1,0:T(8,128)(2,1)S(1)}, bf16[8,3584]{1,0:T(8,128)(2,1)S(1)}, u32[]{:S(2)}, u32[]{:S(2)}) collective-permute-start(bf16[8,3584]{1,0:T(8,128)(2,1)S(1)} %slice.67), channel_id=1, source_target_pairs={{0,1},{1,0},{2,6},{3,7},{4,5},{5,4},{6,2},{7,3},{8,9},{9,8},{10,14... | collective-permute-start | bytes 172040 | tf_op jit(solution)/shard_map/ppermute | solution.py:125
  47.7 5.1 %collective-permute-start.21 = (bf16[8,3584]{1,0:T(8,128)(2,1)S(1)}, bf16[8,3584]{1,0:T(8,128)(2,1)S(1)}, u32[]{:S(2)}, u32[]{:S(2)}) collective-permute-start(bf16[8,3584]{1,0:T(8,128)(2,1)S(1)} %fusion.7), channel_id=1, source_target_pairs={{0,16},{1,17},{2,18},{3,19},{4,20},{5,21},{6,22},{7,23},{8,24},{9,... | collective-permute-start | bytes 172040 | tf_op jit(solution)/shard_map/ppermute | solution.py:125

commit v5 on v3

--- a/solution.py
+++ b/solution.py
@@ -50,14 +50,19 @@
     extra = -(-experts * TERMS // LANES) * LANES
     return pl.pallas_call(
         lambda *refs: pack_kernel(experts, *refs),
-        out_shape=jax.ShapeDtypeStruct((rows, width + extra), jnp.bfloat16),
+        out_shape=pltpu.VMEM((rows, width + extra), jnp.bfloat16),
         name="pack",
     )(hidden, ids, weights)
 
 
-def expert_kernel(experts, pieces, chunk, me_ref, *refs):
-    ins, (gate_w, up_w, down_w), outs = refs[:pieces], refs[pieces : pieces + 3], refs[pieces + 3 :]
+def expert_kernel(experts, pieces, fetch, chunk, me_ref, *refs):
+    ins, (gate_w, up_w, down_in), outs = refs[:pieces], refs[pieces : pieces + 3], refs[pieces + 3 :]
     step, width = outs[0].shape
+    down_w = down_in
+    if fetch:
+        down_w, sem = outs[pieces:]
+        copy = pltpu.make_async_copy(down_in, down_w, sem)
+        copy.start()
     info = jnp.concatenate([ref[:, width:] for ref in ins], axis=0).astype(jnp.float32)
     lane = lax.broadcasted_iota(jnp.int32, info.shape, 1)
     me = me_ref[0]
@@ -67,6 +72,8 @@
     gate = jnp.dot(rows, gate_w[...], preferred_element_type=jnp.float32)
     up = jnp.dot(rows, up_w[...], preferred_element_type=jnp.float32)
     act = (gate / (1.0 + jnp.exp(-gate)) * up).astype(jnp.bfloat16)
+    if fetch:
+        copy.wait()
     for k in range(width // chunk):
         part = slice(k * chunk, (k + 1) * chunk)
         value = jnp.dot(act, down_w[:, part], preferred_element_type=jnp.float32)
@@ -75,18 +82,26 @@
             outs[p][:, part] = value[p * step : (p + 1) * step]
 
 
-def expert_values(pieces, weights, experts):
+def expert_values(pieces, weights, experts, fetch):
     step, packed = pieces[0].shape
     width, units = weights[0].shape
     rows = step * len(pieces)
     me = lax.axis_index("nodes").astype(jnp.int32).reshape(1)
     vmem = pl.BlockSpec(memory_space=pltpu.VMEM)
     fast = lambda w: pltpu.with_memory_space_constraint(w, pltpu.VMEM)
-    return pl.pallas_call(
-        lambda *refs: expert_kernel(experts, len(pieces), 512, *refs),
-        out_shape=tuple(pltpu.VMEM((step, width), jnp.bfloat16) for _ in pieces),
-        in_specs=[pl.BlockSpec(memory_space=pltpu.SMEM)] + [vmem] * (len(pieces) + 3),
-        out_specs=tuple(vmem for _ in pieces),
+    down = weights[2]
+    outs = [pltpu.VMEM((step, width), jnp.bfloat16) for _ in pieces]
+    if fetch:
+        outs.append(pltpu.VMEM(down.shape, down.dtype))
+        down, place = pltpu.with_memory_space_constraint(down, pltpu.HBM), pl.BlockSpec(memory_space=pltpu.HBM)
+    else:
+        down, place = fast(down), vmem
+    results = pl.pallas_call(
+        lambda *refs: expert_kernel(experts, len(pieces), fetch, 512, *refs),
+        out_shape=tuple(outs),
+        in_specs=[pl.BlockSpec(memory_space=pltpu.SMEM)] + [vmem] * (len(pieces) + 2) + [place],
+        out_specs=tuple(vmem for _ in outs),
+        scratch_shapes=[pltpu.SemaphoreType.DMA] if fetch else [],
         compiler_params=pltpu.CompilerParams(vmem_limit_bytes=12 * 1024 * 1024),
         cost_estimate=pl.CostEstimate(
             flops=2 * rows * width * units * 3,
@@ -94,12 +109,13 @@
             transcendentals=rows * units,
         ),
         name="expert",
-    )(me, *(fast(p) for p in pieces), *(fast(w) for w in weights))
-
-
-def load_kernel(gate_hbm, up_hbm, down_hbm, gate_out, up_out, down_out, sems):
-    pairs = ((gate_hbm, gate_out), (up_hbm, up_out), (down_hbm, down_out))
-    copies = [pltpu.make_async_copy(a, b, sems.at[i]) for i, (a, b) in enumerate(pairs)]
+    )(me, *(fast(p) for p in pieces), fast(weights[0]), fast(weights[1]), down)
+    return results[: len(pieces)], results[-1]
+
+
+def load_kernel(*refs):
+    count = len(refs) // 2
+    copies = [pltpu.make_async_copy(refs[i], refs[count + i], refs[-1].at[i]) for i in range(count)]
     for copy in copies:
         copy.start()
     for copy in copies:
@@ -140,13 +156,12 @@
     experts = w_gate.shape[0] * nodes
     far_bit = core * nodes // 2
     cube = [1 << k for k in range((core * nodes).bit_length() - 1) if (1 << k) not in (core, far_bit)]
-    turn = lambda k: cube[k:] + cube[:k]
-    near_steps = list(zip(turn(0), turn(1)))
-    far_steps = list(zip(turn(2), turn(0)))
+    shared, rest = cube[1], cube[:1] + cube[2:]
+    near_steps = list(zip(rest + [shared], rest[1:] + rest[:1] + [shared]))
+    far_steps = list(zip(cube, cube[1:] + cube[:1]))
     sibling, across = (core, core), (far_bit, far_bit)
 
     packed = pack(hidden, ids, weights, experts)
-    loaded = load(w_gate[0], w_up[0], w_down[0])
 
     def gather(held, steps):
         for masks in steps[:-1]:
@@ -163,12 +178,19 @@
         return held
 
     far = flip(packed, across)
-    results = []
-    for held, steps in ((packed, near_steps), (far, far_steps)):
-        low, high = gather(held, steps)
-        pieces = (low, high, flip(low, sibling), flip(high, sibling))
-        results.append(scatter(*expert_values(pieces, loaded, experts), steps))
-    near, far = results
+    far_low, far_high = gather(far, far_steps)
+    near_low, near_high = gather(packed, near_steps)
+    w_gate, w_up, w_down, _ = lax.optimization_barrier((w_gate[0], w_up[0], w_down[0], far_low))
+    gate, up = load(w_gate, w_up)
+    far_high, gate, up = lax.optimization_barrier((far_high, gate, up))
+
+    pieces = (far_low, far_high, flip(far_low, sibling), flip(far_high, sibling))
+    values, down = expert_values(pieces, (gate, up, w_down), experts, True)
+    near_high, _ = lax.optimization_barrier((near_high, values[1]))
+    far = scatter(*values, far_steps)
+    pieces = (near_low, near_high, flip(near_low, sibling), flip(near_high, sibling))
+    values, _ = expert_values(pieces, (gate, up, down), experts, False)
+    near = scatter(*values, near_steps)
     return add(near, flip(far.astype(jnp.bfloat16), across)).astype(jnp.bfloat16)
 
 

time: 57.6 us -> 60.3 us (1.047)
  starting transfers between devices: 19.8 us -> 24.7 us
  waiting for transfers between devices: 22.9 us -> 21.3 us
  Pallas kernels: 9.38 us -> 8.71 us
    ppermute x22, starting transfers between devices: 19.8 us -> 24.7 us  [flip(): lax.ppermute(x, axes, [(i, i ^ masks[bool(i & core)]) for i in range(coun...]
    ppermute x22, waiting for transfers between devices: 22.9 us -> 21.3 us  [flip(): lax.ppermute(x, axes, [(i, i ^ masks[bool(i & core)]) for i in range(coun...]
    pallas_call x1, Pallas kernels: 4.31 us -> 3.17 us  [load(): pl.pallas_call(load_kernel, out_shape=tuple((pltpu.VMEM(m.shape, m.dtype)...]
  transfers between devices with their start and end apart: 22 -> 22, of which waited for: 9 -> 11; matrix products, arithmetic and copies ran while one was open for 7% -> 7% of each run, Pallas kernels for 13% -> 13%
where the time goes in v5:
time: 60.3 us; the launch traced here: 60.1 us
  starting transfers between devices  24.7 us (41%)
  waiting for transfers between devices  21.3 us (35%)
  Pallas kernels  8.71 us (14%)
  other arithmetic  2 us (3%)
  matrix products  1.38 us (2%)
  local copies, waits for them, and re-layouts  1.19 us (2%)
  between operations  0.82 us (1%)
    ppermute x22, starting transfers between devices, flip(): lax.ppermute(x, axes, [(i, i ^ masks[bool(i & core)]) for i in range(coun...  24.7 us
    ppermute x22, waiting for transfers between devices, flip(): lax.ppermute(x, axes, [(i, i ^ masks[bool(i & core)]) for i in range(coun...  21.3 us
    pallas_call x2, Pallas kernels, expert_values(): pl.pallas_call(lambda *refs: expert_kernel(experts, len(pieces), fetch, 5...  4.53 us
    pallas_call x1, Pallas kernels, load(): pl.pallas_call(load_kernel, out_shape=tuple((pltpu.VMEM(m.shape, m.dtype)...  3.17 us
  transfers between devices with their start and end apart: 22, of which 11 were waited for; matrix products, arithmetic and copies ran while one was open for 7% of the time, Pallas kernels for 13%

profile of v5, /device:TPU:0, one launch (start us, length us, event | category | flops | bytes accessed | tf_op | source)
XLA Modules:
  0.0 60.1 jit_solution(9879344642927554477)
XLA Ops:
  1.7 4.1 %collective-permute-start.3 = (bf16[8,3712]{1,0:T(8,128)(2,1)S(1)}, bf16[8,3712]{1,0:T(8,128)(2,1)S(1)}, u32[]{:S(2)}, u32[]{:S(2)}) collective-permute-start(bf16[8,3712]{1,0:T(8,128)(2,1)S(1)} %pack.1), channel_id=1, source_target_pairs={{0,16},{1,17},{2,18},{3,19},{4,20},{5,21},{6,22},{7,23},{8,24},{9,... | collective-permute-start | bytes 178184 | tf_op jit(solution)/shard_map/ppermute | solution.py:143
  5.8 1.5 %collective-permute-start = (bf16[8,3712]{1,0:T(8,128)(2,1)S(1)}, bf16[8,3712]{1,0:T(8,128)(2,1)S(1)}, u32[]{:S(2)}, u32[]{:S(2)}) collective-permute-start(bf16[8,3712]{1,0:T(8,128)(2,1)S(1)} %pack.1), channel_id=1, source_target_pairs={{0,1},{1,0},{2,10},{3,11},{4,5},{5,4},{6,14},{7,15},{8,9},{9,8},{1... | collective-permute-start | bytes 178184 | tf_op jit(solution)/shard_map/ppermute | solution.py:143
  7.2 1.4 %collective-permute-done.3 = bf16[8,3712]{1,0:T(8,128)(2,1)S(1)} collective-permute-done((bf16[8,3712]{1,0:T(8,128)(2,1)S(1)}, bf16[8,3712]{1,0:T(8,128)(2,1)S(1)}, u32[]{:S(2)}, u32[]{:S(2)}) %collective-permute-start.3) | collective-permute-done | bytes 59424 | tf_op jit(solution)/shard_map/ppermute | solution.py:143
  8.7 1.7 %collective-permute-start.4 = (bf16[8,3712]{1,0:T(8,128)(2,1)S(1)}, bf16[8,3712]{1,0:T(8,128)(2,1)S(1)}, u32[]{:S(2)}, u32[]{:S(2)}) collective-permute-start(bf16[8,3712]{1,0:T(8,128)(2,1)S(1)} %collective-permute-done.3), channel_id=1, source_target_pairs={{0,1},{1,0},{2,6},{3,7},{4,5},{5,4},{6,2},{7,3},{8,9},{9,8},{10,14... | collective-permute-start | bytes 178184 | tf_op jit(solution)/shard_map/ppermute | solution.py:143
  10.4 2.5 %collective-permute-done.4 = bf16[8,3712]{1,0:T(8,128)(2,1)S(1)} collective-permute-done((bf16[8,3712]{1,0:T(8,128)(2,1)S(1)}, bf16[8,3712]{1,0:T(8,128)(2,1)S(1)}, u32[]{:S(2)}, u32[]{:S(2)}) %collective-permute-start.4) | collective-permute-done | bytes 59424 | tf_op jit(solution)/shard_map/ppermute | solution.py:143
  12.9 1.8 %collective-permute-start.5 = (bf16[16,3712]{1,0:T(8,128)(2,1)S(1)}, bf16[16,3712]{1,0:T(8,128)(2,1)S(1)}, u32[]{:S(2)}, u32[]{:S(2)}) collective-permute-start(bf16[16,3712]{1,0:T(8,128)(2,1)S(1)} %pad_maximum_fusion.2), channel_id=1, source_target_pairs={{0,4},{1,5},{2,10},{3,11},{4,0},{5,1},{6,14},{7,15},{8,12},{9,13},... | collective-permute-start | bytes 356360 | tf_op jit(solution)/shard_map/ppermute | solution.py:143
  14.7 3.1 %collective-permute-done.5 = bf16[16,3712]{1,0:T(8,128)(2,1)S(1)} collective-permute-done((bf16[16,3712]{1,0:T(8,128)(2,1)S(1)}, bf16[16,3712]{1,0:T(8,128)(2,1)S(1)}, u32[]{:S(2)}, u32[]{:S(2)}) %collective-permute-start.5) | collective-permute-done | bytes 118816 | tf_op jit(solution)/shard_map/ppermute | solution.py:143
  17.8 1.4 %collective-permute-start.6 = (bf16[32,3712]{1,0:T(8,128)(2,1)S(1)}, bf16[32,3712]{1,0:T(8,128)(2,1)S(1)}, u32[]{:S(2)}, u32[]{:S(2)}) collective-permute-start(bf16[32,3712]{1,0:T(8,128)(2,1)S(1)} %constant_dynamic-update-slice_fusion.refs_1_), channel_id=1, source_target_pairs={{0,8},{1,9},{2,3},{3,2},{4,12},{5,13},{6,7},{7,6},{8,0},{9,1},{10,... | collective-permute-start | bytes 712712 | tf_op jit(solution)/shard_map/ppermute | solution.py:143
  20.7 3.2 %load.1 = (bf16[3584,512]{1,0:T(8,128)(2,1)S(1)}, bf16[3584,512]{1,0:T(8,128)(2,1)S(1)}) custom-call(bf16[3584,512]{1,0:T(8,128)(2,1)} %bitcast.11, bf16[3584,512]{1,0:T(8,128)(2,1)} %bitcast.12), custom_call_target="tpu_custom_call" | custom-call | bytes 14680064 | tf_op jit(solution)/shard_map/load/pallas_call | solution.py:127
  25.3 1.8 %collective-permute-start.2 = (bf16[32,3712]{1,0:T(8,128)(2,1)S(1)}, bf16[32,3712]{1,0:T(8,128)(2,1)S(1)}, u32[]{:S(2)}, u32[]{:S(2)}) collective-permute-start(bf16[32,3712]{1,0:T(8,128)(2,1)S(1)} %pad_maximum_fusion.refs_1_), channel_id=1, source_target_pairs={{0,4},{1,5},{2,6},{3,7},{4,0},{5,1},{6,2},{7,3},{8,12},{9,13},{10,... | collective-permute-start | bytes 712712 | tf_op jit(solution)/shard_map/ppermute | solution.py:143
  27.1 2.8 %expert.2 = (bf16[32,3584]{1,0:T(8,128)(2,1)S(1)}, bf16[32,3584]{1,0:T(8,128)(2,1)S(1)}, bf16[32,3584]{1,0:T(8,128)(2,1)S(1)}, bf16[32,3584]{1,0:T(8,128)(2,1)S(1)}, bf16[512,3584]{1,0:T(8,128)(2,1)S(1)}) custom-call(s32[1]{0:T(128)} %bitcast.refs_0_, bf16[32,3712]{1,0:T(8,128)(2,1)S(1)} %constant_dynamic-update-slice_fusion.refs_1_, ...), custom_call_target="tpu_custom_call" | custom-call | flops 1409286144 | bytes 12910592 | tf_op jit(solution)/shard_map/expert/pallas_call | solution.py:99
  31.0 1.3 %collective-permute-done.2.refs_2_ = bf16[32,3712]{1,0:T(8,128)(2,1)S(1)} collective-permute-done((bf16[32,3712]{1,0:T(8,128)(2,1)S(1)}, bf16[32,3712]{1,0:T(8,128)(2,1)S(1)}, u32[]{:S(2)}, u32[]{:S(2)}) %collective-permute-start.2) | collective-permute-done | bytes 237600 | tf_op jit(solution)/shard_map/ppermute | solution.py:143
  32.3 1.4 %collective-permute-start.18 = (bf16[32,3584]{1,0:T(8,128)(2,1)S(1)}, bf16[32,3584]{1,0:T(8,128)(2,1)S(1)}, u32[]{:S(2)}, u32[]{:S(2)}) collective-permute-start(bf16[32,3584]{1,0:T(8,128)(2,1)S(1)} %add_convert_fusion), channel_id=1, source_target_pairs={{0,8},{1,9},{2,3},{3,2},{4,12},{5,13},{6,7},{7,6},{8,0},{9,1},{10,... | collective-permute-start | bytes 688136 | tf_op jit(solution)/shard_map/ppermute | solution.py:143
  34.0 1.7 %expert.3 = (bf16[32,3584]{1,0:T(8,128)(2,1)S(1)}, bf16[32,3584]{1,0:T(8,128)(2,1)S(1)}, bf16[32,3584]{1,0:T(8,128)(2,1)S(1)}, bf16[32,3584]{1,0:T(8,128)(2,1)S(1)}) custom-call(s32[1]{0:T(128)} %bitcast.refs_0_, bf16[32,3712]{1,0:T(8,128)(2,1)S(1)} %pad_maximum_fusion.refs_1_, bf16[32,3712]{1,0:T(8,128)(2,1)S(1)} %collective-permute-done.2.refs_2_, ...), custom_call_target="tpu_custom_call" | custom-call | flops 1409286144 | bytes 12910592 | tf_op jit(solution)/shard_map/expert/pallas_call | solution.py:99
  36.5 1.9 %collective-permute-done.18 = bf16[32,3584]{1,0:T(8,128)(2,1)S(1)} collective-permute-done((bf16[32,3584]{1,0:T(8,128)(2,1)S(1)}, bf16[32,3584]{1,0:T(8,128)(2,1)S(1)}, u32[]{:S(2)}, u32[]{:S(2)}) %collective-permute-start.18) | collective-permute-done | bytes 229408 | tf_op jit(solution)/shard_map/ppermute | solution.py:143
  38.5 1.8 %collective-permute-start.19 = (bf16[16,3584]{1,0:T(8,128)(2,1)S(1)}, bf16[16,3584]{1,0:T(8,128)(2,1)S(1)}, u32[]{:S(2)}, u32[]{:S(2)}) collective-permute-start(bf16[16,3584]{1,0:T(8,128)(2,1)S(1)} %slice.64), channel_id=1, source_target_pairs={{0,4},{1,5},{2,10},{3,11},{4,0},{5,1},{6,14},{7,15},{8,12},{9,13},... | collective-permute-start | bytes 344072 | tf_op jit(solution)/shard_map/ppermute | solution.py:143
  40.8 3.9 %collective-permute-done.19 = bf16[16,3584]{1,0:T(8,128)(2,1)S(1)} collective-permute-done((bf16[16,3584]{1,0:T(8,128)(2,1)S(1)}, bf16[16,3584]{1,0:T(8,128)(2,1)S(1)}, u32[]{:S(2)}, u32[]{:S(2)}) %collective-permute-start.19) | collective-permute-done | bytes 114720 | tf_op jit(solution)/shard_map/ppermute | solution.py:143
  44.7 1.7 %collective-permute-start.20 = (bf16[8,3584]{1,0:T(8,128)(2,1)S(1)}, bf16[8,3584]{1,0:T(8,128)(2,1)S(1)}, u32[]{:S(2)}, u32[]{:S(2)}) collective-permute-start(bf16[8,3584]{1,0:T(8,128)(2,1)S(1)} %slice.66), channel_id=1, source_target_pairs={{0,1},{1,0},{2,6},{3,7},{4,5},{5,4},{6,2},{7,3},{8,9},{9,8},{10,14... | collective-permute-start | bytes 172040 | tf_op jit(solution)/shard_map/ppermute | solution.py:143
  46.4 2.4 %collective-permute-done.13 = bf16[32,3584]{1,0:T(8,128)(2,1)S(1)} collective-permute-done((bf16[32,3584]{1,0:T(8,128)(2,1)S(1)}, bf16[32,3584]{1,0:T(8,128)(2,1)S(1)}, u32[]{:S(2)}, u32[]{:S(2)}) %collective-permute-start.13) | collective-permute-done | bytes 229408 | tf_op jit(solution)/shard_map/ppermute | solution.py:143
  49.7 2.7 %collective-permute-start.21 = (bf16[8,3584]{1,0:T(8,128)(2,1)S(1)}, bf16[8,3584]{1,0:T(8,128)(2,1)S(1)}, u32[]{:S(2)}, u32[]{:S(2)}) collective-permute-start(bf16[8,3584]{1,0:T(8,128)(2,1)S(1)} %fusion.7), channel_id=1, source_target_pairs={{0,16},{1,17},{2,18},{3,19},{4,20},{5,21},{6,22},{7,23},{8,24},{9,... | collective-permute-start | bytes 172040 | tf_op jit(solution)/shard_map/ppermute | solution.py:143
  52.4 2.8 %collective-permute-done.14 = bf16[16,3584]{1,0:T(8,128)(2,1)S(1)} collective-permute-done((bf16[16,3584]{1,0:T(8,128)(2,1)S(1)}, bf16[16,3584]{1,0:T(8,128)(2,1)S(1)}, u32[]{:S(2)}, u32[]{:S(2)}) %collective-permute-start.14) | collective-permute-done | bytes 114720 | tf_op jit(solution)/shard_map/ppermute | solution.py:143
  56.2 1.0 %fusion.1 = bf16[1,8,64,512]{3,2,1,0:T(8,128)(2,1)S(1)} fusion(bf16[8,128,576]{1,2,0:T(8,128)(2,1)S(1)} %copy-done.1, f32[8,64]{1,0:T(8,128)S(1)} %fusion.11, f32[8,64,128]{2,1,0:T(8,128)S(1)} %fusion.4), kind=kOutput, calls=%fused_computation.2 | convolution fusion | flops 67568256 | bytes 2101248 | tf_op jit(solution)/shard_map/bht,btc->bhc/dot_general | solution.py:25
  57.2 1.1 %copy.13 = bf16[1,8,64,512]{3,1,2,0:T(8,128)(2,1)} copy(bf16[1,8,64,512]{3,2,1,0:T(8,128)(2,1)S(1)} %fusion.1) | data formatting | bytes 1048576
  58.3 1.2 %collective-permute-done.15 = bf16[8,3584]{1,0:T(8,128)(2,1)S(1)} collective-permute-done((bf16[8,3584]{1,0:T(8,128)(2,1)S(1)}, bf16[8,3584]{1,0:T(8,128)(2,1)S(1)}, u32[]{:S(2)}, u32[]{:S(2)}) %collective-permute-start.15) | collective-permute-done | bytes 57376 | tf_op jit(solution)/shard_map/ppermute | solution.py:143
  (51 shorter events, 9.2 us)
Async XLA Ops:
  0.6 29.4 %copy-start = (bf16[8,64,576]{2,1,0:T(8,128)(2,1)S(1)}, bf16[8,64,576]{2,1,0:T(8,128)(2,1)}, u32[]{:S(2)}) copy-start(bf16[8,64,576]{2,1,0:T(8,128)(2,1)} %param.10) | copy-start | bytes 1769476
  1.7 7.0 %collective-permute-start.3 = (bf16[8,3712]{1,0:T(8,128)(2,1)S(1)}, bf16[8,3712]{1,0:T(8,128)(2,1)S(1)}, u32[]{:S(2)}, u32[]{:S(2)}) collective-permute-start(bf16[8,3712]{1,0:T(8,128)(2,1)S(1)} %pack.1), channel_id=1, source_target_pairs={{0,16},{1,17},{2,18},{3,19},{4,20},{5,21},{6,22},{7,23},{8,24},{9,... | collective-permute-start | bytes 178184 | tf_op jit(solution)/shard_map/ppermute | solution.py:143
  5.8 13.4 %collective-permute-start = (bf16[8,3712]{1,0:T(8,128)(2,1)S(1)}, bf16[8,3712]{1,0:T(8,128)(2,1)S(1)}, u32[]{:S(2)}, u32[]{:S(2)}) collective-permute-start(bf16[8,3712]{1,0:T(8,128)(2,1)S(1)} %pack.1), channel_id=1, source_target_pairs={{0,1},{1,0},{2,10},{3,11},{4,5},{5,4},{6,14},{7,15},{8,9},{9,8},{1... | collective-permute-start | bytes 178184 | tf_op jit(solution)/shard_map/ppermute | solution.py:143
  8.7 4.2 %collective-permute-start.4 = (bf16[8,3712]{1,0:T(8,128)(2,1)S(1)}, bf16[8,3712]{1,0:T(8,128)(2,1)S(1)}, u32[]{:S(2)}, u32[]{:S(2)}) collective-permute-start(bf16[8,3712]{1,0:T(8,128)(2,1)S(1)} %collective-permute-done.3), channel_id=1, source_target_pairs={{0,1},{1,0},{2,6},{3,7},{4,5},{5,4},{6,2},{7,3},{8,9},{9,8},{10,14... | collective-permute-start | bytes 178184 | tf_op jit(solution)/shard_map/ppermute | solution.py:143
  12.9 4.9 %collective-permute-start.5 = (bf16[16,3712]{1,0:T(8,128)(2,1)S(1)}, bf16[16,3712]{1,0:T(8,128)(2,1)S(1)}, u32[]{:S(2)}, u32[]{:S(2)}) collective-permute-start(bf16[16,3712]{1,0:T(8,128)(2,1)S(1)} %pad_maximum_fusion.2), channel_id=1, source_target_pairs={{0,4},{1,5},{2,10},{3,11},{4,0},{5,1},{6,14},{7,15},{8,12},{9,13},... | collective-permute-start | bytes 356360 | tf_op jit(solution)/shard_map/ppermute | solution.py:143
  17.8 6.2 %collective-permute-start.6 = (bf16[32,3712]{1,0:T(8,128)(2,1)S(1)}, bf16[32,3712]{1,0:T(8,128)(2,1)S(1)}, u32[]{:S(2)}, u32[]{:S(2)}) collective-permute-start(bf16[32,3712]{1,0:T(8,128)(2,1)S(1)} %constant_dynamic-update-slice_fusion.refs_1_), channel_id=1, source_target_pairs={{0,8},{1,9},{2,3},{3,2},{4,12},{5,13},{6,7},{7,6},{8,0},{9,1},{10,... | collective-permute-start | bytes 712712 | tf_op jit(solution)/shard_map/ppermute | solution.py:143
  19.2 6.1 %collective-permute-start.1 = (bf16[16,3712]{1,0:T(8,128)(2,1)S(1)}, bf16[16,3712]{1,0:T(8,128)(2,1)S(1)}, u32[]{:S(2)}, u32[]{:S(2)}) collective-permute-start(bf16[16,3712]{1,0:T(8,128)(2,1)S(1)} %pad_maximum_fusion.1), channel_id=1, source_target_pairs={{0,8},{1,9},{2,3},{3,2},{4,12},{5,13},{6,7},{7,6},{8,0},{9,1},{10,... | collective-permute-start | bytes 356360 | tf_op jit(solution)/shard_map/ppermute | solution.py:143
  20.7 6.4 %collective-permute-start.7 = (bf16[32,3712]{1,0:T(8,128)(2,1)S(1)}, bf16[32,3712]{1,0:T(8,128)(2,1)S(1)}, u32[]{:S(2)}, u32[]{:S(2)}) collective-permute-start(bf16[32,3712]{1,0:T(8,128)(2,1)S(1)} %constant_dynamic-update-slice_fusion.refs_1_), channel_id=1, source_target_pairs={{0,2},{1,3},{2,0},{3,1},{4,6},{5,7},{6,4},{7,5},{8,10},{9,11},{10,... | collective-permute-start | bytes 712712 | tf_op jit(solution)/shard_map/ppermute | solution.py:143
  24.0 3.1 %collective-permute-start.8 = (bf16[32,3712]{1,0:T(8,128)(2,1)S(1)}, bf16[32,3712]{1,0:T(8,128)(2,1)S(1)}, u32[]{:S(2)}, u32[]{:S(2)}) collective-permute-start(bf16[32,3712]{1,0:T(8,128)(2,1)S(1)} %collective-permute-done.6.refs_2_), channel_id=1, source_target_pairs={{0,2},{1,3},{2,0},{3,1},{4,6},{5,7},{6,4},{7,5},{8,10},{9,11},{10,... | collective-permute-start | bytes 712712 | tf_op jit(solution)/shard_map/ppermute | solution.py:143
  25.3 7.0 %collective-permute-start.2 = (bf16[32,3712]{1,0:T(8,128)(2,1)S(1)}, bf16[32,3712]{1,0:T(8,128)(2,1)S(1)}, u32[]{:S(2)}, u32[]{:S(2)}) collective-permute-start(bf16[32,3712]{1,0:T(8,128)(2,1)S(1)} %pad_maximum_fusion.refs_1_), channel_id=1, source_target_pairs={{0,4},{1,5},{2,6},{3,7},{4,0},{5,1},{6,2},{7,3},{8,12},{9,13},{10,... | collective-permute-start | bytes 712712 | tf_op jit(solution)/shard_map/ppermute | solution.py:143
  27.1 2.9 %copy-start.1 = (bf16[8,128,576]{1,2,0:T(8,128)(2,1)S(1)}, bf16[8,128,576]{1,2,0:T(8,128)(2,1)}, u32[]{:S(2)}) copy-start(bf16[8,128,576]{1,2,0:T(8,128)(2,1)} %param.11) | copy-start | bytes 3538948
  29.9 2.4 %collective-permute-start.17 = (bf16[32,3584]{1,0:T(8,128)(2,1)S(1)}, bf16[32,3584]{1,0:T(8,128)(2,1)S(1)}, u32[]{:S(2)}, u32[]{:S(2)}) collective-permute-start(bf16[32,3584]{1,0:T(8,128)(2,1)S(1)} %get-tuple-element.37), channel_id=1, source_target_pairs={{0,2},{1,3},{2,0},{3,1},{4,6},{5,7},{6,4},{7,5},{8,10},{9,11},{10,... | collective-permute-start | bytes 688136 | tf_op jit(solution)/shard_map/ppermute | solution.py:143
  30.4 3.6 %collective-permute-start.9 = (bf16[32,3712]{1,0:T(8,128)(2,1)S(1)}, bf16[32,3712]{1,0:T(8,128)(2,1)S(1)}, u32[]{:S(2)}, u32[]{:S(2)}) collective-permute-start(bf16[32,3712]{1,0:T(8,128)(2,1)S(1)} %pad_maximum_fusion.refs_1_), channel_id=1, source_target_pairs={{0,2},{1,3},{2,0},{3,1},{4,6},{5,7},{6,4},{7,5},{8,10},{9,11},{10,... | collective-permute-start | bytes 712712 | tf_op jit(solution)/shard_map/ppermute | solution.py:143
  30.9 5.6 %collective-permute-start.16 = (bf16[32,3584]{1,0:T(8,128)(2,1)S(1)}, bf16[32,3584]{1,0:T(8,128)(2,1)S(1)}, u32[]{:S(2)}, u32[]{:S(2)}) collective-permute-start(bf16[32,3584]{1,0:T(8,128)(2,1)S(1)} %get-tuple-element.36), channel_id=1, source_target_pairs={{0,2},{1,3},{2,0},{3,1},{4,6},{5,7},{6,4},{7,5},{8,10},{9,11},{10,... | collective-permute-start | bytes 688136 | tf_op jit(solution)/shard_map/ppermute | solution.py:143
  32.3 1.7 %collective-permute-start.10 = (bf16[32,3712]{1,0:T(8,128)(2,1)S(1)}, bf16[32,3712]{1,0:T(8,128)(2,1)S(1)}, u32[]{:S(2)}, u32[]{:S(2)}) collective-permute-start(bf16[32,3712]{1,0:T(8,128)(2,1)S(1)} %collective-permute-done.2.refs_2_), channel_id=1, source_target_pairs={{0,2},{1,3},{2,0},{3,1},{4,6},{5,7},{6,4},{7,5},{8,10},{9,11},{10,... | collective-permute-start | bytes 712712 | tf_op jit(solution)/shard_map/ppermute | solution.py:143
  32.3 6.1 %collective-permute-start.18 = (bf16[32,3584]{1,0:T(8,128)(2,1)S(1)}, bf16[32,3584]{1,0:T(8,128)(2,1)S(1)}, u32[]{:S(2)}, u32[]{:S(2)}) collective-permute-start(bf16[32,3584]{1,0:T(8,128)(2,1)S(1)} %add_convert_fusion), channel_id=1, source_target_pairs={{0,8},{1,9},{2,3},{3,2},{4,12},{5,13},{6,7},{7,6},{8,0},{9,1},{10,... | collective-permute-start | bytes 688136 | tf_op jit(solution)/shard_map/ppermute | solution.py:143
  35.7 4.7 %collective-permute-start.12 = (bf16[32,3584]{1,0:T(8,128)(2,1)S(1)}, bf16[32,3584]{1,0:T(8,128)(2,1)S(1)}, u32[]{:S(2)}, u32[]{:S(2)}) collective-permute-start(bf16[32,3584]{1,0:T(8,128)(2,1)S(1)} %get-tuple-element.34), channel_id=1, source_target_pairs={{0,2},{1,3},{2,0},{3,1},{4,6},{5,7},{6,4},{7,5},{8,10},{9,11},{10,... | collective-permute-start | bytes 688136 | tf_op jit(solution)/shard_map/ppermute | solution.py:143
  36.4 10.0 %collective-permute-start.11 = (bf16[32,3584]{1,0:T(8,128)(2,1)S(1)}, bf16[32,3584]{1,0:T(8,128)(2,1)S(1)}, u32[]{:S(2)}, u32[]{:S(2)}) collective-permute-start(bf16[32,3584]{1,0:T(8,128)(2,1)S(1)} %get-tuple-element.32), channel_id=1, source_target_pairs={{0,2},{1,3},{2,0},{3,1},{4,6},{5,7},{6,4},{7,5},{8,10},{9,11},{10,... | collective-permute-start | bytes 688136 | tf_op jit(solution)/shard_map/ppermute | solution.py:143
  38.5 6.1 %collective-permute-start.19 = (bf16[16,3584]{1,0:T(8,128)(2,1)S(1)}, bf16[16,3584]{1,0:T(8,128)(2,1)S(1)}, u32[]{:S(2)}, u32[]{:S(2)}) collective-permute-start(bf16[16,3584]{1,0:T(8,128)(2,1)S(1)} %slice.64), channel_id=1, source_target_pairs={{0,4},{1,5},{2,10},{3,11},{4,0},{5,1},{6,14},{7,15},{8,12},{9,13},... | collective-permute-start | bytes 344072 | tf_op jit(solution)/shard_map/ppermute | solution.py:143
  40.4 8.3 %collective-permute-start.13 = (bf16[32,3584]{1,0:T(8,128)(2,1)S(1)}, bf16[32,3584]{1,0:T(8,128)(2,1)S(1)}, u32[]{:S(2)}, u32[]{:S(2)}) collective-permute-start(bf16[32,3584]{1,0:T(8,128)(2,1)S(1)} %add_convert_fusion.1), channel_id=1, source_target_pairs={{0,4},{1,5},{2,6},{3,7},{4,0},{5,1},{6,2},{7,3},{8,12},{9,13},{10,... | collective-permute-start | bytes 688136 | tf_op jit(solution)/shard_map/ppermute | solution.py:143
  44.7 5.0 %collective-permute-start.20 = (bf16[8,3584]{1,0:T(8,128)(2,1)S(1)}, bf16[8,3584]{1,0:T(8,128)(2,1)S(1)}, u32[]{:S(2)}, u32[]{:S(2)}) collective-permute-start(bf16[8,3584]{1,0:T(8,128)(2,1)S(1)} %slice.66), channel_id=1, source_target_pairs={{0,1},{1,0},{2,6},{3,7},{4,5},{5,4},{6,2},{7,3},{8,9},{9,8},{10,14... | collective-permute-start | bytes 172040 | tf_op jit(solution)/shard_map/ppermute | solution.py:143
  48.9 6.3 %collective-permute-start.14 = (bf16[16,3584]{1,0:T(8,128)(2,1)S(1)}, bf16[16,3584]{1,0:T(8,128)(2,1)S(1)}, u32[]{:S(2)}, u32[]{:S(2)}) collective-permute-start(bf16[16,3584]{1,0:T(8,128)(2,1)S(1)} %slice.65), channel_id=1, source_target_pairs={{0,8},{1,9},{2,3},{3,2},{4,12},{5,13},{6,7},{7,6},{8,0},{9,1},{10,... | collective-permute-start | bytes 344072 | tf_op jit(solution)/shard_map/ppermute | solution.py:143
  49.7 8.6 %collective-permute-start.21 = (bf16[8,3584]{1,0:T(8,128)(2,1)S(1)}, bf16[8,3584]{1,0:T(8,128)(2,1)S(1)}, u32[]{:S(2)}, u32[]{:S(2)}) collective-permute-start(bf16[8,3584]{1,0:T(8,128)(2,1)S(1)} %fusion.7), channel_id=1, source_target_pairs={{0,16},{1,17},{2,18},{3,19},{4,20},{5,21},{6,22},{7,23},{8,24},{9,... | collective-permute-start | bytes 172040 | tf_op jit(solution)/shard_map/ppermute | solution.py:143
  55.2 4.2 %collective-permute-start.15 = (bf16[8,3584]{1,0:T(8,128)(2,1)S(1)}, bf16[8,3584]{1,0:T(8,128)(2,1)S(1)}, u32[]{:S(2)}, u32[]{:S(2)}) collective-permute-start(bf16[8,3584]{1,0:T(8,128)(2,1)S(1)} %slice.67), channel_id=1, source_target_pairs={{0,1},{1,0},{2,10},{3,11},{4,5},{5,4},{6,14},{7,15},{8,9},{9,8},{1... | collective-permute-start | bytes 172040 | tf_op jit(solution)/shard_map/ppermute | solution.py:143

commit v6 on v4

--- a/solution.py
+++ b/solution.py
@@ -75,11 +75,10 @@
             outs[p][:, part] = value[p * step : (p + 1) * step]
 
 
-def expert_values(pieces, weights, experts):
+def expert_values(me, pieces, weights, experts):
     step, packed = pieces[0].shape
     width, units = weights[0].shape
     rows = step * len(pieces)
-    me = lax.axis_index("nodes").astype(jnp.int32).reshape(1)
     vmem = pl.BlockSpec(memory_space=pltpu.VMEM)
     fast = lambda w: pltpu.with_memory_space_constraint(w, pltpu.VMEM)
     return pl.pallas_call(
@@ -97,25 +96,34 @@
     )(me, *(fast(p) for p in pieces), *(fast(w) for w in weights))
 
 
-def load_kernel(source, target, sem):
-    copy = pltpu.make_async_copy(source, target, sem)
-    copy.start()
-    copy.wait()
-
-
-def load(matrix, after):
-    matrix, _ = lax.optimization_barrier((matrix, after))
-    size = matrix.size * matrix.dtype.itemsize
+def load_kernel(cuts, *refs):
+    count = len(refs) // 2
+    copies = []
+    for i in range(count):
+        rows = refs[i].shape[0] // cuts
+        for k in range(cuts):
+            part = pl.ds(k * rows, rows)
+            copies.append(pltpu.make_async_copy(refs[i].at[part], refs[count + i].at[part], refs[-1].at[i, k]))
+    for copy in copies:
+        copy.start()
+    for copy in copies:
+        copy.wait()
+
+
+def load(matrices, after):
+    *matrices, _ = lax.optimization_barrier((*matrices, after))
+    size = sum(m.size * m.dtype.itemsize for m in matrices)
+    cuts = 1
     return pl.pallas_call(
-        load_kernel,
-        out_shape=pltpu.VMEM(matrix.shape, matrix.dtype),
-        in_specs=[pl.BlockSpec(memory_space=pltpu.HBM)],
-        out_specs=pl.BlockSpec(memory_space=pltpu.VMEM),
-        scratch_shapes=[pltpu.SemaphoreType.DMA],
+        lambda *refs: load_kernel(cuts, *refs),
+        out_shape=tuple(pltpu.VMEM(m.shape, m.dtype) for m in matrices),
+        in_specs=[pl.BlockSpec(memory_space=pltpu.HBM)] * len(matrices),
+        out_specs=tuple(pl.BlockSpec(memory_space=pltpu.VMEM) for _ in matrices),
+        scratch_shapes=[pltpu.SemaphoreType.DMA((len(matrices), cuts))],
         compiler_params=pltpu.CompilerParams(vmem_limit_bytes=1024 * 1024),
         cost_estimate=pl.CostEstimate(flops=0, bytes_accessed=2 * size, transcendentals=0),
         name="load",
-    )(pltpu.with_memory_space_constraint(matrix, pltpu.HBM))
+    )(*(pltpu.with_memory_space_constraint(m, pltpu.HBM) for m in matrices))
 
 
 def flip(x, masks):
@@ -139,17 +147,19 @@
     far_bit = core * nodes // 2
     cube = [1 << k for k in range((core * nodes).bit_length() - 1) if (1 << k) not in (core, far_bit)]
     turn = lambda k: cube[k:] + cube[:k]
-    near_steps = list(zip(turn(0), turn(1)))
-    far_steps = list(zip(turn(2), turn(0)))
+    near_steps = list(zip(turn(1), turn(2)))
+    far_steps = list(zip(turn(0), turn(1)))
     sibling, across = (core, core), (far_bit, far_bit)
 
+    me = lax.axis_index("nodes").astype(jnp.int32).reshape(1)
+    hidden, me = lax.optimization_barrier((hidden, me))
     packed = pack(hidden, ids, weights, experts)
 
     def gather(held, steps, beside=None):
         for masks in steps[:-1]:
             sent = flip(held, masks)
             if beside is not None and masks == steps[-2]:
-                beside = load(beside, held)
+                (beside,) = load((beside,), held)
                 sent, beside = lax.optimization_barrier((sent, beside))
             held = jnp.concatenate([held, sent], axis=0)
         return held, flip(held, steps[-1]), beside
@@ -166,13 +176,13 @@
     far = flip(packed, across)
     near_low, near_high, _ = gather(packed, near_steps)
     far_low, far_high, gate = gather(far, far_steps, w_gate[0])
-    up, down = load(w_up[0], far_low), load(w_down[0], far_low)
+    up, down = load((w_up[0], w_down[0]), far_low)
     far_high, up, down = lax.optimization_barrier((far_high, up, down))
     loaded = (gate, up, down)
     results = []
     for low, high, steps in ((near_low, near_high, near_steps), (far_low, far_high, far_steps)):
         pieces = (low, high, flip(low, sibling), flip(high, sibling))
-        results.append(scatter(*expert_values(pieces, loaded, experts), steps))
+        results.append(scatter(*expert_values(me, pieces, loaded, experts), steps))
     near, far = results
     return add(near, flip(far.astype(jnp.bfloat16), across)).astype(jnp.bfloat16)
 

time: 53.7 us -> 52.5 us (0.978)
  Pallas kernels: 10.7 us -> 9.77 us
  starting transfers between devices: 26.6 us -> 25.8 us
    pallas_call x3 -> x2, Pallas kernels: 6.24 us -> 5.3 us  [load(): pl.pallas_call(lambda *refs: load_kernel(cuts, *refs), out_shape=tuple((p...]
    ppermute x22, starting transfers between devices: 26.6 us -> 25.8 us  [flip(): lax.ppermute(x, axes, [(i, i ^ masks[bool(i & core)]) for i in range(coun...]
    ppermute x22, waiting for transfers between devices: 10.8 us -> 11.3 us  [flip(): lax.ppermute(x, axes, [(i, i ^ masks[bool(i & core)]) for i in range(coun...]
  transfers between devices with their start and end apart: 22 -> 22, of which waited for: 8 -> 11; matrix products, arithmetic and copies ran while one was open for 7% -> 7% of each run, Pallas kernels for 18% -> 17%
where the time goes in v6:
time: 52.5 us; the launch traced here: 52.3 us
  starting transfers between devices  25.8 us (49%)
  waiting for transfers between devices  11.3 us (22%)
  Pallas kernels  9.77 us (19%)
  other arithmetic  1.98 us (4%)
  matrix products  1.37 us (3%)
  local copies, waits for them, and re-layouts  1.2 us (2%)
  between operations  0.82 us (2%)
    ppermute x22, starting transfers between devices, flip(): lax.ppermute(x, axes, [(i, i ^ masks[bool(i & core)]) for i in range(coun...  25.8 us
    ppermute x22, waiting for transfers between devices, flip(): lax.ppermute(x, axes, [(i, i ^ masks[bool(i & core)]) for i in range(coun...  11.3 us
    pallas_call x2, Pallas kernels, load(): pl.pallas_call(lambda *refs: load_kernel(cuts, *refs), out_shape=tuple((p...  5.3 us
    pallas_call x2, Pallas kernels, expert_values(): pl.pallas_call(lambda *refs: expert_kernel(experts, len(pieces), 512, *re...  3.47 us
    unnamed x7, local copies, waits for them, and re-layouts  1.14 us
  transfers between devices with their start and end apart: 22, of which 11 were waited for; matrix products, arithmetic and copies ran while one was open for 7% of the time, Pallas kernels for 17%

profile of v6, /device:TPU:0, one launch (start us, length us, event | category | flops | bytes accessed | tf_op | source)
XLA Modules:
  0.0 52.3 jit_solution(10290450735608281718)
XLA Ops:
  0.6 1.0 %pack.1 = bf16[8,3712]{1,0:T(8,128)(2,1)S(1)} custom-call(bf16[8,3584]{1,0:T(8,128)(2,1)} %refs_0_, s32[8,8]{1,0:T(8,128)} %refs_1_.1, f32[8,8]{1,0:T(8,128)} %refs_2_.1), custom_call_target="tpu_custom_call" | custom-call | tf_op jit(solution)/shard_map/pack/pallas_call | solution.py:51
  1.7 4.1 %collective-permute-start.5 = (bf16[8,3712]{1,0:T(8,128)(2,1)S(1)}, bf16[8,3712]{1,0:T(8,128)(2,1)S(1)}, u32[]{:S(2)}, u32[]{:S(2)}) collective-permute-start(bf16[8,3712]{1,0:T(8,128)(2,1)S(1)} %pack.1), channel_id=1, source_target_pairs={{0,16},{1,17},{2,18},{3,19},{4,20},{5,21},{6,22},{7,23},{8,24},{9,... | collective-permute-start | bytes 178184 | tf_op jit(solution)/shard_map/ppermute | solution.py:133
  5.8 1.5 %collective-permute-start = (bf16[8,3712]{1,0:T(8,128)(2,1)S(1)}, bf16[8,3712]{1,0:T(8,128)(2,1)S(1)}, u32[]{:S(2)}, u32[]{:S(2)}) collective-permute-start(bf16[8,3712]{1,0:T(8,128)(2,1)S(1)} %pack.1), channel_id=1, source_target_pairs={{0,4},{1,5},{2,10},{3,11},{4,0},{5,1},{6,14},{7,15},{8,12},{9,13},... | collective-permute-start | bytes 178184 | tf_op jit(solution)/shard_map/ppermute | solution.py:133
  8.7 1.7 %collective-permute-start.6 = (bf16[8,3712]{1,0:T(8,128)(2,1)S(1)}, bf16[8,3712]{1,0:T(8,128)(2,1)S(1)}, u32[]{:S(2)}, u32[]{:S(2)}) collective-permute-start(bf16[8,3712]{1,0:T(8,128)(2,1)S(1)} %collective-permute-done.5), channel_id=1, source_target_pairs={{0,1},{1,0},{2,6},{3,7},{4,5},{5,4},{6,2},{7,3},{8,9},{9,8},{10,14... | collective-permute-start | bytes 178184 | tf_op jit(solution)/shard_map/ppermute | solution.py:133
  10.4 2.5 %collective-permute-done.6 = bf16[8,3712]{1,0:T(8,128)(2,1)S(1)} collective-permute-done((bf16[8,3712]{1,0:T(8,128)(2,1)S(1)}, bf16[8,3712]{1,0:T(8,128)(2,1)S(1)}, u32[]{:S(2)}, u32[]{:S(2)}) %collective-permute-start.6) | collective-permute-done | bytes 59424 | tf_op jit(solution)/shard_map/ppermute | solution.py:133
  12.9 1.8 %collective-permute-start.7 = (bf16[16,3712]{1,0:T(8,128)(2,1)S(1)}, bf16[16,3712]{1,0:T(8,128)(2,1)S(1)}, u32[]{:S(2)}, u32[]{:S(2)}) collective-permute-start(bf16[16,3712]{1,0:T(8,128)(2,1)S(1)} %get-tuple-element.43), channel_id=1, source_target_pairs={{0,4},{1,5},{2,10},{3,11},{4,0},{5,1},{6,14},{7,15},{8,12},{9,13},... | collective-permute-start | bytes 356360 | tf_op jit(solution)/shard_map/ppermute | solution.py:133
  14.7 1.1 %collective-permute-start.1 = (bf16[16,3712]{1,0:T(8,128)(2,1)S(1)}, bf16[16,3712]{1,0:T(8,128)(2,1)S(1)}, u32[]{:S(2)}, u32[]{:S(2)}) collective-permute-start(bf16[16,3712]{1,0:T(8,128)(2,1)S(1)} %pad_maximum_fusion.1), channel_id=1, source_target_pairs={{0,8},{1,9},{2,3},{3,2},{4,12},{5,13},{6,7},{7,6},{8,0},{9,1},{10,... | collective-permute-start | bytes 356360 | tf_op jit(solution)/shard_map/ppermute | solution.py:133
  15.9 2.0 %load.2.refs_5_ = bf16[3584,512]{1,0:T(8,128)(2,1)S(1)} custom-call(bf16[3584,512]{1,0:T(8,128)(2,1)} %bitcast.11), custom_call_target="tpu_custom_call" | custom-call | bytes 7340032 | tf_op jit(solution)/shard_map/load/pallas_call | solution.py:117
  17.9 1.2 %collective-permute-start.8 = (bf16[32,3712]{1,0:T(8,128)(2,1)S(1)}, bf16[32,3712]{1,0:T(8,128)(2,1)S(1)}, u32[]{:S(2)}, u32[]{:S(2)}) collective-permute-start(bf16[32,3712]{1,0:T(8,128)(2,1)S(1)} %constant_dynamic-update-slice_fusion.2.refs_1_), channel_id=1, source_target_pairs={{0,8},{1,9},{2,3},{3,2},{4,12},{5,13},{6,7},{7,6},{8,0},{9,1},{10,... | collective-permute-start | bytes 712712 | tf_op jit(solution)/shard_map/ppermute | solution.py:133
  19.6 1.6 %collective-permute-start.2 = (bf16[32,3712]{1,0:T(8,128)(2,1)S(1)}, bf16[32,3712]{1,0:T(8,128)(2,1)S(1)}, u32[]{:S(2)}, u32[]{:S(2)}) collective-permute-start(bf16[32,3712]{1,0:T(8,128)(2,1)S(1)} %pad_maximum_fusion.refs_1_), channel_id=1, source_target_pairs={{0,1},{1,0},{2,6},{3,7},{4,5},{5,4},{6,2},{7,3},{8,9},{9,8},{10,14... | collective-permute-start | bytes 712712 | tf_op jit(solution)/shard_map/ppermute | solution.py:133
  21.2 3.3 %load.3 = (bf16[3584,512]{1,0:T(8,128)(2,1)S(1)}, bf16[512,3584]{1,0:T(8,128)(2,1)S(1)}) custom-call(bf16[3584,512]{1,0:T(8,128)(2,1)} %bitcast.12, bf16[512,3584]{1,0:T(8,128)(2,1)} %bitcast.13), custom_call_target="tpu_custom_call" | custom-call | bytes 14680064 | tf_op jit(solution)/shard_map/load/pallas_call | solution.py:117
  26.2 1.7 %expert.3 = (bf16[32,3584]{1,0:T(8,128)(2,1)S(1)}, bf16[32,3584]{1,0:T(8,128)(2,1)S(1)}, bf16[32,3584]{1,0:T(8,128)(2,1)S(1)}, bf16[32,3584]{1,0:T(8,128)(2,1)S(1)}) custom-call(s32[1]{0:T(128)} %bitcast.refs_0_, bf16[32,3712]{1,0:T(8,128)(2,1)S(1)} %constant_dynamic-update-slice_fusion.2.refs_1_, bf16[32,3712]{1,0:T(8,128)(2,1)S(1)} %collective-permute-done.8.refs_2_, ...), custom_call_target="tpu_custom_call" | custom-call | flops 1409286144 | bytes 12910592 | tf_op jit(solution)/shard_map/expert/pallas_call | solution.py:84
  28.6 1.7 %expert.2 = (bf16[32,3584]{1,0:T(8,128)(2,1)S(1)}, bf16[32,3584]{1,0:T(8,128)(2,1)S(1)}, bf16[32,3584]{1,0:T(8,128)(2,1)S(1)}, bf16[32,3584]{1,0:T(8,128)(2,1)S(1)}) custom-call(s32[1]{0:T(128)} %bitcast.refs_0_, bf16[32,3712]{1,0:T(8,128)(2,1)S(1)} %pad_maximum_fusion.refs_1_, bf16[32,3712]{1,0:T(8,128)(2,1)S(1)} %collective-permute-done.2.refs_2_, ...), custom_call_target="tpu_custom_call" | custom-call | flops 1409286144 | bytes 12910592 | tf_op jit(solution)/shard_map/expert/pallas_call | solution.py:84
  31.1 1.1 %collective-permute-start.18 = (bf16[32,3584]{1,0:T(8,128)(2,1)S(1)}, bf16[32,3584]{1,0:T(8,128)(2,1)S(1)}, u32[]{:S(2)}, u32[]{:S(2)}) collective-permute-start(bf16[32,3584]{1,0:T(8,128)(2,1)S(1)} %add_convert_fusion), channel_id=1, source_target_pairs={{0,8},{1,9},{2,3},{3,2},{4,12},{5,13},{6,7},{7,6},{8,0},{9,1},{10,... | collective-permute-start | bytes 688136 | tf_op jit(solution)/shard_map/ppermute | solution.py:133
  32.3 1.4 %collective-permute-start.11 = (bf16[32,3584]{1,0:T(8,128)(2,1)S(1)}, bf16[32,3584]{1,0:T(8,128)(2,1)S(1)}, u32[]{:S(2)}, u32[]{:S(2)}) collective-permute-start(bf16[32,3584]{1,0:T(8,128)(2,1)S(1)} %add_convert_fusion.1), channel_id=1, source_target_pairs={{0,1},{1,0},{2,6},{3,7},{4,5},{5,4},{6,2},{7,3},{8,9},{9,8},{10,14... | collective-permute-start | bytes 688136 | tf_op jit(solution)/shard_map/ppermute | solution.py:133
  33.8 3.5 %collective-permute-done.18 = bf16[32,3584]{1,0:T(8,128)(2,1)S(1)} collective-permute-done((bf16[32,3584]{1,0:T(8,128)(2,1)S(1)}, bf16[32,3584]{1,0:T(8,128)(2,1)S(1)}, u32[]{:S(2)}, u32[]{:S(2)}) %collective-permute-start.18) | collective-permute-done | bytes 229408 | tf_op jit(solution)/shard_map/ppermute | solution.py:133
  37.3 1.5 %collective-permute-start.19 = (bf16[16,3584]{1,0:T(8,128)(2,1)S(1)}, bf16[16,3584]{1,0:T(8,128)(2,1)S(1)}, u32[]{:S(2)}, u32[]{:S(2)}) collective-permute-start(bf16[16,3584]{1,0:T(8,128)(2,1)S(1)} %slice.64), channel_id=1, source_target_pairs={{0,4},{1,5},{2,10},{3,11},{4,0},{5,1},{6,14},{7,15},{8,12},{9,13},... | collective-permute-start | bytes 344072 | tf_op jit(solution)/shard_map/ppermute | solution.py:133
  39.2 1.1 %collective-permute-start.12 = (bf16[16,3584]{1,0:T(8,128)(2,1)S(1)}, bf16[16,3584]{1,0:T(8,128)(2,1)S(1)}, u32[]{:S(2)}, u32[]{:S(2)}) collective-permute-start(bf16[16,3584]{1,0:T(8,128)(2,1)S(1)} %slice.65), channel_id=1, source_target_pairs={{0,8},{1,9},{2,3},{3,2},{4,12},{5,13},{6,7},{7,6},{8,0},{9,1},{10,... | collective-permute-start | bytes 344072 | tf_op jit(solution)/shard_map/ppermute | solution.py:133
  40.3 1.9 %collective-permute-done.19 = bf16[16,3584]{1,0:T(8,128)(2,1)S(1)} collective-permute-done((bf16[16,3584]{1,0:T(8,128)(2,1)S(1)}, bf16[16,3584]{1,0:T(8,128)(2,1)S(1)}, u32[]{:S(2)}, u32[]{:S(2)}) %collective-permute-start.19) | collective-permute-done | bytes 114720 | tf_op jit(solution)/shard_map/ppermute | solution.py:133
  42.2 1.3 %collective-permute-start.20 = (bf16[8,3584]{1,0:T(8,128)(2,1)S(1)}, bf16[8,3584]{1,0:T(8,128)(2,1)S(1)}, u32[]{:S(2)}, u32[]{:S(2)}) collective-permute-start(bf16[8,3584]{1,0:T(8,128)(2,1)S(1)} %slice.66), channel_id=1, source_target_pairs={{0,1},{1,0},{2,6},{3,7},{4,5},{5,4},{6,2},{7,3},{8,9},{9,8},{10,14... | collective-permute-start | bytes 172040 | tf_op jit(solution)/shard_map/ppermute | solution.py:133
  44.1 1.5 %collective-permute-start.13 = (bf16[8,3584]{1,0:T(8,128)(2,1)S(1)}, bf16[8,3584]{1,0:T(8,128)(2,1)S(1)}, u32[]{:S(2)}, u32[]{:S(2)}) collective-permute-start(bf16[8,3584]{1,0:T(8,128)(2,1)S(1)} %slice.67), channel_id=1, source_target_pairs={{0,4},{1,5},{2,10},{3,11},{4,0},{5,1},{6,14},{7,15},{8,12},{9,13},... | collective-permute-start | bytes 172040 | tf_op jit(solution)/shard_map/ppermute | solution.py:133
  46.5 2.8 %collective-permute-start.21 = (bf16[8,3584]{1,0:T(8,128)(2,1)S(1)}, bf16[8,3584]{1,0:T(8,128)(2,1)S(1)}, u32[]{:S(2)}, u32[]{:S(2)}) collective-permute-start(bf16[8,3584]{1,0:T(8,128)(2,1)S(1)} %fusion.7), channel_id=1, source_target_pairs={{0,16},{1,17},{2,18},{3,19},{4,20},{5,21},{6,22},{7,23},{8,24},{9,... | collective-permute-start | bytes 172040 | tf_op jit(solution)/shard_map/ppermute | solution.py:133
  49.3 1.0 %fusion.1 = bf16[1,8,64,512]{3,2,1,0:T(8,128)(2,1)S(1)} fusion(bf16[8,128,576]{1,2,0:T(8,128)(2,1)S(1)} %copy-done.1, f32[8,64]{1,0:T(8,128)S(1)} %fusion.11, f32[8,64,128]{2,1,0:T(8,128)S(1)} %fusion.4), kind=kOutput, calls=%fused_computation.2 | convolution fusion | flops 67568256 | bytes 2101248 | tf_op jit(solution)/shard_map/bht,btc->bhc/dot_general | solution.py:25
  50.3 1.1 %copy.13 = bf16[1,8,64,512]{3,1,2,0:T(8,128)(2,1)} copy(bf16[1,8,64,512]{3,2,1,0:T(8,128)(2,1)S(1)} %fusion.1) | data formatting | bytes 1048576
  (51 shorter events, 8.0 us)
Async XLA Ops:
  0.6 24.4 %copy-start = (bf16[8,64,576]{2,1,0:T(8,128)(2,1)S(1)}, bf16[8,64,576]{2,1,0:T(8,128)(2,1)}, u32[]{:S(2)}) copy-start(bf16[8,64,576]{2,1,0:T(8,128)(2,1)} %param.10) | copy-start | bytes 1769476
  1.7 7.0 %collective-permute-start.5 = (bf16[8,3712]{1,0:T(8,128)(2,1)S(1)}, bf16[8,3712]{1,0:T(8,128)(2,1)S(1)}, u32[]{:S(2)}, u32[]{:S(2)}) collective-permute-start(bf16[8,3712]{1,0:T(8,128)(2,1)S(1)} %pack.1), channel_id=1, source_target_pairs={{0,16},{1,17},{2,18},{3,19},{4,20},{5,21},{6,22},{7,23},{8,24},{9,... | collective-permute-start | bytes 178184 | tf_op jit(solution)/shard_map/ppermute | solution.py:133
  5.8 8.9 %collective-permute-start = (bf16[8,3712]{1,0:T(8,128)(2,1)S(1)}, bf16[8,3712]{1,0:T(8,128)(2,1)S(1)}, u32[]{:S(2)}, u32[]{:S(2)}) collective-permute-start(bf16[8,3712]{1,0:T(8,128)(2,1)S(1)} %pack.1), channel_id=1, source_target_pairs={{0,4},{1,5},{2,10},{3,11},{4,0},{5,1},{6,14},{7,15},{8,12},{9,13},... | collective-permute-start | bytes 178184 | tf_op jit(solution)/shard_map/ppermute | solution.py:133
  8.7 4.2 %collective-permute-start.6 = (bf16[8,3712]{1,0:T(8,128)(2,1)S(1)}, bf16[8,3712]{1,0:T(8,128)(2,1)S(1)}, u32[]{:S(2)}, u32[]{:S(2)}) collective-permute-start(bf16[8,3712]{1,0:T(8,128)(2,1)S(1)} %collective-permute-done.5), channel_id=1, source_target_pairs={{0,1},{1,0},{2,6},{3,7},{4,5},{5,4},{6,2},{7,3},{8,9},{9,8},{10,14... | collective-permute-start | bytes 178184 | tf_op jit(solution)/shard_map/ppermute | solution.py:133
  12.9 5.0 %collective-permute-start.7 = (bf16[16,3712]{1,0:T(8,128)(2,1)S(1)}, bf16[16,3712]{1,0:T(8,128)(2,1)S(1)}, u32[]{:S(2)}, u32[]{:S(2)}) collective-permute-start(bf16[16,3712]{1,0:T(8,128)(2,1)S(1)} %get-tuple-element.43), channel_id=1, source_target_pairs={{0,4},{1,5},{2,10},{3,11},{4,0},{5,1},{6,14},{7,15},{8,12},{9,13},... | collective-permute-start | bytes 356360 | tf_op jit(solution)/shard_map/ppermute | solution.py:133
  14.7 4.9 %collective-permute-start.1 = (bf16[16,3712]{1,0:T(8,128)(2,1)S(1)}, bf16[16,3712]{1,0:T(8,128)(2,1)S(1)}, u32[]{:S(2)}, u32[]{:S(2)}) collective-permute-start(bf16[16,3712]{1,0:T(8,128)(2,1)S(1)} %pad_maximum_fusion.1), channel_id=1, source_target_pairs={{0,8},{1,9},{2,3},{3,2},{4,12},{5,13},{6,7},{7,6},{8,0},{9,1},{10,... | collective-permute-start | bytes 356360 | tf_op jit(solution)/shard_map/ppermute | solution.py:133
  17.9 6.5 %collective-permute-start.8 = (bf16[32,3712]{1,0:T(8,128)(2,1)S(1)}, bf16[32,3712]{1,0:T(8,128)(2,1)S(1)}, u32[]{:S(2)}, u32[]{:S(2)}) collective-permute-start(bf16[32,3712]{1,0:T(8,128)(2,1)S(1)} %constant_dynamic-update-slice_fusion.2.refs_1_), channel_id=1, source_target_pairs={{0,8},{1,9},{2,3},{3,2},{4,12},{5,13},{6,7},{7,6},{8,0},{9,1},{10,... | collective-permute-start | bytes 712712 | tf_op jit(solution)/shard_map/ppermute | solution.py:133
  19.6 6.2 %collective-permute-start.2 = (bf16[32,3712]{1,0:T(8,128)(2,1)S(1)}, bf16[32,3712]{1,0:T(8,128)(2,1)S(1)}, u32[]{:S(2)}, u32[]{:S(2)}) collective-permute-start(bf16[32,3712]{1,0:T(8,128)(2,1)S(1)} %pad_maximum_fusion.refs_1_), channel_id=1, source_target_pairs={{0,1},{1,0},{2,6},{3,7},{4,5},{5,4},{6,2},{7,3},{8,9},{9,8},{10,14... | collective-permute-start | bytes 712712 | tf_op jit(solution)/shard_map/ppermute | solution.py:133
  21.2 4.8 %collective-permute-start.14 = (bf16[32,3712]{1,0:T(8,128)(2,1)S(1)}, bf16[32,3712]{1,0:T(8,128)(2,1)S(1)}, u32[]{:S(2)}, u32[]{:S(2)}) collective-permute-start(bf16[32,3712]{1,0:T(8,128)(2,1)S(1)} %constant_dynamic-update-slice_fusion.2.refs_1_), channel_id=1, source_target_pairs={{0,2},{1,3},{2,0},{3,1},{4,6},{5,7},{6,4},{7,5},{8,10},{9,11},{10,... | collective-permute-start | bytes 712712 | tf_op jit(solution)/shard_map/ppermute | solution.py:133
  21.2 3.9 %copy-start.1 = (bf16[8,128,576]{1,2,0:T(8,128)(2,1)S(1)}, bf16[8,128,576]{1,2,0:T(8,128)(2,1)}, u32[]{:S(2)}) copy-start(bf16[8,128,576]{1,2,0:T(8,128)(2,1)} %param.11) | copy-start | bytes 3538948
  24.5 1.7 %collective-permute-start.15 = (bf16[32,3712]{1,0:T(8,128)(2,1)S(1)}, bf16[32,3712]{1,0:T(8,128)(2,1)S(1)}, u32[]{:S(2)}, u32[]{:S(2)}) collective-permute-start(bf16[32,3712]{1,0:T(8,128)(2,1)S(1)} %collective-permute-done.8.refs_2_), channel_id=1, source_target_pairs={{0,2},{1,3},{2,0},{3,1},{4,6},{5,7},{6,4},{7,5},{8,10},{9,11},{10,... | collective-permute-start | bytes 712712 | tf_op jit(solution)/shard_map/ppermute | solution.py:133
  25.4 3.2 %collective-permute-start.3 = (bf16[32,3712]{1,0:T(8,128)(2,1)S(1)}, bf16[32,3712]{1,0:T(8,128)(2,1)S(1)}, u32[]{:S(2)}, u32[]{:S(2)}) collective-permute-start(bf16[32,3712]{1,0:T(8,128)(2,1)S(1)} %pad_maximum_fusion.refs_1_), channel_id=1, source_target_pairs={{0,2},{1,3},{2,0},{3,1},{4,6},{5,7},{6,4},{7,5},{8,10},{9,11},{10,... | collective-permute-start | bytes 712712 | tf_op jit(solution)/shard_map/ppermute | solution.py:133
  25.8 2.8 %collective-permute-start.4 = (bf16[32,3712]{1,0:T(8,128)(2,1)S(1)}, bf16[32,3712]{1,0:T(8,128)(2,1)S(1)}, u32[]{:S(2)}, u32[]{:S(2)}) collective-permute-start(bf16[32,3712]{1,0:T(8,128)(2,1)S(1)} %collective-permute-done.2.refs_2_), channel_id=1, source_target_pairs={{0,2},{1,3},{2,0},{3,1},{4,6},{5,7},{6,4},{7,5},{8,10},{9,11},{10,... | collective-permute-start | bytes 712712 | tf_op jit(solution)/shard_map/ppermute | solution.py:133
  27.9 3.2 %collective-permute-start.17 = (bf16[32,3584]{1,0:T(8,128)(2,1)S(1)}, bf16[32,3584]{1,0:T(8,128)(2,1)S(1)}, u32[]{:S(2)}, u32[]{:S(2)}) collective-permute-start(bf16[32,3584]{1,0:T(8,128)(2,1)S(1)} %get-tuple-element.41), channel_id=1, source_target_pairs={{0,2},{1,3},{2,0},{3,1},{4,6},{5,7},{6,4},{7,5},{8,10},{9,11},{10,... | collective-permute-start | bytes 688136 | tf_op jit(solution)/shard_map/ppermute | solution.py:133
  30.4 1.9 %collective-permute-start.10 = (bf16[32,3584]{1,0:T(8,128)(2,1)S(1)}, bf16[32,3584]{1,0:T(8,128)(2,1)S(1)}, u32[]{:S(2)}, u32[]{:S(2)}) collective-permute-start(bf16[32,3584]{1,0:T(8,128)(2,1)S(1)} %get-tuple-element.36), channel_id=1, source_target_pairs={{0,2},{1,3},{2,0},{3,1},{4,6},{5,7},{6,4},{7,5},{8,10},{9,11},{10,... | collective-permute-start | bytes 688136 | tf_op jit(solution)/shard_map/ppermute | solution.py:133
  30.6 8.2 %collective-permute-start.9 = (bf16[32,3584]{1,0:T(8,128)(2,1)S(1)}, bf16[32,3584]{1,0:T(8,128)(2,1)S(1)}, u32[]{:S(2)}, u32[]{:S(2)}) collective-permute-start(bf16[32,3584]{1,0:T(8,128)(2,1)S(1)} %get-tuple-element.34), channel_id=1, source_target_pairs={{0,2},{1,3},{2,0},{3,1},{4,6},{5,7},{6,4},{7,5},{8,10},{9,11},{10,... | collective-permute-start | bytes 688136 | tf_op jit(solution)/shard_map/ppermute | solution.py:133
  30.9 2.8 %collective-permute-start.16 = (bf16[32,3584]{1,0:T(8,128)(2,1)S(1)}, bf16[32,3584]{1,0:T(8,128)(2,1)S(1)}, u32[]{:S(2)}, u32[]{:S(2)}) collective-permute-start(bf16[32,3584]{1,0:T(8,128)(2,1)S(1)} %get-tuple-element.39), channel_id=1, source_target_pairs={{0,2},{1,3},{2,0},{3,1},{4,6},{5,7},{6,4},{7,5},{8,10},{9,11},{10,... | collective-permute-start | bytes 688136 | tf_op jit(solution)/shard_map/ppermute | solution.py:133
  31.1 6.1 %collective-permute-start.18 = (bf16[32,3584]{1,0:T(8,128)(2,1)S(1)}, bf16[32,3584]{1,0:T(8,128)(2,1)S(1)}, u32[]{:S(2)}, u32[]{:S(2)}) collective-permute-start(bf16[32,3584]{1,0:T(8,128)(2,1)S(1)} %add_convert_fusion), channel_id=1, source_target_pairs={{0,8},{1,9},{2,3},{3,2},{4,12},{5,13},{6,7},{7,6},{8,0},{9,1},{10,... | collective-permute-start | bytes 688136 | tf_op jit(solution)/shard_map/ppermute | solution.py:133
  32.3 6.7 %collective-permute-start.11 = (bf16[32,3584]{1,0:T(8,128)(2,1)S(1)}, bf16[32,3584]{1,0:T(8,128)(2,1)S(1)}, u32[]{:S(2)}, u32[]{:S(2)}) collective-permute-start(bf16[32,3584]{1,0:T(8,128)(2,1)S(1)} %add_convert_fusion.1), channel_id=1, source_target_pairs={{0,1},{1,0},{2,6},{3,7},{4,5},{5,4},{6,2},{7,3},{8,9},{9,8},{10,14... | collective-permute-start | bytes 688136 | tf_op jit(solution)/shard_map/ppermute | solution.py:133
  37.3 4.9 %collective-permute-start.19 = (bf16[16,3584]{1,0:T(8,128)(2,1)S(1)}, bf16[16,3584]{1,0:T(8,128)(2,1)S(1)}, u32[]{:S(2)}, u32[]{:S(2)}) collective-permute-start(bf16[16,3584]{1,0:T(8,128)(2,1)S(1)} %slice.64), channel_id=1, source_target_pairs={{0,4},{1,5},{2,10},{3,11},{4,0},{5,1},{6,14},{7,15},{8,12},{9,13},... | collective-permute-start | bytes 344072 | tf_op jit(solution)/shard_map/ppermute | solution.py:133
  39.2 4.9 %collective-permute-start.12 = (bf16[16,3584]{1,0:T(8,128)(2,1)S(1)}, bf16[16,3584]{1,0:T(8,128)(2,1)S(1)}, u32[]{:S(2)}, u32[]{:S(2)}) collective-permute-start(bf16[16,3584]{1,0:T(8,128)(2,1)S(1)} %slice.65), channel_id=1, source_target_pairs={{0,8},{1,9},{2,3},{3,2},{4,12},{5,13},{6,7},{7,6},{8,0},{9,1},{10,... | collective-permute-start | bytes 344072 | tf_op jit(solution)/shard_map/ppermute | solution.py:133
  42.2 4.2 %collective-permute-start.20 = (bf16[8,3584]{1,0:T(8,128)(2,1)S(1)}, bf16[8,3584]{1,0:T(8,128)(2,1)S(1)}, u32[]{:S(2)}, u32[]{:S(2)}) collective-permute-start(bf16[8,3584]{1,0:T(8,128)(2,1)S(1)} %slice.66), channel_id=1, source_target_pairs={{0,1},{1,0},{2,6},{3,7},{4,5},{5,4},{6,2},{7,3},{8,9},{9,8},{10,14... | collective-permute-start | bytes 172040 | tf_op jit(solution)/shard_map/ppermute | solution.py:133
  44.1 7.3 %collective-permute-start.13 = (bf16[8,3584]{1,0:T(8,128)(2,1)S(1)}, bf16[8,3584]{1,0:T(8,128)(2,1)S(1)}, u32[]{:S(2)}, u32[]{:S(2)}) collective-permute-start(bf16[8,3584]{1,0:T(8,128)(2,1)S(1)} %slice.67), channel_id=1, source_target_pairs={{0,4},{1,5},{2,10},{3,11},{4,0},{5,1},{6,14},{7,15},{8,12},{9,13},... | collective-permute-start | bytes 172040 | tf_op jit(solution)/shard_map/ppermute | solution.py:133
  46.5 5.1 %collective-permute-start.21 = (bf16[8,3584]{1,0:T(8,128)(2,1)S(1)}, bf16[8,3584]{1,0:T(8,128)(2,1)S(1)}, u32[]{:S(2)}, u32[]{:S(2)}) collective-permute-start(bf16[8,3584]{1,0:T(8,128)(2,1)S(1)} %fusion.7), channel_id=1, source_target_pairs={{0,16},{1,17},{2,18},{3,19},{4,20},{5,21},{6,22},{7,23},{8,24},{9,... | collective-permute-start | bytes 172040 | tf_op jit(solution)/shard_map/ppermute | solution.py:133

commit v7 on v6

--- a/solution.py
+++ b/solution.py
@@ -155,17 +155,23 @@
     hidden, me = lax.optimization_barrier((hidden, me))
     packed = pack(hidden, ids, weights, experts)
 
-    def gather(held, steps, beside=None):
-        for masks in steps[:-1]:
+    def gather(held, steps, matrices=()):
+        loaded = []
+        for k, masks in enumerate(steps):
             sent = flip(held, masks)
-            if beside is not None and masks == steps[-2]:
-                (beside,) = load((beside,), held)
-                sent, beside = lax.optimization_barrier((sent, beside))
-            held = jnp.concatenate([held, sent], axis=0)
-        return held, flip(held, steps[-1]), beside
+            place = k - len(steps) + len(matrices)
+            if matrices and place >= 0:
+                (matrix,) = load((matrices[place],), held)
+                sent, matrix = lax.optimization_barrier((sent, matrix))
+                loaded.append(matrix)
+            if masks != steps[-1]:
+                held = jnp.concatenate([held, sent], axis=0)
+        return held, sent, loaded
 
     def scatter(low, high, from_low, from_high, steps):
-        sent = flip(add(high, flip(from_high, sibling)).astype(jnp.bfloat16), steps[-1])
+        high = add(high, flip(from_high, sibling)).astype(jnp.bfloat16)
+        sent = flip(high, steps[-1])
+        from_low, _ = lax.optimization_barrier((from_low, high))
         held = add(low, flip(from_low, sibling), sent)
         for masks in steps[-2::-1]:
             half = held.shape[0] // 2
@@ -175,10 +181,7 @@
 
     far = flip(packed, across)
     near_low, near_high, _ = gather(packed, near_steps)
-    far_low, far_high, gate = gather(far, far_steps, w_gate[0])
-    up, down = load((w_up[0], w_down[0]), far_low)
-    far_high, up, down = lax.optimization_barrier((far_high, up, down))
-    loaded = (gate, up, down)
+    far_low, far_high, loaded = gather(far, far_steps, (w_gate[0], w_up[0], w_down[0]))
     results = []
     for low, high, steps in ((near_low, near_high, near_steps), (far_low, far_high, far_steps)):
         pieces = (low, high, flip(low, sibling), flip(high, sibling))

time: 52.5 us -> 51.7 us (0.985)
  waiting for transfers between devices: 11.3 us -> 9.79 us
  Pallas kernels: 9.77 us -> 10.7 us
    ppermute x22, waiting for transfers between devices: 11.3 us -> 9.79 us  [flip(): lax.ppermute(x, axes, [(i, i ^ masks[bool(i & core)]) for i in range(coun...]
    pallas_call x2 -> x3, Pallas kernels: 5.3 us -> 6.24 us  [load(): pl.pallas_call(lambda *refs: load_kernel(cuts, *refs), out_shape=tuple((p...]
  transfers between devices with their start and end apart: 22 -> 22, of which waited for: 11 -> 11; matrix products, arithmetic and copies ran while one was open for 7% -> 8% of each run, Pallas kernels for 17% -> 19%
where the time goes in v7:
time: 51.7 us; the launch traced here: 51.5 us
  starting transfers between devices  25.6 us (50%)
  Pallas kernels  10.7 us (21%)
  waiting for transfers between devices  9.79 us (19%)
  other arithmetic  1.99 us (4%)
  matrix products  1.38 us (3%)
  local copies, waits for them, and re-layouts  1.2 us (2%)
  between operations  0.84 us (2%)
    ppermute x22, starting transfers between devices, flip(): lax.ppermute(x, axes, [(i, i ^ masks[bool(i & core)]) for i in range(coun...  25.6 us
    ppermute x22, waiting for transfers between devices, flip(): lax.ppermute(x, axes, [(i, i ^ masks[bool(i & core)]) for i in range(coun...  9.79 us
    pallas_call x3, Pallas kernels, load(): pl.pallas_call(lambda *refs: load_kernel(cuts, *refs), out_shape=tuple((p...  6.24 us
    pallas_call x2, Pallas kernels, expert_values(): pl.pallas_call(lambda *refs: expert_kernel(experts, len(pieces), 512, *re...  3.48 us
    unnamed x7, local copies, waits for them, and re-layouts  1.14 us
  transfers between devices with their start and end apart: 22, of which 11 were waited for; matrix products, arithmetic and copies ran while one was open for 8% of the time, Pallas kernels for 19%

profile of v7, /device:TPU:0, one launch (start us, length us, event | category | flops | bytes accessed | tf_op | source)
XLA Modules:
  0.0 51.5 jit_solution(150945802558886419)
XLA Ops:
  0.6 1.0 %pack.1 = bf16[8,3712]{1,0:T(8,128)(2,1)S(1)} custom-call(bf16[8,3584]{1,0:T(8,128)(2,1)} %refs_0_, s32[8,8]{1,0:T(8,128)} %refs_1_.1, f32[8,8]{1,0:T(8,128)} %refs_2_.1), custom_call_target="tpu_custom_call" | custom-call | tf_op jit(solution)/shard_map/pack/pallas_call | solution.py:51
  1.7 4.1 %collective-permute-start.5 = (bf16[8,3712]{1,0:T(8,128)(2,1)S(1)}, bf16[8,3712]{1,0:T(8,128)(2,1)S(1)}, u32[]{:S(2)}, u32[]{:S(2)}) collective-permute-start(bf16[8,3712]{1,0:T(8,128)(2,1)S(1)} %pack.1), channel_id=1, source_target_pairs={{0,16},{1,17},{2,18},{3,19},{4,20},{5,21},{6,22},{7,23},{8,24},{9,... | collective-permute-start | bytes 178184 | tf_op jit(solution)/shard_map/ppermute | solution.py:133
  5.8 1.5 %collective-permute-start = (bf16[8,3712]{1,0:T(8,128)(2,1)S(1)}, bf16[8,3712]{1,0:T(8,128)(2,1)S(1)}, u32[]{:S(2)}, u32[]{:S(2)}) collective-permute-start(bf16[8,3712]{1,0:T(8,128)(2,1)S(1)} %pack.1), channel_id=1, source_target_pairs={{0,4},{1,5},{2,10},{3,11},{4,0},{5,1},{6,14},{7,15},{8,12},{9,13},... | collective-permute-start | bytes 178184 | tf_op jit(solution)/shard_map/ppermute | solution.py:133
  8.7 1.7 %collective-permute-start.6 = (bf16[8,3712]{1,0:T(8,128)(2,1)S(1)}, bf16[8,3712]{1,0:T(8,128)(2,1)S(1)}, u32[]{:S(2)}, u32[]{:S(2)}) collective-permute-start(bf16[8,3712]{1,0:T(8,128)(2,1)S(1)} %collective-permute-done.5), channel_id=1, source_target_pairs={{0,1},{1,0},{2,6},{3,7},{4,5},{5,4},{6,2},{7,3},{8,9},{9,8},{10,14... | collective-permute-start | bytes 178184 | tf_op jit(solution)/shard_map/ppermute | solution.py:133
  10.4 2.0 %load.3.refs_5_ = bf16[3584,512]{1,0:T(8,128)(2,1)S(1)} custom-call(bf16[3584,512]{1,0:T(8,128)(2,1)} %bitcast.11), custom_call_target="tpu_custom_call" | custom-call | bytes 7340032 | tf_op jit(solution)/shard_map/load/pallas_call | solution.py:117
  12.9 1.8 %collective-permute-start.7 = (bf16[16,3712]{1,0:T(8,128)(2,1)S(1)}, bf16[16,3712]{1,0:T(8,128)(2,1)S(1)}, u32[]{:S(2)}, u32[]{:S(2)}) collective-permute-start(bf16[16,3712]{1,0:T(8,128)(2,1)S(1)} %get-tuple-element.45), channel_id=1, source_target_pairs={{0,4},{1,5},{2,10},{3,11},{4,0},{5,1},{6,14},{7,15},{8,12},{9,13},... | collective-permute-start | bytes 356360 | tf_op jit(solution)/shard_map/ppermute | solution.py:133
  14.7 1.1 %collective-permute-start.1 = (bf16[16,3712]{1,0:T(8,128)(2,1)S(1)}, bf16[16,3712]{1,0:T(8,128)(2,1)S(1)}, u32[]{:S(2)}, u32[]{:S(2)}) collective-permute-start(bf16[16,3712]{1,0:T(8,128)(2,1)S(1)} %pad_maximum_fusion.1), channel_id=1, source_target_pairs={{0,8},{1,9},{2,3},{3,2},{4,12},{5,13},{6,7},{7,6},{8,0},{9,1},{10,... | collective-permute-start | bytes 356360 | tf_op jit(solution)/shard_map/ppermute | solution.py:133
  15.9 2.0 %load.4.refs_6_ = bf16[3584,512]{1,0:T(8,128)(2,1)S(1)} custom-call(bf16[3584,512]{1,0:T(8,128)(2,1)} %bitcast.12), custom_call_target="tpu_custom_call" | custom-call | bytes 7340032 | tf_op jit(solution)/shard_map/load/pallas_call | solution.py:117
  17.9 1.2 %collective-permute-start.8 = (bf16[32,3712]{1,0:T(8,128)(2,1)S(1)}, bf16[32,3712]{1,0:T(8,128)(2,1)S(1)}, u32[]{:S(2)}, u32[]{:S(2)}) collective-permute-start(bf16[32,3712]{1,0:T(8,128)(2,1)S(1)} %constant_dynamic-update-slice_fusion.2.refs_1_), channel_id=1, source_target_pairs={{0,8},{1,9},{2,3},{3,2},{4,12},{5,13},{6,7},{7,6},{8,0},{9,1},{10,... | collective-permute-start | bytes 712712 | tf_op jit(solution)/shard_map/ppermute | solution.py:133
  19.6 1.6 %collective-permute-start.2 = (bf16[32,3712]{1,0:T(8,128)(2,1)S(1)}, bf16[32,3712]{1,0:T(8,128)(2,1)S(1)}, u32[]{:S(2)}, u32[]{:S(2)}) collective-permute-start(bf16[32,3712]{1,0:T(8,128)(2,1)S(1)} %pad_maximum_fusion.refs_1_), channel_id=1, source_target_pairs={{0,1},{1,0},{2,6},{3,7},{4,5},{5,4},{6,2},{7,3},{8,9},{9,8},{10,14... | collective-permute-start | bytes 712712 | tf_op jit(solution)/shard_map/ppermute | solution.py:133
  21.2 2.1 %load.5.refs_7_ = bf16[512,3584]{1,0:T(8,128)(2,1)S(1)} custom-call(bf16[512,3584]{1,0:T(8,128)(2,1)} %bitcast.13), custom_call_target="tpu_custom_call" | custom-call | bytes 7340032 | tf_op jit(solution)/shard_map/load/pallas_call | solution.py:117
  25.8 1.7 %expert.3 = (bf16[32,3584]{1,0:T(8,128)(2,1)S(1)}, bf16[32,3584]{1,0:T(8,128)(2,1)S(1)}, bf16[32,3584]{1,0:T(8,128)(2,1)S(1)}, bf16[32,3584]{1,0:T(8,128)(2,1)S(1)}) custom-call(s32[1]{0:T(128)} %bitcast.refs_0_, bf16[32,3712]{1,0:T(8,128)(2,1)S(1)} %constant_dynamic-update-slice_fusion.2.refs_1_, bf16[32,3712]{1,0:T(8,128)(2,1)S(1)} %collective-permute-done.8.refs_2_, ...), custom_call_target="tpu_custom_call" | custom-call | flops 1409286144 | bytes 12910592 | tf_op jit(solution)/shard_map/expert/pallas_call | solution.py:84
  28.4 1.7 %expert.2 = (bf16[32,3584]{1,0:T(8,128)(2,1)S(1)}, bf16[32,3584]{1,0:T(8,128)(2,1)S(1)}, bf16[32,3584]{1,0:T(8,128)(2,1)S(1)}, bf16[32,3584]{1,0:T(8,128)(2,1)S(1)}) custom-call(s32[1]{0:T(128)} %bitcast.refs_0_, bf16[32,3712]{1,0:T(8,128)(2,1)S(1)} %pad_maximum_fusion.refs_1_, bf16[32,3712]{1,0:T(8,128)(2,1)S(1)} %collective-permute-done.2.refs_2_, ...), custom_call_target="tpu_custom_call" | custom-call | flops 1409286144 | bytes 12910592 | tf_op jit(solution)/shard_map/expert/pallas_call | solution.py:84
  30.3 1.1 %collective-permute-start.18 = (bf16[32,3584]{1,0:T(8,128)(2,1)S(1)}, bf16[32,3584]{1,0:T(8,128)(2,1)S(1)}, u32[]{:S(2)}, u32[]{:S(2)}) collective-permute-start(bf16[32,3584]{1,0:T(8,128)(2,1)S(1)} %add_convert_fusion), channel_id=1, source_target_pairs={{0,8},{1,9},{2,3},{3,2},{4,12},{5,13},{6,7},{7,6},{8,0},{9,1},{10,... | collective-permute-start | bytes 688136 | tf_op jit(solution)/shard_map/ppermute | solution.py:133
  32.1 1.2 %collective-permute-start.11 = (bf16[32,3584]{1,0:T(8,128)(2,1)S(1)}, bf16[32,3584]{1,0:T(8,128)(2,1)S(1)}, u32[]{:S(2)}, u32[]{:S(2)}) collective-permute-start(bf16[32,3584]{1,0:T(8,128)(2,1)S(1)} %add_convert_fusion.1), channel_id=1, source_target_pairs={{0,1},{1,0},{2,6},{3,7},{4,5},{5,4},{6,2},{7,3},{8,9},{9,8},{10,14... | collective-permute-start | bytes 688136 | tf_op jit(solution)/shard_map/ppermute | solution.py:133
  33.3 3.1 %collective-permute-done.18 = bf16[32,3584]{1,0:T(8,128)(2,1)S(1)} collective-permute-done((bf16[32,3584]{1,0:T(8,128)(2,1)S(1)}, bf16[32,3584]{1,0:T(8,128)(2,1)S(1)}, u32[]{:S(2)}, u32[]{:S(2)}) %collective-permute-start.18) | collective-permute-done | bytes 229408 | tf_op jit(solution)/shard_map/ppermute | solution.py:133
  36.5 1.4 %collective-permute-start.19 = (bf16[16,3584]{1,0:T(8,128)(2,1)S(1)}, bf16[16,3584]{1,0:T(8,128)(2,1)S(1)}, u32[]{:S(2)}, u32[]{:S(2)}) collective-permute-start(bf16[16,3584]{1,0:T(8,128)(2,1)S(1)} %slice.64), channel_id=1, source_target_pairs={{0,4},{1,5},{2,10},{3,11},{4,0},{5,1},{6,14},{7,15},{8,12},{9,13},... | collective-permute-start | bytes 344072 | tf_op jit(solution)/shard_map/ppermute | solution.py:133
  38.5 1.1 %collective-permute-start.12 = (bf16[16,3584]{1,0:T(8,128)(2,1)S(1)}, bf16[16,3584]{1,0:T(8,128)(2,1)S(1)}, u32[]{:S(2)}, u32[]{:S(2)}) collective-permute-start(bf16[16,3584]{1,0:T(8,128)(2,1)S(1)} %slice.65), channel_id=1, source_target_pairs={{0,8},{1,9},{2,3},{3,2},{4,12},{5,13},{6,7},{7,6},{8,0},{9,1},{10,... | collective-permute-start | bytes 344072 | tf_op jit(solution)/shard_map/ppermute | solution.py:133
  39.6 1.8 %collective-permute-done.19 = bf16[16,3584]{1,0:T(8,128)(2,1)S(1)} collective-permute-done((bf16[16,3584]{1,0:T(8,128)(2,1)S(1)}, bf16[16,3584]{1,0:T(8,128)(2,1)S(1)}, u32[]{:S(2)}, u32[]{:S(2)}) %collective-permute-start.19) | collective-permute-done | bytes 114720 | tf_op jit(solution)/shard_map/ppermute | solution.py:133
  41.4 1.5 %collective-permute-start.20 = (bf16[8,3584]{1,0:T(8,128)(2,1)S(1)}, bf16[8,3584]{1,0:T(8,128)(2,1)S(1)}, u32[]{:S(2)}, u32[]{:S(2)}) collective-permute-start(bf16[8,3584]{1,0:T(8,128)(2,1)S(1)} %slice.66), channel_id=1, source_target_pairs={{0,1},{1,0},{2,6},{3,7},{4,5},{5,4},{6,2},{7,3},{8,9},{9,8},{10,14... | collective-permute-start | bytes 172040 | tf_op jit(solution)/shard_map/ppermute | solution.py:133
  43.4 1.3 %collective-permute-start.13 = (bf16[8,3584]{1,0:T(8,128)(2,1)S(1)}, bf16[8,3584]{1,0:T(8,128)(2,1)S(1)}, u32[]{:S(2)}, u32[]{:S(2)}) collective-permute-start(bf16[8,3584]{1,0:T(8,128)(2,1)S(1)} %slice.67), channel_id=1, source_target_pairs={{0,4},{1,5},{2,10},{3,11},{4,0},{5,1},{6,14},{7,15},{8,12},{9,13},... | collective-permute-start | bytes 172040 | tf_op jit(solution)/shard_map/ppermute | solution.py:133
  45.7 2.9 %collective-permute-start.21 = (bf16[8,3584]{1,0:T(8,128)(2,1)S(1)}, bf16[8,3584]{1,0:T(8,128)(2,1)S(1)}, u32[]{:S(2)}, u32[]{:S(2)}) collective-permute-start(bf16[8,3584]{1,0:T(8,128)(2,1)S(1)} %fusion.7), channel_id=1, source_target_pairs={{0,16},{1,17},{2,18},{3,19},{4,20},{5,21},{6,22},{7,23},{8,24},{9,... | collective-permute-start | bytes 172040 | tf_op jit(solution)/shard_map/ppermute | solution.py:133
  48.6 1.0 %fusion.1 = bf16[1,8,64,512]{3,2,1,0:T(8,128)(2,1)S(1)} fusion(bf16[8,128,576]{1,2,0:T(8,128)(2,1)S(1)} %copy-done.1, f32[8,64]{1,0:T(8,128)S(1)} %fusion.11, f32[8,64,128]{2,1,0:T(8,128)S(1)} %fusion.4), kind=kOutput, calls=%fused_computation.2 | convolution fusion | flops 67568256 | bytes 2101248 | tf_op jit(solution)/shard_map/bht,btc->bhc/dot_general | solution.py:25
  49.6 1.1 %copy.13 = bf16[1,8,64,512]{3,1,2,0:T(8,128)(2,1)} copy(bf16[1,8,64,512]{3,2,1,0:T(8,128)(2,1)S(1)} %fusion.1) | data formatting | bytes 1048576
  (52 shorter events, 9.2 us)
Async XLA Ops:
  0.6 23.5 %copy-start = (bf16[8,64,576]{2,1,0:T(8,128)(2,1)S(1)}, bf16[8,64,576]{2,1,0:T(8,128)(2,1)}, u32[]{:S(2)}) copy-start(bf16[8,64,576]{2,1,0:T(8,128)(2,1)} %param.10) | copy-start | bytes 1769476
  1.7 7.0 %collective-permute-start.5 = (bf16[8,3712]{1,0:T(8,128)(2,1)S(1)}, bf16[8,3712]{1,0:T(8,128)(2,1)S(1)}, u32[]{:S(2)}, u32[]{:S(2)}) collective-permute-start(bf16[8,3712]{1,0:T(8,128)(2,1)S(1)} %pack.1), channel_id=1, source_target_pairs={{0,16},{1,17},{2,18},{3,19},{4,20},{5,21},{6,22},{7,23},{8,24},{9,... | collective-permute-start | bytes 178184 | tf_op jit(solution)/shard_map/ppermute | solution.py:133
  5.8 8.9 %collective-permute-start = (bf16[8,3712]{1,0:T(8,128)(2,1)S(1)}, bf16[8,3712]{1,0:T(8,128)(2,1)S(1)}, u32[]{:S(2)}, u32[]{:S(2)}) collective-permute-start(bf16[8,3712]{1,0:T(8,128)(2,1)S(1)} %pack.1), channel_id=1, source_target_pairs={{0,4},{1,5},{2,10},{3,11},{4,0},{5,1},{6,14},{7,15},{8,12},{9,13},... | collective-permute-start | bytes 178184 | tf_op jit(solution)/shard_map/ppermute | solution.py:133
  8.7 4.2 %collective-permute-start.6 = (bf16[8,3712]{1,0:T(8,128)(2,1)S(1)}, bf16[8,3712]{1,0:T(8,128)(2,1)S(1)}, u32[]{:S(2)}, u32[]{:S(2)}) collective-permute-start(bf16[8,3712]{1,0:T(8,128)(2,1)S(1)} %collective-permute-done.5), channel_id=1, source_target_pairs={{0,1},{1,0},{2,6},{3,7},{4,5},{5,4},{6,2},{7,3},{8,9},{9,8},{10,14... | collective-permute-start | bytes 178184 | tf_op jit(solution)/shard_map/ppermute | solution.py:133
  12.9 5.0 %collective-permute-start.7 = (bf16[16,3712]{1,0:T(8,128)(2,1)S(1)}, bf16[16,3712]{1,0:T(8,128)(2,1)S(1)}, u32[]{:S(2)}, u32[]{:S(2)}) collective-permute-start(bf16[16,3712]{1,0:T(8,128)(2,1)S(1)} %get-tuple-element.45), channel_id=1, source_target_pairs={{0,4},{1,5},{2,10},{3,11},{4,0},{5,1},{6,14},{7,15},{8,12},{9,13},... | collective-permute-start | bytes 356360 | tf_op jit(solution)/shard_map/ppermute | solution.py:133
  14.7 4.9 %collective-permute-start.1 = (bf16[16,3712]{1,0:T(8,128)(2,1)S(1)}, bf16[16,3712]{1,0:T(8,128)(2,1)S(1)}, u32[]{:S(2)}, u32[]{:S(2)}) collective-permute-start(bf16[16,3712]{1,0:T(8,128)(2,1)S(1)} %pad_maximum_fusion.1), channel_id=1, source_target_pairs={{0,8},{1,9},{2,3},{3,2},{4,12},{5,13},{6,7},{7,6},{8,0},{9,1},{10,... | collective-permute-start | bytes 356360 | tf_op jit(solution)/shard_map/ppermute | solution.py:133
  17.9 6.2 %collective-permute-start.8 = (bf16[32,3712]{1,0:T(8,128)(2,1)S(1)}, bf16[32,3712]{1,0:T(8,128)(2,1)S(1)}, u32[]{:S(2)}, u32[]{:S(2)}) collective-permute-start(bf16[32,3712]{1,0:T(8,128)(2,1)S(1)} %constant_dynamic-update-slice_fusion.2.refs_1_), channel_id=1, source_target_pairs={{0,8},{1,9},{2,3},{3,2},{4,12},{5,13},{6,7},{7,6},{8,0},{9,1},{10,... | collective-permute-start | bytes 712712 | tf_op jit(solution)/shard_map/ppermute | solution.py:133
  19.6 6.2 %collective-permute-start.2 = (bf16[32,3712]{1,0:T(8,128)(2,1)S(1)}, bf16[32,3712]{1,0:T(8,128)(2,1)S(1)}, u32[]{:S(2)}, u32[]{:S(2)}) collective-permute-start(bf16[32,3712]{1,0:T(8,128)(2,1)S(1)} %pad_maximum_fusion.refs_1_), channel_id=1, source_target_pairs={{0,1},{1,0},{2,6},{3,7},{4,5},{5,4},{6,2},{7,3},{8,9},{9,8},{10,14... | collective-permute-start | bytes 712712 | tf_op jit(solution)/shard_map/ppermute | solution.py:133
  21.2 4.6 %collective-permute-start.14 = (bf16[32,3712]{1,0:T(8,128)(2,1)S(1)}, bf16[32,3712]{1,0:T(8,128)(2,1)S(1)}, u32[]{:S(2)}, u32[]{:S(2)}) collective-permute-start(bf16[32,3712]{1,0:T(8,128)(2,1)S(1)} %constant_dynamic-update-slice_fusion.2.refs_1_), channel_id=1, source_target_pairs={{0,2},{1,3},{2,0},{3,1},{4,6},{5,7},{6,4},{7,5},{8,10},{9,11},{10,... | collective-permute-start | bytes 712712 | tf_op jit(solution)/shard_map/ppermute | solution.py:133
  21.2 2.9 %copy-start.1 = (bf16[8,128,576]{1,2,0:T(8,128)(2,1)S(1)}, bf16[8,128,576]{1,2,0:T(8,128)(2,1)}, u32[]{:S(2)}) copy-start(bf16[8,128,576]{1,2,0:T(8,128)(2,1)} %param.11) | copy-start | bytes 3538948
  24.1 1.7 %collective-permute-start.15 = (bf16[32,3712]{1,0:T(8,128)(2,1)S(1)}, bf16[32,3712]{1,0:T(8,128)(2,1)S(1)}, u32[]{:S(2)}, u32[]{:S(2)}) collective-permute-start(bf16[32,3712]{1,0:T(8,128)(2,1)S(1)} %collective-permute-done.8.refs_2_), channel_id=1, source_target_pairs={{0,2},{1,3},{2,0},{3,1},{4,6},{5,7},{6,4},{7,5},{8,10},{9,11},{10,... | collective-permute-start | bytes 712712 | tf_op jit(solution)/shard_map/ppermute | solution.py:133
  24.5 3.9 %collective-permute-start.3 = (bf16[32,3712]{1,0:T(8,128)(2,1)S(1)}, bf16[32,3712]{1,0:T(8,128)(2,1)S(1)}, u32[]{:S(2)}, u32[]{:S(2)}) collective-permute-start(bf16[32,3712]{1,0:T(8,128)(2,1)S(1)} %pad_maximum_fusion.refs_1_), channel_id=1, source_target_pairs={{0,2},{1,3},{2,0},{3,1},{4,6},{5,7},{6,4},{7,5},{8,10},{9,11},{10,... | collective-permute-start | bytes 712712 | tf_op jit(solution)/shard_map/ppermute | solution.py:133
  25.8 2.6 %collective-permute-start.4 = (bf16[32,3712]{1,0:T(8,128)(2,1)S(1)}, bf16[32,3712]{1,0:T(8,128)(2,1)S(1)}, u32[]{:S(2)}, u32[]{:S(2)}) collective-permute-start(bf16[32,3712]{1,0:T(8,128)(2,1)S(1)} %collective-permute-done.2.refs_2_), channel_id=1, source_target_pairs={{0,2},{1,3},{2,0},{3,1},{4,6},{5,7},{6,4},{7,5},{8,10},{9,11},{10,... | collective-permute-start | bytes 712712 | tf_op jit(solution)/shard_map/ppermute | solution.py:133
  27.6 2.7 %collective-permute-start.16 = (bf16[32,3584]{1,0:T(8,128)(2,1)S(1)}, bf16[32,3584]{1,0:T(8,128)(2,1)S(1)}, u32[]{:S(2)}, u32[]{:S(2)}) collective-permute-start(bf16[32,3584]{1,0:T(8,128)(2,1)S(1)} %get-tuple-element.42), channel_id=1, source_target_pairs={{0,2},{1,3},{2,0},{3,1},{4,6},{5,7},{6,4},{7,5},{8,10},{9,11},{10,... | collective-permute-start | bytes 688136 | tf_op jit(solution)/shard_map/ppermute | solution.py:133
  30.2 1.9 %collective-permute-start.9 = (bf16[32,3584]{1,0:T(8,128)(2,1)S(1)}, bf16[32,3584]{1,0:T(8,128)(2,1)S(1)}, u32[]{:S(2)}, u32[]{:S(2)}) collective-permute-start(bf16[32,3584]{1,0:T(8,128)(2,1)S(1)} %get-tuple-element.36), channel_id=1, source_target_pairs={{0,2},{1,3},{2,0},{3,1},{4,6},{5,7},{6,4},{7,5},{8,10},{9,11},{10,... | collective-permute-start | bytes 688136 | tf_op jit(solution)/shard_map/ppermute | solution.py:133
  30.3 6.1 %collective-permute-start.18 = (bf16[32,3584]{1,0:T(8,128)(2,1)S(1)}, bf16[32,3584]{1,0:T(8,128)(2,1)S(1)}, u32[]{:S(2)}, u32[]{:S(2)}) collective-permute-start(bf16[32,3584]{1,0:T(8,128)(2,1)S(1)} %add_convert_fusion), channel_id=1, source_target_pairs={{0,8},{1,9},{2,3},{3,2},{4,12},{5,13},{6,7},{7,6},{8,0},{9,1},{10,... | collective-permute-start | bytes 688136 | tf_op jit(solution)/shard_map/ppermute | solution.py:133
  31.4 1.9 %collective-permute-start.17 = (bf16[32,3584]{1,0:T(8,128)(2,1)S(1)}, bf16[32,3584]{1,0:T(8,128)(2,1)S(1)}, u32[]{:S(2)}, u32[]{:S(2)}) collective-permute-start(bf16[32,3584]{1,0:T(8,128)(2,1)S(1)} %get-tuple-element.43), channel_id=1, source_target_pairs={{0,2},{1,3},{2,0},{3,1},{4,6},{5,7},{6,4},{7,5},{8,10},{9,11},{10,... | collective-permute-start | bytes 688136 | tf_op jit(solution)/shard_map/ppermute | solution.py:133
  32.1 6.2 %collective-permute-start.11 = (bf16[32,3584]{1,0:T(8,128)(2,1)S(1)}, bf16[32,3584]{1,0:T(8,128)(2,1)S(1)}, u32[]{:S(2)}, u32[]{:S(2)}) collective-permute-start(bf16[32,3584]{1,0:T(8,128)(2,1)S(1)} %add_convert_fusion.1), channel_id=1, source_target_pairs={{0,1},{1,0},{2,6},{3,7},{4,5},{5,4},{6,2},{7,3},{8,9},{9,8},{10,14... | collective-permute-start | bytes 688136 | tf_op jit(solution)/shard_map/ppermute | solution.py:133
  33.3 4.6 %collective-permute-start.10 = (bf16[32,3584]{1,0:T(8,128)(2,1)S(1)}, bf16[32,3584]{1,0:T(8,128)(2,1)S(1)}, u32[]{:S(2)}, u32[]{:S(2)}) collective-permute-start(bf16[32,3584]{1,0:T(8,128)(2,1)S(1)} %get-tuple-element.37), channel_id=1, source_target_pairs={{0,2},{1,3},{2,0},{3,1},{4,6},{5,7},{6,4},{7,5},{8,10},{9,11},{10,... | collective-permute-start | bytes 688136 | tf_op jit(solution)/shard_map/ppermute | solution.py:133
  36.5 4.9 %collective-permute-start.19 = (bf16[16,3584]{1,0:T(8,128)(2,1)S(1)}, bf16[16,3584]{1,0:T(8,128)(2,1)S(1)}, u32[]{:S(2)}, u32[]{:S(2)}) collective-permute-start(bf16[16,3584]{1,0:T(8,128)(2,1)S(1)} %slice.64), channel_id=1, source_target_pairs={{0,4},{1,5},{2,10},{3,11},{4,0},{5,1},{6,14},{7,15},{8,12},{9,13},... | collective-permute-start | bytes 344072 | tf_op jit(solution)/shard_map/ppermute | solution.py:133
  38.5 4.9 %collective-permute-start.12 = (bf16[16,3584]{1,0:T(8,128)(2,1)S(1)}, bf16[16,3584]{1,0:T(8,128)(2,1)S(1)}, u32[]{:S(2)}, u32[]{:S(2)}) collective-permute-start(bf16[16,3584]{1,0:T(8,128)(2,1)S(1)} %slice.65), channel_id=1, source_target_pairs={{0,8},{1,9},{2,3},{3,2},{4,12},{5,13},{6,7},{7,6},{8,0},{9,1},{10,... | collective-permute-start | bytes 344072 | tf_op jit(solution)/shard_map/ppermute | solution.py:133
  41.4 4.2 %collective-permute-start.20 = (bf16[8,3584]{1,0:T(8,128)(2,1)S(1)}, bf16[8,3584]{1,0:T(8,128)(2,1)S(1)}, u32[]{:S(2)}, u32[]{:S(2)}) collective-permute-start(bf16[8,3584]{1,0:T(8,128)(2,1)S(1)} %slice.66), channel_id=1, source_target_pairs={{0,1},{1,0},{2,6},{3,7},{4,5},{5,4},{6,2},{7,3},{8,9},{9,8},{10,14... | collective-permute-start | bytes 172040 | tf_op jit(solution)/shard_map/ppermute | solution.py:133
  43.4 7.3 %collective-permute-start.13 = (bf16[8,3584]{1,0:T(8,128)(2,1)S(1)}, bf16[8,3584]{1,0:T(8,128)(2,1)S(1)}, u32[]{:S(2)}, u32[]{:S(2)}) collective-permute-start(bf16[8,3584]{1,0:T(8,128)(2,1)S(1)} %slice.67), channel_id=1, source_target_pairs={{0,4},{1,5},{2,10},{3,11},{4,0},{5,1},{6,14},{7,15},{8,12},{9,13},... | collective-permute-start | bytes 172040 | tf_op jit(solution)/shard_map/ppermute | solution.py:133
  45.7 5.1 %collective-permute-start.21 = (bf16[8,3584]{1,0:T(8,128)(2,1)S(1)}, bf16[8,3584]{1,0:T(8,128)(2,1)S(1)}, u32[]{:S(2)}, u32[]{:S(2)}) collective-permute-start(bf16[8,3584]{1,0:T(8,128)(2,1)S(1)} %fusion.7), channel_id=1, source_target_pairs={{0,16},{1,17},{2,18},{3,19},{4,20},{5,21},{6,22},{7,23},{8,24},{9,... | collective-permute-start | bytes 172040 | tf_op jit(solution)/shard_map/ppermute | solution.py:133
